TPU v7x, 128 devices: a whole 4x4x4 slice. The times are simulated.
128 devices in a mesh: layer: 2 (over core), dp: 16 (over y, x), mp: 4 (over z).
Axes of the slice: x: 4, y: 4, z: 4, core: 2. Of those that a mesh axis runs over, the one named last changes fastest.
Arguments:
- grad: bfloat16 [8192, 4096], P(('layer', 'dp'), 'mp'), parts along dimension 0, may hold values from -6 to 6
- left_basis: bfloat16 [8192, 4096], P(('layer', 'mp'), 'dp'), parts along dimension 0, may hold values from -0.09375 to 0.09375
- right_basis: bfloat16 [8192, 4096], P(('layer', 'dp'), 'mp'), parts along dimension 0, may hold values from -0.09375 to 0.09375
- left_stat: float32 [8192, 4096], P(('layer', 'mp'), 'dp'), parts along dimension 0, may hold values from -6 to 6
- right_stat: float32 [8192, 4096], P(('layer', 'dp'), 'mp'), parts along dimension 0, may hold values from -6 to 6
- first_moment: float32 [8192, 4096], P(('layer', 'dp'), 'mp'), parts along dimension 0, may hold values from -6 to 6
- second_moment: float32 [8192, 4096], P(('layer', 'dp'), 'mp'), parts along dimension 0, may hold values from 0.3 to 3
Outputs:
- update: float32 [8192, 4096], P(('layer', 'dp'), 'mp'), parts along dimension 0
- left_stat_new: float32 [8192, 4096], P(('layer', 'mp'), 'dp'), parts along dimension 0
- right_stat_new: float32 [8192, 4096], P(('layer', 'dp'), 'mp'), parts along dimension 0
- first_new: float32 [8192, 4096], P(('layer', 'dp'), 'mp'), parts along dimension 0
- second_new: float32 [8192, 4096], P(('layer', 'dp'), 'mp'), parts along dimension 0
There are 2 independent parts, one for each index of `layer`. A program takes and returns all parts, laid end to end along the dimension named above; each array names one. Nothing has to cross between parts.
All inputs are finite; a program needn't handle non-finite values.
Results may differ from a plain program's by a relative error of at most 0.022.
Values may be sent and summed in bfloat16 or wider, within the bound.
No kernel may reach another device: no remote copies, remote signals or barrier semaphores. Data moves between devices by JAX's collectives and lax.ppermute only.
A program may use at most 128 MiB of HBM per device.

v0:
```python
import jax
import jax.numpy as jnp
from jax import lax
from jax.sharding import PartitionSpec as P

stat_decay = 0.95
first_decay = 0.9
second_decay = 0.95
first_bias = 1.0 - 0.9**10
second_bias = 1.0 - 0.95**10
adam_eps = 1e-08


def contract(left, right, left_dim, right_dim):
    return lax.dot_general(
        left, right, (((left_dim,), (right_dim,)), ((), ())), preferred_element_type=jnp.float32
    )


def per_device(grad, left_basis, right_basis, left_stat, right_stat, first_moment, second_moment):
    grad_rows = lax.all_gather(grad, "mp", axis=1, tiled=True)
    grad_cols = lax.all_gather(grad, "dp", axis=0, tiled=True)
    left_cols = lax.all_gather(left_basis, "mp", axis=0, tiled=True)
    right_cols = lax.all_gather(right_basis, "dp", axis=0, tiled=True)
    left_sum = lax.psum_scatter(
        contract(grad_cols, grad, 1, 1).astype(jnp.bfloat16), "mp", scatter_dimension=0, tiled=True
    ).astype(jnp.float32)
    right_sum = lax.psum_scatter(
        contract(grad_rows, grad, 0, 0).astype(jnp.bfloat16), "dp", scatter_dimension=0, tiled=True
    ).astype(jnp.float32)
    half_rotated = contract(left_cols, grad_cols, 0, 0).astype(jnp.bfloat16)
    rotated_full = lax.all_gather(half_rotated, "mp", axis=1, tiled=True)
    rotated = jnp.dot(rotated_full, right_cols, preferred_element_type=jnp.float32)
    first_new = first_decay * first_moment + (1.0 - first_decay) * rotated
    second_new = second_decay * second_moment + (1.0 - second_decay) * rotated * rotated
    direction = (first_new / first_bias / (jnp.sqrt(second_new / second_bias) + adam_eps)).astype(
        jnp.bfloat16
    )
    back_trans = lax.psum_scatter(
        contract(right_cols, direction, 1, 1).astype(jnp.bfloat16),
        "mp",
        scatter_dimension=0,
        tiled=True,
    )
    update = lax.psum_scatter(
        contract(left_cols, back_trans, 1, 1).astype(jnp.bfloat16),
        "dp",
        scatter_dimension=0,
        tiled=True,
    ).astype(jnp.float32)
    left_stat_new = stat_decay * left_stat + (1.0 - stat_decay) * left_sum
    right_stat_new = stat_decay * right_stat + (1.0 - stat_decay) * right_sum
    return (update, left_stat_new, right_stat_new, first_new, second_new)


def solution(mesh):
    placed = (
        P(("layer", "dp"), "mp"),
        P(("layer", "mp"), "dp"),
        P(("layer", "dp"), "mp"),
        P(("layer", "mp"), "dp"),
        P(("layer", "dp"), "mp"),
        P(("layer", "dp"), "mp"),
        P(("layer", "dp"), "mp"),
    )
    return jax.shard_map(
        per_device,
        mesh=mesh,
        in_specs=placed,
        out_specs=(
            P(("layer", "dp"), "mp"),
            P(("layer", "mp"), "dp"),
            P(("layer", "dp"), "mp"),
            P(("layer", "dp"), "mp"),
            P(("layer", "dp"), "mp"),
        ),
        check_vma=False,
    )
```

profile of v0, /device:TPU:24, one launch (start us, length us, event | category | flops | bytes accessed | tf_op | source)
XLA Modules:
  0.0 502.2 jit_solution(13705130881148730926)
XLA Ops:
  7.2 0.0 all-gather.6.cloned.1.call-start
  7.2 0.7 all-gather.6.cloned.1.call-update
  7.9 0.0 all-gather.8.cloned.1.call-start
  7.9 0.7 all-gather.8.cloned.1.call-update
  8.6 0.0 all-gather.12.cloned.1.call-start
  8.7 0.7 all-gather.12.cloned.1.call-update
  9.4 0.0 copy-start.5
  9.4 0.0 copy-start.6
  9.4 0.0 all-gather.10.cloned.1.call-start
  9.4 33.4 %all-gather.6.cloned.1.call-done = bf16[4096,256]{1,0:T(8,128)(2,1)} async-done(((bf16[1024,256]{1,0:T(8,128)(2,1)}), bf16[4096,256]{1,0:T(8,128)(2,1)}) %all-gather.6.cloned.1.call-update) | async-done | bytes 2097168 | tf_op jit(solution)/shard_map/all_gather | solution.py:23
  42.9 72.6 %all-gather.8.cloned.1.call-done = bf16[4096,1024]{1,0:T(8,128)(2,1)} async-done(((bf16[256,1024]{1,0:T(8,128)(2,1)}), bf16[4096,1024]{1,0:T(8,128)(2,1)}) %all-gather.8.cloned.1.call-update) | async-done | bytes 8388624 | tf_op jit(solution)/shard_map/all_gather | solution.py:22
  115.5 7.2 %convolution_convert_fusion.3 = bf16[256,1024]{1,0:T(8,128)(2,1)} fusion(bf16[4096,256]{1,0:T(8,128)(2,1)} %all-gather.6.cloned.1.call-done, bf16[4096,1024]{1,0:T(8,128)(2,1)} %all-gather.8.cloned.1.call-done), kind=kOutput, calls=%fused_computation.6 | convolution fusion | flops 2147745792 | bytes 11010048 | tf_op jit(solution)/shard_map/dot_general | solution.py:15
  122.6 0.0 all-gather.10.cloned.1.call-update
  122.7 0.0 all-gather.14.cloned.1.call-start
  122.7 0.5 all-gather.14.cloned.1.call-update
  123.3 0.0 reduce-scatter.5.cloned.1.call-start
  123.3 64.7 %all-gather.12.cloned.1.call-done = bf16[4096,1024]{1,0:T(8,128)(2,1)} async-done(((bf16[256,1024]{1,0:T(8,128)(2,1)}), bf16[4096,1024]{1,0:T(8,128)(2,1)}) %all-gather.12.cloned.1.call-update) | async-done | bytes 8388624 | tf_op jit(solution)/shard_map/all_gather | solution.py:24
  188.0 33.0 %all-gather.10.cloned.1.call-done = bf16[256,4096]{1,0:T(8,128)(2,1)} async-done(((bf16[256,1024]{1,0:T(8,128)(2,1)}), bf16[256,4096]{1,0:T(8,128)(2,1)}) %all-gather.10.cloned.1.call-update) | async-done | bytes 2097168 | tf_op jit(solution)/shard_map/all_gather | solution.py:32
  220.9 0.0 copy-done.5
  220.9 0.0 copy-done.6
  220.9 6.7 %multiply_add_fusion.2 = (f32[256,1024]{1,0:T(8,128)S(1)}, f32[256,1024]{1,0:T(8,128)S(1)}) fusion(f32[256,1024]{1,0:T(8,128)S(1)} %copy-done.5, f32[256,1024]{1,0:T(8,128)S(1)} %copy-done.6, bf16[256,4096]{1,0:T(8,128)(2,1)} %all-gather.10.cloned.1.call-done, bf16[4096,1024]{1,0:T(8,128)(2,1)} %all-gather.12.cloned.1.call-done), kind=kOutput, calls=%fused_computation.11 | convolution fusion | flops 2149318656 | bytes 14680064 | tf_op jit(solution)/shard_map/dot_general | solution.py:33
  227.6 0.0 copy-start.7
  227.6 0.0 copy-start.8
  227.6 0.9 copy-done.7
  228.6 0.3 copy-done.8
  228.9 0.0 copy-done.4
  228.9 4.1 fusion
  233.0 0.0 reduce-scatter.5.cloned.1.call-update
  233.0 0.0 reduce-scatter.11.cloned.1.call-start
  233.1 20.3 %all-gather.14.cloned.1.call-done = bf16[256,4096]{1,0:T(8,128)(2,1)} async-done(((bf16[256,1024]{1,0:T(8,128)(2,1)}), bf16[256,4096]{1,0:T(8,128)(2,1)}) %all-gather.14.cloned.1.call-update) | async-done | bytes 2097168 | tf_op jit(solution)/shard_map/all_gather | solution.py:21
  253.4 0.0 copy-done.1
  253.4 7.2 %convolution_convert_fusion = bf16[4096,1024]{1,0:T(8,128)(2,1)} fusion(bf16[256,4096]{1,0:T(8,128)(2,1)} %all-gather.14.cloned.1.call-done, bf16[256,1024]{1,0:T(8,128)(2,1)S(1)} %copy-done.1), kind=kOutput, calls=%fused_computation.1 | convolution fusion | flops 2151677952 | bytes 11010048 | tf_op jit(solution)/shard_map/dot_general | solution.py:15
  260.6 0.0 reduce-scatter.11.cloned.1.call-update
  260.6 0.0 copy-start
  260.6 0.0 reduce-scatter.9.cloned.1.call-start
  260.7 7.2 %convolution_convert_fusion.1 = bf16[4096,256]{1,0:T(8,128)(2,1)} fusion(bf16[4096,1024]{1,0:T(8,128)(2,1)} %all-gather.8.cloned.1.call-done, bf16[256,1024]{1,0:T(8,128)(2,1)S(1)} %copy-done.1), kind=kOutput, calls=%fused_computation.2 | convolution fusion | flops 2148532224 | bytes 11010048 | tf_op jit(solution)/shard_map/dot_general | solution.py:15
  267.9 0.0 reduce-scatter.9.cloned.1.call-update
  267.9 0.2 reduce-scatter.7.cloned.1.call-start
  268.2 17.3 %reduce-scatter.5.cloned.1.call-done = bf16[1024,256]{0,1:T(8,128)(2,1)} async-done(((bf16[4096,256]{0,1:T(8,128)(2,1)}), bf16[1024,256]{0,1:T(8,128)(2,1)}) %reduce-scatter.5.cloned.1.call-update) | async-done | bytes 524304 | tf_op jit(solution)/shard_map/reduce_scatter | solution.py:39
  285.5 0.0 copy-done
  285.5 6.7 %convert_bitcast_fusion = bf16[4096,1024]{0,1:T(8,128)(2,1)} fusion(bf16[1024,256]{0,1:T(8,128)(2,1)} %reduce-scatter.5.cloned.1.call-done, bf16[4096,256]{1,0:T(8,128)(2,1)S(1)} %copy-done), kind=kOutput, calls=%fused_computation | convolution fusion | flops 2151677952 | bytes 11010048 | tf_op jit(solution)/shard_map/dot_general | solution.py:15
  292.2 0.0 reduce-scatter.7.cloned.1.call-update
  292.2 81.6 %reduce-scatter.11.cloned.1.call-done = bf16[256,1024]{1,0:T(8,128)(2,1)} async-done(((bf16[4096,1024]{1,0:T(8,128)(2,1)}), bf16[256,1024]{1,0:T(8,128)(2,1)}) %reduce-scatter.11.cloned.1.call-update) | async-done | bytes 524304 | tf_op jit(solution)/shard_map/reduce_scatter | solution.py:28
  373.8 2.2 multiply_add_fusion
  376.0 29.7 %reduce-scatter.9.cloned.1.call-done = bf16[1024,256]{1,0:T(8,128)(2,1)} async-done(((bf16[4096,256]{1,0:T(8,128)(2,1)}), bf16[1024,256]{1,0:T(8,128)(2,1)}) %reduce-scatter.9.cloned.1.call-update) | async-done | bytes 524304 | tf_op jit(solution)/shard_map/reduce_scatter | solution.py:25
  405.7 2.2 multiply_add_fusion.1
  407.9 85.6 %reduce-scatter.7.cloned.1.call-done = bf16[256,1024]{0,1:T(8,128)(2,1)} async-done(((bf16[4096,1024]{0,1:T(8,128)(2,1)}), bf16[256,1024]{0,1:T(8,128)(2,1)}) %reduce-scatter.7.cloned.1.call-update) | async-done | bytes 524304 | tf_op jit(solution)/shard_map/reduce_scatter | solution.py:45
  493.4 2.2 copy.12
  (6 shorter events, 0.0 us)
Async XLA Ops:
  7.2 35.7 %all-gather.6.cloned.1.call-start = ((), (), s32[]{:S(2)}) async-start(), calls=%async_computation.4 | async-start | bytes 2621440 | tf_op jit(solution)/shard_map/all_gather | solution.py:23
  7.9 107.6 %all-gather.8.cloned.1.call-start = ((), (), s32[]{:S(2)}) async-start(), calls=%async_computation.5 | async-start | bytes 8912896 | tf_op jit(solution)/shard_map/all_gather | solution.py:22
  8.6 179.3 %all-gather.12.cloned.1.call-start = ((), (), s32[]{:S(2)}) async-start(), calls=%async_computation.7 | async-start | bytes 8912896 | tf_op jit(solution)/shard_map/all_gather | solution.py:24
  9.4 211.5 %copy-start.5 = (f32[256,1024]{1,0:T(8,128)S(1)}, f32[256,1024]{1,0:T(8,128)}, u32[]{:S(2)}) copy-start(f32[256,1024]{1,0:T(8,128)} %param.12) | copy-start | bytes 3145732
  9.4 211.5 %copy-start.6 = (f32[256,1024]{1,0:T(8,128)S(1)}, f32[256,1024]{1,0:T(8,128)}, u32[]{:S(2)}) copy-start(f32[256,1024]{1,0:T(8,128)} %param.13) | copy-start | bytes 3145732
  9.4 211.5 %all-gather.10.cloned.1.call-start = ((), (), s32[]{:S(2)}) async-start(), calls=%async_computation.6 | async-start | bytes 2621440 | tf_op jit(solution)/shard_map/all_gather | solution.py:32
  122.7 130.7 %all-gather.14.cloned.1.call-start = ((), (), s32[]{:S(2)}) async-start(), calls=%async_computation.11 | async-start | bytes 2621440 | tf_op jit(solution)/shard_map/all_gather | solution.py:21
  123.3 162.2 %reduce-scatter.5.cloned.1.call-start = ((), (), s32[]{:S(2)}) async-start(), calls=%async_computation.8 | async-start | bytes 2621440 | tf_op jit(solution)/shard_map/reduce_scatter | solution.py:39
  220.9 8.0 %copy-start.4 = (bf16[4096,1024]{1,0:T(8,128)(2,1)S(1)}, bf16[4096,1024]{1,0:T(8,128)(2,1)}, u32[]{:S(2)}) copy-start(bf16[4096,1024]{1,0:T(8,128)(2,1)} %all-gather.12.cloned.1.call-done) | copy-start | bytes 25165828
  227.6 1.0 copy-start.7
  227.6 1.3 copy-start.8
  228.9 24.5 %copy-start.1 = (bf16[256,1024]{1,0:T(8,128)(2,1)S(1)}, bf16[256,1024]{1,0:T(8,128)(2,1)}, u32[]{:S(2)}) copy-start(bf16[256,1024]{1,0:T(8,128)(2,1)} %param.7) | copy-start | bytes 1572868
  233.0 140.8 %reduce-scatter.11.cloned.1.call-start = ((), (), s32[]{:S(2)}) async-start(), calls=%async_computation.12 | async-start | bytes 8912896 | tf_op jit(solution)/shard_map/reduce_scatter | solution.py:28
  260.6 24.8 %copy-start = (bf16[4096,256]{1,0:T(8,128)(2,1)S(1)}, bf16[4096,256]{1,0:T(8,128)(2,1)}, u32[]{:S(2)}) copy-start(bf16[4096,256]{1,0:T(8,128)(2,1)} %all-gather.6.cloned.1.call-done) | copy-start | bytes 6291460
  260.6 145.1 %reduce-scatter.9.cloned.1.call-start = ((), (), s32[]{:S(2)}) async-start(), calls=%async_computation.10 | async-start | bytes 2621440 | tf_op jit(solution)/shard_map/reduce_scatter | solution.py:25
  267.9 225.5 %reduce-scatter.7.cloned.1.call-start = ((), (), s32[]{:S(2)}) async-start(), calls=%async_computation.9 | async-start | bytes 8912896 | tf_op jit(solution)/shard_map/reduce_scatter | solution.py:45
  292.2 81.6 %copy-start.2 = (f32[256,1024]{1,0:T(8,128)S(1)}, f32[256,1024]{1,0:T(8,128)}, u32[]{:S(2)}) copy-start(f32[256,1024]{1,0:T(8,128)} %param.11) | copy-start | bytes 3145732
  292.2 113.5 %copy-start.3 = (f32[1024,256]{1,0:T(8,128)S(1)}, f32[1024,256]{1,0:T(8,128)}, u32[]{:S(2)}) copy-start(f32[1024,256]{1,0:T(8,128)} %param.10) | copy-start | bytes 3145732
Sparse Core Ops, SparseCore 0:
  9.7 33.1 all-gather.5
  45.0 70.4 all-gather.7
  117.6 70.3 all-gather.11
  190.1 30.8 all-gather.9
  222.4 30.9 all-gather.13
  255.7 29.7 reduce-scatter.4
  289.2 84.5 reduce-scatter.10
  376.3 29.3 reduce-scatter.8
  409.1 84.2 reduce-scatter.6
where the time goes:
time: 503 us; the launch traced here: 502 us
  waiting for transfers between devices  441 us (88%)
  matrix products  39 us (8%)
  between operations  13.9 us (3%)
    reduce_scatter x1, waiting for transfers between devices, per_device(): lax.psum_scatter(contract(left_cols, back_trans, 1, 1).astype(jnp.bfloat1...  85.6 us
    reduce_scatter x1, waiting for transfers between devices, per_device(): lax.psum_scatter(contract(grad_rows, grad, 0, 0).astype(jnp.bfloat16), 'd...  81.6 us
    all_gather x1, waiting for transfers between devices, per_device(): grad_cols = lax.all_gather(grad, 'dp', axis=0, tiled=True)  72.6 us
    all_gather x1, waiting for transfers between devices, per_device(): right_cols = lax.all_gather(right_basis, 'dp', axis=0, tiled=True)  64.7 us
    all_gather x1, waiting for transfers between devices, per_device(): left_cols = lax.all_gather(left_basis, 'mp', axis=0, tiled=True)  33.4 us
    all_gather x1, waiting for transfers between devices, per_device(): rotated_full = lax.all_gather(half_rotated, 'mp', axis=1, tiled=True)  33 us
    dot_general x5, matrix products, contract(): lax.dot_general(left, right, (((left_dim,), (right_dim,)), ((), ())), pre...  32.4 us
    reduce_scatter x1, waiting for transfers between devices, per_device(): lax.psum_scatter(contract(grad_cols, grad, 1, 1).astype(jnp.bfloat16), 'm...  29.7 us
  transfers between devices with their start and end apart: 9, of which 9 were waited for; matrix products, arithmetic and copies ran while one was open for 9% of the time, Pallas kernels for 0%

commit v1 on v0

v1 whole, which is shorter than its diff:
```python
import jax
import jax.numpy as jnp
from jax import lax
from jax.experimental import pallas as pl
from jax.experimental.pallas import tpu as pltpu
from jax.sharding import PartitionSpec as P

stat_decay = 0.95
first_decay = 0.9
second_decay = 0.95
first_bias = 1.0 - 0.9**10
second_bias = 1.0 - 0.95**10
adam_eps = 1e-08

SIDE = 4
bf16, f32 = jnp.bfloat16, jnp.float32


def permute(value, target):
    pairs = []
    for y in range(SIDE):
        for x in range(SIDE):
            for z in range(SIDE):
                a, b, c = (v % SIDE for v in target(x, y, z))
                pairs.append(((y * SIDE + x) * SIDE + z, (b * SIDE + a) * SIDE + c))
    return lax.ppermute(value, ("dp", "mp"), pairs)


def shift(value, axis, by):
    dx, dy, dz = (by if axis == name else 0 for name in "xyz")
    return permute(value, lambda x, y, z: (x + dx, y + dy, z + dz))


def swap_xy(value):
    return permute(value, lambda x, y, z: (y, x, z))


def swap_xz(value):
    return permute(value, lambda x, y, z: (z, y, x))


def turn(value):
    return permute(value, lambda x, y, z: (y, z, x))


def ring_gather(value, axis):
    return [value, shift(value, axis, -1), shift(value, axis, 2), shift(value, axis, 1)]


def ring_scatter(parts, axis):
    return [
        parts[0],
        shift(parts[1], axis, 1),
        shift(parts[2], axis, 2),
        shift(parts[3], axis, -1),
    ]


def total(parts):
    return (parts[0].astype(f32) + parts[1].astype(f32)) + (parts[2].astype(f32) + parts[3].astype(f32))


def contract(left, right, left_dim, right_dim):
    return lax.dot_general(
        left, right, (((left_dim,), (right_dim,)), ((), ())), preferred_element_type=f32
    )


def rows(ref, block, size):
    return ref[pl.ds(pl.multiple_of(block * size, size), size), :]


def half_kernel(at, *refs):
    x, y, z = at[0], at[1], at[2]
    lefts, grads, outs, left_abs = refs[:4], refs[4:8], refs[8:12], refs[12]
    for i in range(4):
        left_abs[(z + i) % 4] = lefts[i][...]
    grad = jnp.concatenate([g[...] for g in grads], axis=0)
    for j in range(4):
        left = left_abs.at[(x + j) % 4]
        left = jnp.concatenate([rows(left, (y + s) % 4, 256) for s in range(4)], axis=0)
        outs[j][...] = contract(left, grad, 0, 0).astype(bf16)


def step_kernel(at, *refs):
    z = at[2]
    halves, right, first, second = refs[:4], refs[4], refs[5], refs[6]
    first_out, second_out, outs = refs[7], refs[8], refs[9:13]
    rotated = contract(halves[0][...], rows(right, z, 1024), 1, 0)
    for i in range(1, 4):
        rotated += contract(halves[i][...], rows(right, (z + i) % 4, 1024), 1, 0)
    first_new = first_decay * first[...] + (1.0 - first_decay) * rotated
    second_new = second_decay * second[...] + (1.0 - second_decay) * rotated * rotated
    first_out[...] = first_new
    second_out[...] = second_new
    direction = (first_new / first_bias / (jnp.sqrt(second_new / second_bias) + adam_eps)).astype(bf16)
    for j in range(4):
        outs[j][...] = contract(direction, rows(right, (z + j) % 4, 1024), 1, 1).astype(bf16)


def update_kernel(at, *refs):
    x, y, z = at[0], at[1], at[2]
    lefts, backs, outs, back_abs = refs[:4], refs[4:8], refs[8:12], refs[12]
    for i in range(4):
        back_abs[(x + i) % 4] = backs[i][...]
    back = jnp.concatenate([back_abs[(z + i) % 4] for i in range(4)], axis=0)
    for j in range(4):
        left = jnp.concatenate([rows(lefts[i], (y + j) % 4, 256) for i in range(4)], axis=1)
        outs[j][...] = contract(left, back, 1, 0).astype(bf16)


def left_kernel(at, *refs):
    x, y, z = at[0], at[1], at[2]
    grads, others, outs, grad_abs, other_abs = refs[:4], refs[4:8], refs[8:12], refs[12], refs[13]
    for i in range(4):
        grad_abs[pl.ds(pl.multiple_of((y + i) % 4 * 256, 256), 256), :] = grads[i][...]
        other_abs[(x + i) % 4] = others[i][...]
    for j in range(4):
        outs[j][...] = contract(grad_abs[...], other_abs[(z + j) % 4], 1, 1).astype(bf16)


def right_kernel(at, *refs):
    x, y, z = at[0], at[1], at[2]
    others, grads, outs, other_abs, grad_abs = refs[:4], refs[4:8], refs[8:12], refs[12], refs[13]
    for i in range(4):
        grad_abs[pl.ds(pl.multiple_of((y + i) % 4 * 256, 256), 256), :] = grads[i][...]
        other_abs[pl.ds(pl.multiple_of((z + i) % 4 * 256, 256), 256), :] = others[i][...]
    for j in range(4):
        columns = pl.ds(pl.multiple_of((x + j) % 4 * 256, 256), 256)
        outs[j][...] = contract(other_abs[:, columns], grad_abs[...], 0, 0).astype(bf16)


def call(kernel, name, at, operands, out_shapes, scratch=()):
    flops = 2 * 1024**3 * (2 if kernel is step_kernel else 1)
    moved = sum(v.size * v.dtype.itemsize for v in operands)
    moved += sum(v.size * v.dtype.itemsize for v in out_shapes)
    return pl.pallas_call(
        kernel,
        out_shape=out_shapes,
        in_specs=[pl.BlockSpec(memory_space=pltpu.SMEM)]
        + [pl.BlockSpec(memory_space=pltpu.VMEM)] * len(operands),
        out_specs=[pl.BlockSpec(memory_space=pltpu.VMEM)] * len(out_shapes),
        scratch_shapes=[pltpu.VMEM(s, bf16) for s in scratch],
        compiler_params=pltpu.CompilerParams(vmem_limit_bytes=48 * 1024 * 1024),
        cost_estimate=pl.CostEstimate(flops=flops, bytes_accessed=moved, transcendentals=0),
        name=name,
    )(at, *operands)


def per_device(grad, left_basis, right_basis, left_stat, right_stat, first_moment, second_moment):
    dp, z = lax.axis_index("dp"), lax.axis_index("mp")
    at = jnp.stack([dp % SIDE, dp // SIDE, z]).astype(jnp.int32)
    wide = [jax.ShapeDtypeStruct((256, 1024), bf16)] * 4
    tall = [jax.ShapeDtypeStruct((1024, 256), bf16)] * 4
    moment = [jax.ShapeDtypeStruct((256, 1024), f32)] * 2

    right_cols = lax.all_gather(right_basis, "dp", axis=0, tiled=True)
    lefts = ring_gather(swap_xz(left_basis), "z")
    grad_xz = ring_gather(swap_xy(grad), "y")
    half = call(half_kernel, "half", at, lefts + grad_xz, wide, [(4, 1024, 256)])
    half = total(ring_scatter(half, "x")).astype(bf16)
    halves = ring_gather(half, "z")
    first_new, second_new, *back = call(
        step_kernel, "step", at, halves + [right_cols, first_moment, second_moment], moment + wide
    )
    back = total(ring_scatter(back, "z")).astype(bf16)
    backs = ring_gather(back, "x")
    update = call(update_kernel, "update", at, lefts + backs, wide, [(4, 256, 1024)])
    update = swap_xy(total(ring_scatter(update, "y")).astype(bf16)).astype(f32)

    grad_yz = ring_gather(grad, "x")
    left_sum = call(left_kernel, "left_sum", at, grad_xz + grad_yz, tall, [(1024, 1024), (4, 256, 1024)])
    left_sum = swap_xz(total(ring_scatter(left_sum, "z")).astype(bf16)).astype(f32)
    left_stat_new = stat_decay * left_stat + (1.0 - stat_decay) * left_sum

    grad_xy = ring_gather(turn(grad), "z")
    right_sum = call(right_kernel, "right_sum", at, grad_xy + grad_xz, wide, [(1024, 1024)] * 2)
    right_sum = total(ring_scatter(right_sum, "x"))
    right_stat_new = stat_decay * right_stat + (1.0 - stat_decay) * right_sum
    return (update, left_stat_new, right_stat_new, first_new, second_new)


def solution(mesh):
    placed = (
        P(("layer", "dp"), "mp"),
        P(("layer", "mp"), "dp"),
        P(("layer", "dp"), "mp"),
        P(("layer", "mp"), "dp"),
        P(("layer", "dp"), "mp"),
        P(("layer", "dp"), "mp"),
        P(("layer", "dp"), "mp"),
    )
    return jax.shard_map(
        per_device,
        mesh=mesh,
        in_specs=placed,
        out_specs=(
            P(("layer", "dp"), "mp"),
            P(("layer", "mp"), "dp"),
            P(("layer", "dp"), "mp"),
            P(("layer", "dp"), "mp"),
            P(("layer", "dp"), "mp"),
        ),
        check_vma=False,
    )
```

time: 503 us -> 382 us (0.76)
  waiting for transfers between devices: 441 us -> 271 us
  starting transfers between devices: 0.54 us -> 60.4 us
  matrix products: 39 us -> 0 us
  Pallas kernels: 0 us -> 24.7 us
    ppermute x0 -> x38, waiting for transfers between devices: none -> 270 us  [permute(): return lax.ppermute(value, ('dp', 'mp'), pairs)]
    reduce_scatter x4 -> x0, waiting for transfers between devices: 214 us -> none  [the longest x1 85.6 us: per_device(): lax.psum_scatter(contract(left_cols, back_trans, 1, 1).astype(jnp.bfloat1...]
    all_gather x4 -> x0, waiting for transfers between devices: 159 us -> none  [the longest x1 72.6 us: per_device(): grad_cols = lax.all_gather(grad, 'dp', axis=0, tiled=True)]
    all_gather x1, waiting for transfers between devices: 64.7 us -> 0.01 us  [per_device(): right_cols = lax.all_gather(right_basis, 'dp', axis=0, tiled=True)]
    ppermute x0 -> x38, starting transfers between devices: none -> 60.3 us  [permute(): return lax.ppermute(value, ('dp', 'mp'), pairs)]
    dot_general x6 -> x0, matrix products: 39 us -> none  [the longest x5 32.4 us: contract(): lax.dot_general(left, right, (((left_dim,), (right_dim,)), ((), ())), pre...]
    pallas_call x0 -> x5, Pallas kernels: none -> 24.7 us  [call(): pl.pallas_call(kernel, out_shape=out_shapes, in_specs=[pl.BlockSpec(memor...]
  transfers between devices with their start and end apart: 9 -> 39, of which waited for: 9 -> 19; matrix products, arithmetic and copies ran while one was open for 9% -> 1% of each run, Pallas kernels for 0% -> 4%
where the time goes in v1:
time: 382 us; the launch traced here: 381 us
  waiting for transfers between devices  271 us (71%)
  starting transfers between devices  60.4 us (16%)
  Pallas kernels  24.7 us (6%)
  between operations  14.3 us (4%)
  local copies, waits for them, and re-layouts  6.27 us (2%)
  other arithmetic  5.07 us (1%)
    ppermute x38, waiting for transfers between devices, permute(): return lax.ppermute(value, ('dp', 'mp'), pairs)  270 us
    ppermute x38, starting transfers between devices, permute(): return lax.ppermute(value, ('dp', 'mp'), pairs)  60.3 us
    pallas_call x5, Pallas kernels, call(): pl.pallas_call(kernel, out_shape=out_shapes, in_specs=[pl.BlockSpec(memor...  24.7 us
  transfers between devices with their start and end apart: 39, of which 19 were waited for; matrix products, arithmetic and copies ran while one was open for 1% of the time, Pallas kernels for 4%

profile of v1, /device:TPU:24, one launch (start us, length us, event | category | flops | bytes accessed | tf_op | source)
XLA Modules:
  0.0 381.4 jit_solution(13381182230063870060)
XLA Ops:
  7.9 4.3 %collective-permute-start.4 = (bf16[256,1024]{1,0:T(8,128)(2,1)}, bf16[256,1024]{1,0:T(8,128)(2,1)S(1)}, u32[]{:S(2)}, u32[]{:S(2)}) collective-permute-start(bf16[256,1024]{1,0:T(8,128)(2,1)} %refs_4_.1), channel_id=1, source_target_pairs={{0,0},{1,1},{2,2},{3,3},{4,16},{5,17},{6,18},{7,19},{8,32},{9,33},... | collective-permute-start | bytes 1572872 | tf_op jit(solution)/shard_map/ppermute | solution.py:26
  12.2 5.4 %collective-permute-start = (bf16[1024,256]{1,0:T(8,128)(2,1)}, bf16[1024,256]{1,0:T(8,128)(2,1)}, u32[]{:S(2)}, u32[]{:S(2)}) collective-permute-start(bf16[1024,256]{1,0:T(8,128)(2,1)} %param.8), channel_id=1, source_target_pairs={{0,0},{1,4},{2,8},{3,12},{4,1},{5,5},{6,9},{7,13},{8,2},{9,6},{10,... | collective-permute-start | bytes 1572872 | tf_op jit(solution)/shard_map/ppermute | solution.py:26
  17.6 40.6 %collective-permute-done.4.refs_4_.refs_0_ = bf16[256,1024]{1,0:T(8,128)(2,1)S(1)} collective-permute-done((bf16[256,1024]{1,0:T(8,128)(2,1)}, bf16[256,1024]{1,0:T(8,128)(2,1)S(1)}, u32[]{:S(2)}, u32[]{:S(2)}) %collective-permute-start.4) | collective-permute-done | bytes 524320 | tf_op jit(solution)/shard_map/ppermute | solution.py:26
  58.2 3.2 collective-permute-start.7
  61.4 8.5 %collective-permute-start.1 = (bf16[1024,256]{1,0:T(8,128)(2,1)}, bf16[1024,256]{1,0:T(8,128)(2,1)}, u32[]{:S(2)}, u32[]{:S(2)}) collective-permute-start(bf16[1024,256]{1,0:T(8,128)(2,1)} %collective-permute-done.refs_0_), channel_id=1, source_target_pairs={{0,3},{1,0},{2,1},{3,2},{4,7},{5,4},{6,5},{7,6},{8,11},{9,8},{10,9... | collective-permute-start | bytes 1572872 | tf_op jit(solution)/shard_map/ppermute | solution.py:26
  69.9 23.5 %collective-permute-done.5.refs_5_.refs_1_ = bf16[256,1024]{1,0:T(8,128)(2,1)S(1)} collective-permute-done((bf16[256,1024]{1,0:T(8,128)(2,1)S(1)}, bf16[256,1024]{1,0:T(8,128)(2,1)S(1)}, u32[]{:S(2)}, u32[]{:S(2)}) %collective-permute-start.5) | collective-permute-done | bytes 524320 | tf_op jit(solution)/shard_map/ppermute | solution.py:26
  93.5 6.7 %collective-permute-done.7.refs_7_.refs_3_ = bf16[256,1024]{1,0:T(8,128)(2,1)S(1)} collective-permute-done((bf16[256,1024]{1,0:T(8,128)(2,1)S(1)}, bf16[256,1024]{1,0:T(8,128)(2,1)S(1)}, u32[]{:S(2)}, u32[]{:S(2)}) %collective-permute-start.7) | collective-permute-done | bytes 524320 | tf_op jit(solution)/shard_map/ppermute | solution.py:26
  100.2 7.4 %collective-permute-done.3.refs_3_ = bf16[1024,256]{1,0:T(8,128)(2,1)} collective-permute-done((bf16[1024,256]{1,0:T(8,128)(2,1)}, bf16[1024,256]{1,0:T(8,128)(2,1)}, u32[]{:S(2)}, u32[]{:S(2)}) %collective-permute-start.3) | collective-permute-done | bytes 524320 | tf_op jit(solution)/shard_map/ppermute | solution.py:26
  107.6 4.2 %half.1 = (bf16[256,1024]{1,0:T(8,128)(2,1)S(1)}, bf16[256,1024]{1,0:T(8,128)(2,1)S(1)}, bf16[256,1024]{1,0:T(8,128)(2,1)S(1)}, bf16[256,1024]{1,0:T(8,128)(2,1)S(1)}) custom-call(s32[3]{0:T(128)S(1)} %pad_add_fusion.at, bf16[1024,256]{1,0:T(8,128)(2,1)} %collective-permute-done.refs_0_, bf16[1024,256]{1,0:T(8,128)(2,1)} %collective-permute-done.1.refs_1_, ...), custom_call_target="tpu_custom_call" | custom-call | flops 2147483648 | bytes 6291456 | tf_op jit(solution)/shard_map/half/pallas_call | solution.py:137
  111.9 2.0 collective-permute-start.8
  113.9 12.8 %collective-permute-done.10 = bf16[256,1024]{1,0:T(8,128)(2,1)S(1)} collective-permute-done((bf16[256,1024]{1,0:T(8,128)(2,1)S(1)}, bf16[256,1024]{1,0:T(8,128)(2,1)S(1)}, u32[]{:S(2)}, u32[]{:S(2)}) %collective-permute-start.10) | collective-permute-done | bytes 524320 | tf_op jit(solution)/shard_map/ppermute | solution.py:26
  126.8 9.5 %collective-permute-done.8 = bf16[256,1024]{1,0:T(8,128)(2,1)S(1)} collective-permute-done((bf16[256,1024]{1,0:T(8,128)(2,1)S(1)}, bf16[256,1024]{1,0:T(8,128)(2,1)S(1)}, u32[]{:S(2)}, u32[]{:S(2)}) %collective-permute-start.8) | collective-permute-done | bytes 524320 | tf_op jit(solution)/shard_map/ppermute | solution.py:26
  136.7 1.3 collective-permute-start.12
  138.0 0.7 collective-permute-start.13
  138.7 12.8 %collective-permute-done.11.refs_1_ = bf16[256,1024]{1,0:T(8,128)(2,1)S(1)} collective-permute-done((bf16[256,1024]{1,0:T(8,128)(2,1)S(1)}, bf16[256,1024]{1,0:T(8,128)(2,1)S(1)}, u32[]{:S(2)}, u32[]{:S(2)}) %collective-permute-start.11) | collective-permute-done | bytes 524320 | tf_op jit(solution)/shard_map/ppermute | solution.py:26
  151.6 0.8 copy-done.6
  152.4 0.8 collective-permute-done.12.refs_2_
  153.2 0.8 copy-done.8
  154.0 7.1 %collective-permute-done.13.refs_3_ = bf16[256,1024]{1,0:T(8,128)(2,1)S(1)} collective-permute-done((bf16[256,1024]{1,0:T(8,128)(2,1)S(1)}, bf16[256,1024]{1,0:T(8,128)(2,1)S(1)}, u32[]{:S(2)}, u32[]{:S(2)}) %collective-permute-start.13) | collective-permute-done | bytes 524320 | tf_op jit(solution)/shard_map/ppermute | solution.py:26
  161.0 0.8 copy-done.10
  161.8 1.0 copy-done.7
  162.9 1.0 copy-done.9
  163.9 1.0 copy-done.11
  165.0 8.9 %step.1 = (f32[256,1024]{1,0:T(8,128)}, f32[256,1024]{1,0:T(8,128)}, bf16[256,1024]{1,0:T(8,128)(2,1)S(1)}, bf16[256,1024]{1,0:T(8,128)(2,1)S(1)}, bf16[256,1024...) custom-call(s32[3]{0:T(128)S(1)} %pad_add_fusion.at, bf16[256,1024]{1,0:T(8,128)(2,1)S(1)} %add_convert_fusion.3.refs_0_, ...), custom_call_target="tpu_custom_call" | custom-call | flops 4294967296 | bytes 16777216 | tf_op jit(solution)/shard_map/step/pallas_call | solution.py:137
  174.0 3.3 collective-permute-start.15
  177.3 2.6 collective-permute-start.31
  179.9 0.9 collective-permute-start.24
  180.8 19.9 %collective-permute-done.14 = bf16[256,1024]{1,0:T(8,128)(2,1)S(1)} collective-permute-done((bf16[256,1024]{1,0:T(8,128)(2,1)S(1)}, bf16[256,1024]{1,0:T(8,128)(2,1)S(1)}, u32[]{:S(2)}, u32[]{:S(2)}) %collective-permute-start.14) | collective-permute-done | bytes 524320 | tf_op jit(solution)/shard_map/ppermute | solution.py:26
  200.7 9.5 %collective-permute-start.25 = (bf16[256,1024]{1,0:T(8,128)(2,1)S(1)}, bf16[256,1024]{1,0:T(8,128)(2,1)S(1)}, u32[]{:S(2)}, u32[]{:S(2)}) collective-permute-start(bf16[256,1024]{1,0:T(8,128)(2,1)S(1)} %copy-done.1), channel_id=1, source_target_pairs={{0,8},{1,9},{2,10},{3,11},{4,12},{5,13},{6,14},{7,15},{8,0},{9,1},... | collective-permute-start | bytes 1572872 | tf_op jit(solution)/shard_map/ppermute | solution.py:26
  210.2 2.9 collective-permute-start.26
  213.9 15.5 %collective-permute-done.31.refs_0_ = bf16[256,1024]{1,0:T(8,128)(2,1)S(1)} collective-permute-done((bf16[256,1024]{1,0:T(8,128)(2,1)S(1)}, bf16[256,1024]{1,0:T(8,128)(2,1)S(1)}, u32[]{:S(2)}, u32[]{:S(2)}) %collective-permute-start.31) | collective-permute-done | bytes 524320 | tf_op jit(solution)/shard_map/ppermute | solution.py:26
  229.4 17.8 %collective-permute-done.24.refs_5_ = bf16[256,1024]{1,0:T(8,128)(2,1)S(1)} collective-permute-done((bf16[256,1024]{1,0:T(8,128)(2,1)S(1)}, bf16[256,1024]{1,0:T(8,128)(2,1)S(1)}, u32[]{:S(2)}, u32[]{:S(2)}) %collective-permute-start.24) | collective-permute-done | bytes 524320 | tf_op jit(solution)/shard_map/ppermute | solution.py:26
  248.0 3.6 left_sum.1
  251.7 6.1 %collective-permute-done.17.refs_5_ = bf16[256,1024]{1,0:T(8,128)(2,1)S(1)} collective-permute-done((bf16[256,1024]{1,0:T(8,128)(2,1)S(1)}, bf16[256,1024]{1,0:T(8,128)(2,1)S(1)}, u32[]{:S(2)}, u32[]{:S(2)}) %collective-permute-start.17) | collective-permute-done | bytes 524320 | tf_op jit(solution)/shard_map/ppermute | solution.py:26
  257.8 3.9 %collective-permute-done.19.refs_7_ = bf16[256,1024]{1,0:T(8,128)(2,1)S(1)} collective-permute-done((bf16[256,1024]{1,0:T(8,128)(2,1)S(1)}, bf16[256,1024]{1,0:T(8,128)(2,1)S(1)}, u32[]{:S(2)}, u32[]{:S(2)}) %collective-permute-start.19) | collective-permute-done | bytes 524320 | tf_op jit(solution)/shard_map/ppermute | solution.py:26
  261.7 0.8 collective-permute-start.28
  262.5 4.2 %update.1 = (bf16[256,1024]{1,0:T(8,128)(2,1)S(1)}, bf16[256,1024]{1,0:T(8,128)(2,1)S(1)}, bf16[256,1024]{1,0:T(8,128)(2,1)S(1)}, bf16[256,1024]{1,0:T(8,128)(2,1)S(1)}) custom-call(s32[3]{0:T(128)S(1)} %pad_add_fusion.at, bf16[1024,256]{1,0:T(8,128)(2,1)} %collective-permute-done.refs_0_, bf16[1024,256]{1,0:T(8,128)(2,1)} %collective-permute-done.1.refs_1_, ...), custom_call_target="tpu_custom_call" | custom-call | flops 2147483648 | bytes 6291456 | tf_op jit(solution)/shard_map/update/pallas_call | solution.py:137
  266.9 7.0 %collective-permute-done.34.refs_3_ = bf16[256,1024]{1,0:T(8,128)(2,1)S(1)} collective-permute-done((bf16[256,1024]{1,0:T(8,128)(2,1)S(1)}, bf16[256,1024]{1,0:T(8,128)(2,1)S(1)}, u32[]{:S(2)}, u32[]{:S(2)}) %collective-permute-start.34) | collective-permute-done | bytes 524320 | tf_op jit(solution)/shard_map/ppermute | solution.py:26
  273.8 20.8 %collective-permute-done.27 = bf16[1024,256]{1,0:T(8,128)(2,1)S(1)} collective-permute-done((bf16[1024,256]{1,0:T(8,128)(2,1)S(1)}, bf16[1024,256]{1,0:T(8,128)(2,1)S(1)}, u32[]{:S(2)}, u32[]{:S(2)}) %collective-permute-start.27) | collective-permute-done | bytes 524320 | tf_op jit(solution)/shard_map/ppermute | solution.py:26
  294.7 3.8 right_sum.1
  298.6 6.5 %collective-permute-start.36 = (bf16[256,1024]{1,0:T(8,128)(2,1)S(1)}, bf16[256,1024]{1,0:T(8,128)(2,1)S(1)}, u32[]{:S(2)}, u32[]{:S(2)}) collective-permute-start(bf16[256,1024]{1,0:T(8,128)(2,1)S(1)} %get-tuple-element.45), channel_id=1, source_target_pairs={{0,8},{1,9},{2,10},{3,11},{4,12},{5,13},{6,14},{7,15},{8,0},{9,1},... | collective-permute-start | bytes 1572872 | tf_op jit(solution)/shard_map/ppermute | solution.py:26
  306.1 2.1 collective-permute-done.22
  308.6 6.7 %collective-permute-start.23 = (bf16[256,1024]{1,0:T(8,128)(2,1)S(1)}, bf16[256,1024]{1,0:T(8,128)(2,1)S(1)}, u32[]{:S(2)}, u32[]{:S(2)}) collective-permute-start(bf16[256,1024]{1,0:T(8,128)(2,1)S(1)} %add_convert_fusion.1), channel_id=1, source_target_pairs={{0,0},{1,1},{2,2},{3,3},{4,16},{5,17},{6,18},{7,19},{8,32},{9,33},... | collective-permute-start | bytes 1572872 | tf_op jit(solution)/shard_map/ppermute | solution.py:26
  315.3 16.3 %collective-permute-done.35 = bf16[256,1024]{1,0:T(8,128)(2,1)S(1)} collective-permute-done((bf16[256,1024]{1,0:T(8,128)(2,1)S(1)}, bf16[256,1024]{1,0:T(8,128)(2,1)S(1)}, u32[]{:S(2)}, u32[]{:S(2)}) %collective-permute-start.35) | collective-permute-done | bytes 524320 | tf_op jit(solution)/shard_map/ppermute | solution.py:26
  331.6 1.4 multiply_add_fusion
  333.1 1.1 multiply_add_fusion.1
  334.2 39.2 %collective-permute-done.23 = bf16[256,1024]{1,0:T(8,128)(2,1)S(1)} collective-permute-done((bf16[256,1024]{1,0:T(8,128)(2,1)S(1)}, bf16[256,1024]{1,0:T(8,128)(2,1)S(1)}, u32[]{:S(2)}, u32[]{:S(2)}) %collective-permute-start.23) | collective-permute-done | bytes 524320 | tf_op jit(solution)/shard_map/ppermute | solution.py:26
  373.4 1.1 convert_element_type.93
  (76 shorter events, 4.7 us)
Async XLA Ops:
  7.2 154.7 %copy-start = (f32[256,1024]{1,0:T(8,128)S(1)}, f32[256,1024]{1,0:T(8,128)}, u32[]{:S(2)}) copy-start(f32[256,1024]{1,0:T(8,128)} %refs_5_.1) | copy-start | bytes 3145732
  7.2 154.7 %all-gather.2.cloned.1.call-start = ((), (), s32[]{:S(2)}) async-start(), calls=%async_computation | async-start | bytes 8912896 | tf_op jit(solution)/shard_map/all_gather | solution.py:157
  7.9 50.3 %collective-permute-start.4 = (bf16[256,1024]{1,0:T(8,128)(2,1)}, bf16[256,1024]{1,0:T(8,128)(2,1)S(1)}, u32[]{:S(2)}, u32[]{:S(2)}) collective-permute-start(bf16[256,1024]{1,0:T(8,128)(2,1)} %refs_4_.1), channel_id=1, source_target_pairs={{0,0},{1,1},{2,2},{3,3},{4,16},{5,17},{6,18},{7,19},{8,32},{9,33},... | collective-permute-start | bytes 1572872 | tf_op jit(solution)/shard_map/ppermute | solution.py:26
  12.2 49.2 %collective-permute-start = (bf16[1024,256]{1,0:T(8,128)(2,1)}, bf16[1024,256]{1,0:T(8,128)(2,1)}, u32[]{:S(2)}, u32[]{:S(2)}) collective-permute-start(bf16[1024,256]{1,0:T(8,128)(2,1)} %param.8), channel_id=1, source_target_pairs={{0,0},{1,4},{2,8},{3,12},{4,1},{5,5},{6,9},{7,13},{8,2},{9,6},{10,... | collective-permute-start | bytes 1572872 | tf_op jit(solution)/shard_map/ppermute | solution.py:26
  58.2 35.2 %collective-permute-start.5 = (bf16[256,1024]{1,0:T(8,128)(2,1)S(1)}, bf16[256,1024]{1,0:T(8,128)(2,1)S(1)}, u32[]{:S(2)}, u32[]{:S(2)}) collective-permute-start(bf16[256,1024]{1,0:T(8,128)(2,1)S(1)} %collective-permute-done.4.refs_4_.refs_0_), channel_id=1, source_target_pairs={{0,48},{1,49},{2,50},{3,51},{4,52},{5,53},{6,54},{7,55},{8,56},{9,... | collective-permute-start | bytes 1572872 | tf_op jit(solution)/shard_map/ppermute | solution.py:26
  58.2 35.3 %collective-permute-start.6 = (bf16[256,1024]{1,0:T(8,128)(2,1)S(1)}, bf16[256,1024]{1,0:T(8,128)(2,1)S(1)}, u32[]{:S(2)}, u32[]{:S(2)}) collective-permute-start(bf16[256,1024]{1,0:T(8,128)(2,1)S(1)} %collective-permute-done.4.refs_4_.refs_0_), channel_id=1, source_target_pairs={{0,32},{1,33},{2,34},{3,35},{4,36},{5,37},{6,38},{7,39},{8,40},{9,... | collective-permute-start | bytes 1572872 | tf_op jit(solution)/shard_map/ppermute | solution.py:26
  58.2 42.0 %collective-permute-start.7 = (bf16[256,1024]{1,0:T(8,128)(2,1)S(1)}, bf16[256,1024]{1,0:T(8,128)(2,1)S(1)}, u32[]{:S(2)}, u32[]{:S(2)}) collective-permute-start(bf16[256,1024]{1,0:T(8,128)(2,1)S(1)} %collective-permute-done.4.refs_4_.refs_0_), channel_id=1, source_target_pairs={{0,16},{1,17},{2,18},{3,19},{4,20},{5,21},{6,22},{7,23},{8,24},{9,... | collective-permute-start | bytes 1572872 | tf_op jit(solution)/shard_map/ppermute | solution.py:26
  61.4 38.8 %collective-permute-start.1 = (bf16[1024,256]{1,0:T(8,128)(2,1)}, bf16[1024,256]{1,0:T(8,128)(2,1)}, u32[]{:S(2)}, u32[]{:S(2)}) collective-permute-start(bf16[1024,256]{1,0:T(8,128)(2,1)} %collective-permute-done.refs_0_), channel_id=1, source_target_pairs={{0,3},{1,0},{2,1},{3,2},{4,7},{5,4},{6,5},{7,6},{8,11},{9,8},{10,9... | collective-permute-start | bytes 1572872 | tf_op jit(solution)/shard_map/ppermute | solution.py:26
  69.9 30.3 %collective-permute-start.2 = (bf16[1024,256]{1,0:T(8,128)(2,1)}, bf16[1024,256]{1,0:T(8,128)(2,1)}, u32[]{:S(2)}, u32[]{:S(2)}) collective-permute-start(bf16[1024,256]{1,0:T(8,128)(2,1)} %collective-permute-done.refs_0_), channel_id=1, source_target_pairs={{0,2},{1,3},{2,0},{3,1},{4,6},{5,7},{6,4},{7,5},{8,10},{9,11},{10,... | collective-permute-start | bytes 1572872 | tf_op jit(solution)/shard_map/ppermute | solution.py:26
  93.4 14.2 %collective-permute-start.3 = (bf16[1024,256]{1,0:T(8,128)(2,1)}, bf16[1024,256]{1,0:T(8,128)(2,1)}, u32[]{:S(2)}, u32[]{:S(2)}) collective-permute-start(bf16[1024,256]{1,0:T(8,128)(2,1)} %collective-permute-done.refs_0_), channel_id=1, source_target_pairs={{0,1},{1,2},{2,3},{3,0},{4,5},{5,6},{6,7},{7,4},{8,9},{9,10},{10,1... | collective-permute-start | bytes 1572872 | tf_op jit(solution)/shard_map/ppermute | solution.py:26
  93.5 42.7 %copy-start.2 = (bf16[256,1024]{1,0:T(8,128)(2,1)}, bf16[256,1024]{1,0:T(8,128)(2,1)S(1)}, u32[]{:S(2)}) copy-start(bf16[256,1024]{1,0:T(8,128)(2,1)S(1)} %collective-permute-done.6.refs_6_.refs_2_) | copy-start | bytes 1572868
  100.2 7.4 %copy-start.4 = (bf16[256,1024]{1,0:T(8,128)(2,1)}, bf16[256,1024]{1,0:T(8,128)(2,1)S(1)}, u32[]{:S(2)}) copy-start(bf16[256,1024]{1,0:T(8,128)(2,1)S(1)} %collective-permute-done.7.refs_7_.refs_3_) | copy-start | bytes 1572868
  111.8 14.9 %collective-permute-start.10 = (bf16[256,1024]{1,0:T(8,128)(2,1)S(1)}, bf16[256,1024]{1,0:T(8,128)(2,1)S(1)}, u32[]{:S(2)}, u32[]{:S(2)}) collective-permute-start(bf16[256,1024]{1,0:T(8,128)(2,1)S(1)} %get-tuple-element.30), channel_id=1, source_target_pairs={{0,12},{1,13},{2,14},{3,15},{4,0},{5,1},{6,2},{7,3},{8,4},{9,5},{1... | collective-permute-start | bytes 1572872 | tf_op jit(solution)/shard_map/ppermute | solution.py:26
  111.9 24.3 %collective-permute-start.8 = (bf16[256,1024]{1,0:T(8,128)(2,1)S(1)}, bf16[256,1024]{1,0:T(8,128)(2,1)S(1)}, u32[]{:S(2)}, u32[]{:S(2)}) collective-permute-start(bf16[256,1024]{1,0:T(8,128)(2,1)S(1)} %get-tuple-element.28), channel_id=1, source_target_pairs={{0,4},{1,5},{2,6},{3,7},{4,8},{5,9},{6,10},{7,11},{8,12},{9,13},{1... | collective-permute-start | bytes 1572872 | tf_op jit(solution)/shard_map/ppermute | solution.py:26
  113.9 22.3 %collective-permute-start.9 = (bf16[256,1024]{1,0:T(8,128)(2,1)S(1)}, bf16[256,1024]{1,0:T(8,128)(2,1)S(1)}, u32[]{:S(2)}, u32[]{:S(2)}) collective-permute-start(bf16[256,1024]{1,0:T(8,128)(2,1)S(1)} %get-tuple-element.29), channel_id=1, source_target_pairs={{0,8},{1,9},{2,10},{3,11},{4,12},{5,13},{6,14},{7,15},{8,0},{9,1},... | collective-permute-start | bytes 1572872 | tf_op jit(solution)/shard_map/ppermute | solution.py:26
  136.6 40.7 %copy-start.1 = (bf16[256,1024]{1,0:T(8,128)(2,1)S(1)}, bf16[256,1024]{1,0:T(8,128)(2,1)}, u32[]{:S(2)}) copy-start(bf16[256,1024]{1,0:T(8,128)(2,1)} %refs_4_.1) | copy-start | bytes 1572868
  136.6 14.9 %collective-permute-start.11 = (bf16[256,1024]{1,0:T(8,128)(2,1)S(1)}, bf16[256,1024]{1,0:T(8,128)(2,1)S(1)}, u32[]{:S(2)}, u32[]{:S(2)}) collective-permute-start(bf16[256,1024]{1,0:T(8,128)(2,1)S(1)} %add_convert_fusion.3.refs_0_), channel_id=1, source_target_pairs={{0,3},{1,0},{2,1},{3,2},{4,7},{5,4},{6,5},{7,6},{8,11},{9,8},{10,9... | collective-permute-start | bytes 1572872 | tf_op jit(solution)/shard_map/ppermute | solution.py:26
  136.7 16.4 %collective-permute-start.12 = (bf16[256,1024]{1,0:T(8,128)(2,1)S(1)}, bf16[256,1024]{1,0:T(8,128)(2,1)S(1)}, u32[]{:S(2)}, u32[]{:S(2)}) collective-permute-start(bf16[256,1024]{1,0:T(8,128)(2,1)S(1)} %add_convert_fusion.3.refs_0_), channel_id=1, source_target_pairs={{0,2},{1,3},{2,0},{3,1},{4,6},{5,7},{6,4},{7,5},{8,10},{9,11},{10,... | collective-permute-start | bytes 1572872 | tf_op jit(solution)/shard_map/ppermute | solution.py:26
  138.0 23.0 %collective-permute-start.13 = (bf16[256,1024]{1,0:T(8,128)(2,1)S(1)}, bf16[256,1024]{1,0:T(8,128)(2,1)S(1)}, u32[]{:S(2)}, u32[]{:S(2)}) collective-permute-start(bf16[256,1024]{1,0:T(8,128)(2,1)S(1)} %add_convert_fusion.3.refs_0_), channel_id=1, source_target_pairs={{0,1},{1,2},{2,3},{3,0},{4,5},{5,6},{6,7},{7,4},{8,9},{9,10},{10,1... | collective-permute-start | bytes 1572872 | tf_op jit(solution)/shard_map/ppermute | solution.py:26
  161.8 1.0 copy-start.7
  165.0 83.1 %copy-start.3 = (bf16[256,1024]{1,0:T(8,128)(2,1)S(1)}, bf16[256,1024]{1,0:T(8,128)(2,1)}, u32[]{:S(2)}) copy-start(bf16[256,1024]{1,0:T(8,128)(2,1)} %copy-done.2) | copy-start | bytes 1572868
  165.0 83.1 %copy-start.5 = (bf16[256,1024]{1,0:T(8,128)(2,1)S(1)}, bf16[256,1024]{1,0:T(8,128)(2,1)}, u32[]{:S(2)}) copy-start(bf16[256,1024]{1,0:T(8,128)(2,1)} %copy-done.4) | copy-start | bytes 1572868
  173.9 26.9 %collective-permute-start.14 = (bf16[256,1024]{1,0:T(8,128)(2,1)S(1)}, bf16[256,1024]{1,0:T(8,128)(2,1)S(1)}, u32[]{:S(2)}, u32[]{:S(2)}) collective-permute-start(bf16[256,1024]{1,0:T(8,128)(2,1)S(1)} %get-tuple-element.32), channel_id=1, source_target_pairs={{0,1},{1,2},{2,3},{3,0},{4,5},{5,6},{6,7},{7,4},{8,9},{9,10},{10,1... | collective-permute-start | bytes 1572872 | tf_op jit(solution)/shard_map/ppermute | solution.py:26
  174.0 36.3 %collective-permute-start.15 = (bf16[256,1024]{1,0:T(8,128)(2,1)S(1)}, bf16[256,1024]{1,0:T(8,128)(2,1)S(1)}, u32[]{:S(2)}, u32[]{:S(2)}) collective-permute-start(bf16[256,1024]{1,0:T(8,128)(2,1)S(1)} %get-tuple-element.33), channel_id=1, source_target_pairs={{0,2},{1,3},{2,0},{3,1},{4,6},{5,7},{6,4},{7,5},{8,10},{9,11},{10,... | collective-permute-start | bytes 1572872 | tf_op jit(solution)/shard_map/ppermute | solution.py:26
  177.3 35.8 %collective-permute-start.16 = (bf16[256,1024]{1,0:T(8,128)(2,1)S(1)}, bf16[256,1024]{1,0:T(8,128)(2,1)S(1)}, u32[]{:S(2)}, u32[]{:S(2)}) collective-permute-start(bf16[256,1024]{1,0:T(8,128)(2,1)S(1)} %get-tuple-element.34), channel_id=1, source_target_pairs={{0,3},{1,0},{2,1},{3,2},{4,7},{5,4},{6,5},{7,6},{8,11},{9,8},{10,9... | collective-permute-start | bytes 1572872 | tf_op jit(solution)/shard_map/ppermute | solution.py:26
  177.3 52.1 %collective-permute-start.31 = (bf16[256,1024]{1,0:T(8,128)(2,1)S(1)}, bf16[256,1024]{1,0:T(8,128)(2,1)S(1)}, u32[]{:S(2)}, u32[]{:S(2)}) collective-permute-start(bf16[256,1024]{1,0:T(8,128)(2,1)S(1)} %copy-done.1), channel_id=1, source_target_pairs={{0,0},{1,16},{2,32},{3,48},{4,1},{5,17},{6,33},{7,49},{8,2},{9,18}... | collective-permute-start | bytes 1572872 | tf_op jit(solution)/shard_map/ppermute | solution.py:26
  179.9 67.3 %collective-permute-start.24 = (bf16[256,1024]{1,0:T(8,128)(2,1)S(1)}, bf16[256,1024]{1,0:T(8,128)(2,1)S(1)}, u32[]{:S(2)}, u32[]{:S(2)}) collective-permute-start(bf16[256,1024]{1,0:T(8,128)(2,1)S(1)} %copy-done.1), channel_id=1, source_target_pairs={{0,12},{1,13},{2,14},{3,15},{4,0},{5,1},{6,2},{7,3},{8,4},{9,5},{1... | collective-permute-start | bytes 1572872 | tf_op jit(solution)/shard_map/ppermute | solution.py:26
  200.7 46.5 %collective-permute-start.25 = (bf16[256,1024]{1,0:T(8,128)(2,1)S(1)}, bf16[256,1024]{1,0:T(8,128)(2,1)S(1)}, u32[]{:S(2)}, u32[]{:S(2)}) collective-permute-start(bf16[256,1024]{1,0:T(8,128)(2,1)S(1)} %copy-done.1), channel_id=1, source_target_pairs={{0,8},{1,9},{2,10},{3,11},{4,12},{5,13},{6,14},{7,15},{8,0},{9,1},... | collective-permute-start | bytes 1572872 | tf_op jit(solution)/shard_map/ppermute | solution.py:26
  210.2 37.0 %collective-permute-start.26 = (bf16[256,1024]{1,0:T(8,128)(2,1)S(1)}, bf16[256,1024]{1,0:T(8,128)(2,1)S(1)}, u32[]{:S(2)}, u32[]{:S(2)}) collective-permute-start(bf16[256,1024]{1,0:T(8,128)(2,1)S(1)} %copy-done.1), channel_id=1, source_target_pairs={{0,4},{1,5},{2,6},{3,7},{4,8},{5,9},{6,10},{7,11},{8,12},{9,13},{1... | collective-permute-start | bytes 1572872 | tf_op jit(solution)/shard_map/ppermute | solution.py:26
  213.5 44.3 %collective-permute-start.17 = (bf16[256,1024]{1,0:T(8,128)(2,1)S(1)}, bf16[256,1024]{1,0:T(8,128)(2,1)S(1)}, u32[]{:S(2)}, u32[]{:S(2)}) collective-permute-start(bf16[256,1024]{1,0:T(8,128)(2,1)S(1)} %add_convert_fusion.2.refs_4_), channel_id=1, source_target_pairs={{0,12},{1,13},{2,14},{3,15},{4,0},{5,1},{6,2},{7,3},{8,4},{9,5},{1... | collective-permute-start | bytes 1572872 | tf_op jit(solution)/shard_map/ppermute | solution.py:26
  229.4 28.4 %collective-permute-start.18 = (bf16[256,1024]{1,0:T(8,128)(2,1)S(1)}, bf16[256,1024]{1,0:T(8,128)(2,1)S(1)}, u32[]{:S(2)}, u32[]{:S(2)}) collective-permute-start(bf16[256,1024]{1,0:T(8,128)(2,1)S(1)} %add_convert_fusion.2.refs_4_), channel_id=1, source_target_pairs={{0,8},{1,9},{2,10},{3,11},{4,12},{5,13},{6,14},{7,15},{8,0},{9,1},... | collective-permute-start | bytes 1572872 | tf_op jit(solution)/shard_map/ppermute | solution.py:26
  247.2 14.5 %collective-permute-start.19 = (bf16[256,1024]{1,0:T(8,128)(2,1)S(1)}, bf16[256,1024]{1,0:T(8,128)(2,1)S(1)}, u32[]{:S(2)}, u32[]{:S(2)}) collective-permute-start(bf16[256,1024]{1,0:T(8,128)(2,1)S(1)} %add_convert_fusion.2.refs_4_), channel_id=1, source_target_pairs={{0,4},{1,5},{2,6},{3,7},{4,8},{5,9},{6,10},{7,11},{8,12},{9,13},{1... | collective-permute-start | bytes 1572872 | tf_op jit(solution)/shard_map/ppermute | solution.py:26
  247.2 19.5 %collective-permute-start.32 = (bf16[256,1024]{1,0:T(8,128)(2,1)S(1)}, bf16[256,1024]{1,0:T(8,128)(2,1)S(1)}, u32[]{:S(2)}, u32[]{:S(2)}) collective-permute-start(bf16[256,1024]{1,0:T(8,128)(2,1)S(1)} %collective-permute-done.31.refs_0_), channel_id=1, source_target_pairs={{0,3},{1,0},{2,1},{3,2},{4,7},{5,4},{6,5},{7,6},{8,11},{9,8},{10,9... | collective-permute-start | bytes 1572872 | tf_op jit(solution)/shard_map/ppermute | solution.py:26
  247.3 19.5 %collective-permute-start.33 = (bf16[256,1024]{1,0:T(8,128)(2,1)S(1)}, bf16[256,1024]{1,0:T(8,128)(2,1)S(1)}, u32[]{:S(2)}, u32[]{:S(2)}) collective-permute-start(bf16[256,1024]{1,0:T(8,128)(2,1)S(1)} %collective-permute-done.31.refs_0_), channel_id=1, source_target_pairs={{0,2},{1,3},{2,0},{3,1},{4,6},{5,7},{6,4},{7,5},{8,10},{9,11},{10,... | collective-permute-start | bytes 1572872 | tf_op jit(solution)/shard_map/ppermute | solution.py:26
  257.7 16.1 %collective-permute-start.34 = (bf16[256,1024]{1,0:T(8,128)(2,1)S(1)}, bf16[256,1024]{1,0:T(8,128)(2,1)S(1)}, u32[]{:S(2)}, u32[]{:S(2)}) collective-permute-start(bf16[256,1024]{1,0:T(8,128)(2,1)S(1)} %collective-permute-done.31.refs_0_), channel_id=1, source_target_pairs={{0,1},{1,2},{2,3},{3,0},{4,5},{5,6},{6,7},{7,4},{8,9},{9,10},{10,1... | collective-permute-start | bytes 1572872 | tf_op jit(solution)/shard_map/ppermute | solution.py:26
  257.8 36.9 %collective-permute-start.27 = (bf16[1024,256]{1,0:T(8,128)(2,1)S(1)}, bf16[1024,256]{1,0:T(8,128)(2,1)S(1)}, u32[]{:S(2)}, u32[]{:S(2)}) collective-permute-start(bf16[1024,256]{1,0:T(8,128)(2,1)S(1)} %get-tuple-element.40), channel_id=1, source_target_pairs={{0,1},{1,2},{2,3},{3,0},{4,5},{5,6},{6,7},{7,4},{8,9},{9,10},{10,1... | collective-permute-start | bytes 1572872 | tf_op jit(solution)/shard_map/ppermute | solution.py:26
  261.7 36.8 %collective-permute-start.28 = (bf16[1024,256]{1,0:T(8,128)(2,1)S(1)}, bf16[1024,256]{1,0:T(8,128)(2,1)S(1)}, u32[]{:S(2)}, u32[]{:S(2)}) collective-permute-start(bf16[1024,256]{1,0:T(8,128)(2,1)S(1)} %get-tuple-element.41), channel_id=1, source_target_pairs={{0,2},{1,3},{2,0},{3,1},{4,6},{5,7},{6,4},{7,5},{8,10},{9,11},{10,... | collective-permute-start | bytes 1572872 | tf_op jit(solution)/shard_map/ppermute | solution.py:26
  266.7 65.0 %copy-start.13 = (f32[256,1024]{1,0:T(8,128)S(1)}, f32[256,1024]{1,0:T(8,128)}, u32[]{:S(2)}) copy-start(f32[256,1024]{1,0:T(8,128)} %param.11) | copy-start | bytes 3145732
  266.7 31.9 %collective-permute-start.29 = (bf16[1024,256]{1,0:T(8,128)(2,1)S(1)}, bf16[1024,256]{1,0:T(8,128)(2,1)S(1)}, u32[]{:S(2)}, u32[]{:S(2)}) collective-permute-start(bf16[1024,256]{1,0:T(8,128)(2,1)S(1)} %get-tuple-element.42), channel_id=1, source_target_pairs={{0,3},{1,0},{2,1},{3,2},{4,7},{5,4},{6,5},{7,6},{8,11},{9,8},{10,9... | collective-permute-start | bytes 1572872 | tf_op jit(solution)/shard_map/ppermute | solution.py:26
  266.8 38.3 %collective-permute-start.20 = (bf16[256,1024]{1,0:T(8,128)(2,1)S(1)}, bf16[256,1024]{1,0:T(8,128)(2,1)S(1)}, u32[]{:S(2)}, u32[]{:S(2)}) collective-permute-start(bf16[256,1024]{1,0:T(8,128)(2,1)S(1)} %get-tuple-element.36), channel_id=1, source_target_pairs={{0,16},{1,17},{2,18},{3,19},{4,20},{5,21},{6,22},{7,23},{8,24},{9,... | collective-permute-start | bytes 1572872 | tf_op jit(solution)/shard_map/ppermute | solution.py:26
  273.8 31.5 %collective-permute-start.21 = (bf16[256,1024]{1,0:T(8,128)(2,1)S(1)}, bf16[256,1024]{1,0:T(8,128)(2,1)S(1)}, u32[]{:S(2)}, u32[]{:S(2)}) collective-permute-start(bf16[256,1024]{1,0:T(8,128)(2,1)S(1)} %get-tuple-element.37), channel_id=1, source_target_pairs={{0,32},{1,33},{2,34},{3,35},{4,36},{5,37},{6,38},{7,39},{8,40},{9,... | collective-permute-start | bytes 1572872 | tf_op jit(solution)/shard_map/ppermute | solution.py:26
  294.7 38.4 %copy-start.12 = (f32[1024,256]{1,0:T(8,128)S(1)}, f32[1024,256]{1,0:T(8,128)}, u32[]{:S(2)}) copy-start(f32[1024,256]{1,0:T(8,128)} %param.10) | copy-start | bytes 3145732
  294.7 13.5 %collective-permute-start.22 = (bf16[256,1024]{1,0:T(8,128)(2,1)S(1)}, bf16[256,1024]{1,0:T(8,128)(2,1)S(1)}, u32[]{:S(2)}, u32[]{:S(2)}) collective-permute-start(bf16[256,1024]{1,0:T(8,128)(2,1)S(1)} %get-tuple-element.38), channel_id=1, source_target_pairs={{0,48},{1,49},{2,50},{3,51},{4,52},{5,53},{6,54},{7,55},{8,56},{9,... | collective-permute-start | bytes 1572872 | tf_op jit(solution)/shard_map/ppermute | solution.py:26
  298.5 33.1 %collective-permute-start.35 = (bf16[256,1024]{1,0:T(8,128)(2,1)S(1)}, bf16[256,1024]{1,0:T(8,128)(2,1)S(1)}, u32[]{:S(2)}, u32[]{:S(2)}) collective-permute-start(bf16[256,1024]{1,0:T(8,128)(2,1)S(1)} %get-tuple-element.44), channel_id=1, source_target_pairs={{0,4},{1,5},{2,6},{3,7},{4,8},{5,9},{6,10},{7,11},{8,12},{9,13},{1... | collective-permute-start | bytes 1572872 | tf_op jit(solution)/shard_map/ppermute | solution.py:26
  298.6 33.1 %collective-permute-start.36 = (bf16[256,1024]{1,0:T(8,128)(2,1)S(1)}, bf16[256,1024]{1,0:T(8,128)(2,1)S(1)}, u32[]{:S(2)}, u32[]{:S(2)}) collective-permute-start(bf16[256,1024]{1,0:T(8,128)(2,1)S(1)} %get-tuple-element.45), channel_id=1, source_target_pairs={{0,8},{1,9},{2,10},{3,11},{4,12},{5,13},{6,14},{7,15},{8,0},{9,1},... | collective-permute-start | bytes 1572872 | tf_op jit(solution)/shard_map/ppermute | solution.py:26
  305.1 26.6 %collective-permute-start.37 = (bf16[256,1024]{1,0:T(8,128)(2,1)S(1)}, bf16[256,1024]{1,0:T(8,128)(2,1)S(1)}, u32[]{:S(2)}, u32[]{:S(2)}) collective-permute-start(bf16[256,1024]{1,0:T(8,128)(2,1)S(1)} %get-tuple-element.46), channel_id=1, source_target_pairs={{0,12},{1,13},{2,14},{3,15},{4,0},{5,1},{6,2},{7,3},{8,4},{9,5},{1... | collective-permute-start | bytes 1572872 | tf_op jit(solution)/shard_map/ppermute | solution.py:26
  305.4 27.7 %collective-permute-start.30 = (bf16[1024,256]{1,0:T(8,128)(2,1)S(1)}, bf16[1024,256]{1,0:T(8,128)(2,1)S(1)}, u32[]{:S(2)}, u32[]{:S(2)}) collective-permute-start(bf16[1024,256]{1,0:T(8,128)(2,1)S(1)} %add_convert_fusion), channel_id=1, source_target_pairs={{0,0},{1,4},{2,8},{3,12},{4,1},{5,5},{6,9},{7,13},{8,2},{9,6},{10,... | collective-permute-start | bytes 1572872 | tf_op jit(solution)/shard_map/ppermute | solution.py:26
  308.6 64.9 %collective-permute-start.23 = (bf16[256,1024]{1,0:T(8,128)(2,1)S(1)}, bf16[256,1024]{1,0:T(8,128)(2,1)S(1)}, u32[]{:S(2)}, u32[]{:S(2)}) collective-permute-start(bf16[256,1024]{1,0:T(8,128)(2,1)S(1)} %add_convert_fusion.1), channel_id=1, source_target_pairs={{0,0},{1,1},{2,2},{3,3},{4,16},{5,17},{6,18},{7,19},{8,32},{9,33},... | collective-permute-start | bytes 1572872 | tf_op jit(solution)/shard_map/ppermute | solution.py:26
  (7 other events, 6.1 us)
Sparse Core Ops, SparseCore 0:
  10.2 106.8 all-gather.1

commit v2 on v0

v2 whole, which is shorter than its diff:
```python
import jax
import jax.numpy as jnp
from jax import lax
from jax.experimental import pallas as pl
from jax.experimental.pallas import tpu as pltpu
from jax.sharding import PartitionSpec as P

stat_decay = 0.95
first_decay = 0.9
second_decay = 0.95
first_bias = 1.0 - 0.9**10
second_bias = 1.0 - 0.95**10
adam_eps = 1e-08

SIDE = 4
bf16, f32 = jnp.bfloat16, jnp.float32


def permute(value, target):
    pairs = []
    for layer in range(2):
        for y in range(SIDE):
            for x in range(SIDE):
                for z in range(SIDE):
                    a, b, c = (v % SIDE for v in target(layer, x, y, z))
                    pairs.append(
                        (((layer * SIDE + y) * SIDE + x) * SIDE + z, ((layer * SIDE + b) * SIDE + a) * SIDE + c)
                    )
    return lax.ppermute(value, ("layer", "dp", "mp"), pairs)


def moved(axis, by):
    def target(layer, x, y, z):
        name = {"p": "xy"[layer], "o": "yx"[layer]}.get(axis, axis)
        return (x + by * (name == "x"), y + by * (name == "y"), z + by * (name == "z"))

    return target


def shift(value, axis, by):
    return permute(value, moved(axis, by))


def ring_gather(value, axis):
    return [value, shift(value, axis, -1), shift(value, axis, 2), shift(value, axis, 1)]


def ring_scatter(parts, axis):
    return [
        parts[0],
        shift(parts[1], axis, 1),
        shift(parts[2], axis, 2),
        shift(parts[3], axis, -1),
    ]


def exchange(parts, axis):
    own, after, across, before = ring_scatter(parts, axis)
    return [own, before, across, after]


def left_blocks(parts):
    got = []
    for j, part in enumerate(parts):
        along = moved("x", j)
        got.append(
            permute(
                part,
                lambda layer, x, y, z, along=along: (x, z, y) if layer else along(layer, x, y, z),
            )
        )
    return [got[0], got[3], got[2], got[1]]


def after(value, *others):
    return lax.optimization_barrier((value, *others))[0]


def pick(value, block, dim):
    if dim == 0:
        return lax.dynamic_index_in_dim(value, block, 0, keepdims=False)
    return lax.dynamic_slice_in_dim(value, block * 256, 256, dim)


def total(parts):
    return (parts[0].astype(f32) + parts[1].astype(f32)) + (parts[2].astype(f32) + parts[3].astype(f32))


def contract(left, right, left_dim, right_dim):
    return lax.dot_general(
        left, right, (((left_dim,), (right_dim,)), ((), ())), preferred_element_type=f32
    )


def span(block):
    return pl.ds(pl.multiple_of(block % 4 * 256, 256), 256)


def place_left(at, lefts, left_abs):
    layer, p, z = at[0], at[1], at[3]
    for i in range(4):
        for s in range(4):
            row = jnp.where(layer == 0, z + i, 4 - s)
            col = jnp.where(layer == 0, p + s, z + i)
            left_abs[span(row), span(col)] = lefts[i][s]


def half_kernel(at, *refs):
    p, o = at[1], at[2]
    lefts, grads, outs, left_abs, grad_abs = refs[:4], refs[4:8], refs[8:12], refs[12], refs[13]
    place_left(at, lefts, left_abs)
    for i in range(4):
        for j in range(4):
            grad_abs[span(o + i), j * 256 : (j + 1) * 256] = grads[i][:, span(p + j)]
    for k in range(4):
        rows = slice(k * 256, (k + 1) * 256)
        half = contract(left_abs[:, rows], grad_abs[...], 0, 0).astype(bf16)
        for j in range(4):
            outs[j][rows, :] = half[:, j * 256 : (j + 1) * 256]


def rotate_kernel(at, *refs):
    p, o, z = at[1], at[2], at[3]
    halves, rights, outs, right_abs = refs[:4], refs[4:8], refs[8:12], refs[12]
    for i in range(4):
        right_abs[(o + i) % 4] = rights[i][...]
    right = jnp.concatenate([right_abs[(z + i) % 4] for i in range(4)], axis=0)
    for j in range(4):
        half = jnp.concatenate([halves[i][span(p + j), :] for i in range(4)], axis=1)
        outs[j][...] = contract(half, right, 1, 0).astype(bf16)


def back_kernel(at, *refs):
    p, o, z = at[1], at[2], at[3]
    directions, rights, outs, right_abs = refs[:4], refs[4:8], refs[8:12], refs[12]
    for i in range(4):
        right_abs[(o + i) % 4] = rights[i][...]
    direction = jnp.concatenate([d[...] for d in directions], axis=0)
    for j in range(4):
        back = contract(direction, right_abs[(z + j) % 4], 1, 1).astype(bf16)
        for i in range(4):
            outs[j][span(p + i), :] = back[i * 256 : (i + 1) * 256]


def update_kernel(at, *refs):
    p, o = at[1], at[2]
    lefts, backs, outs, left_abs, back_abs = refs[:4], refs[4:8], refs[8:12], refs[12], refs[13]
    place_left(at, lefts, left_abs)
    for i in range(4):
        back_abs[:, span(p + i)] = backs[i][...]
    for j in range(4):
        outs[j][...] = contract(left_abs[span(o + j), :], back_abs[...], 1, 0).astype(bf16)


def place_grads(at, along_o, along_p, both):
    layer, p, o = at[0], at[1], at[2]
    for i in range(4):
        both[layer, (o + i) % 4] = along_o[i][...]
        both[1 - layer, (p + i) % 4] = along_p[i][...]


def left_kernel(at, *refs):
    z, x = at[3], at[4]
    along_o, along_p, outs, both = refs[:4], refs[4:8], refs[8:12], refs[12]
    place_grads(at, along_o, along_p, both)
    for j in range(4):
        for s in range(4):
            outs[j][s] = contract(both[0, (z + j) % 4], both[1, (x + s) % 4], 1, 1).astype(bf16)


def right_kernel(at, *refs):
    z, x, y = at[3], at[4], at[5]
    others, along_o, along_p, outs, both, other_abs = refs[:4], refs[4:8], refs[8:12], refs[12:16], refs[16], refs[17]
    place_grads(at, along_o, along_p, both)
    for i in range(4):
        other_abs[(z + i) % 4] = others[i][...].reshape(1024, 256)
    grad = jnp.concatenate([both[1, (x + i) % 4] for i in range(4)], axis=0)
    for j in range(4):
        outs[j][...] = contract(other_abs[(y + j) % 4], grad, 0, 0).astype(bf16)


def left_stat_kernel(at, *refs):
    x = at[4]
    pieces, stat, out = refs[:4], refs[4], refs[5]
    for i in range(4):
        place = span(x + i)
        out[place, :] = stat_decay * stat[place, :] + (1.0 - stat_decay) * pieces[i][...].astype(f32)


def call(kernel, name, at, operands, out_shapes, scratch=()):
    flops = 2 * 1024**3
    moved = sum(v.size * v.dtype.itemsize for v in operands)
    moved += sum(v.size * v.dtype.itemsize for v in out_shapes)
    return list(pl.pallas_call(
        kernel,
        out_shape=out_shapes,
        in_specs=[pl.BlockSpec(memory_space=pltpu.SMEM)]
        + [pl.BlockSpec(memory_space=pltpu.VMEM)] * len(operands),
        out_specs=[pl.BlockSpec(memory_space=pltpu.VMEM)] * len(out_shapes),
        scratch_shapes=[pltpu.VMEM(s, bf16) for s in scratch],
        compiler_params=pltpu.CompilerParams(vmem_limit_bytes=48 * 1024 * 1024),
        cost_estimate=pl.CostEstimate(flops=flops, bytes_accessed=moved, transcendentals=0),
        name=name,
    )(at, *operands))


def per_device(grad, left_basis, right_basis, left_stat, right_stat, first_moment, second_moment):
    layer, dp, z = lax.axis_index("layer"), lax.axis_index("dp"), lax.axis_index("mp")
    x, y = dp % SIDE, dp // SIDE
    p, o = jnp.where(layer == 0, x, y), jnp.where(layer == 0, y, x)
    at = jnp.stack([layer, p, o, z, x, y]).astype(jnp.int32)
    wide = [jax.ShapeDtypeStruct((256, 1024), bf16)] * 4
    tall = [jax.ShapeDtypeStruct((1024, 256), bf16)] * 4
    cut = [jax.ShapeDtypeStruct((4, 256, 256), bf16)] * 4
    square, blocks = (1024, 1024), (4, 256, 1024)

    left = left_basis.reshape(4, 256, 256)
    left = left_blocks([pick(left, jnp.where(layer == 0, (x + j) % SIDE, j), 0) for j in range(4)])
    grads = ring_gather(grad, "o")
    lefts = ring_gather(jnp.stack(left), "z")
    right = permute(right_basis, lambda layer, x, y, z: (y, x, z) if layer else (x, y, z))
    rights = ring_gather(right, "o")
    other = exchange([pick(grad, (x + j) % SIDE, 1) for j in range(4)], "x")

    half = call(half_kernel, "half", at, lefts + grads, tall, [square, square])
    half = total(ring_scatter(half, "p")).astype(bf16)

    halves = ring_gather(after(half, *rights), "z")
    rows = ring_gather(after(grad, half), "p")

    rotated = call(rotate_kernel, "rotate", at, halves + rights, wide, [blocks])
    rotated[0] = after(rotated[0], *rows)
    rotated = total(ring_scatter(rotated, "p"))
    first_new = first_decay * first_moment + (1.0 - first_decay) * rotated
    second_new = second_decay * second_moment + (1.0 - second_decay) * rotated * rotated
    direction = (first_new / first_bias / (jnp.sqrt(second_new / second_bias) + adam_eps)).astype(bf16)
    others = ring_gather(after(jnp.stack(other), halves[1]), "z")

    directions = ring_gather(after(direction, *others), "p")
    left_sum = call(left_kernel, "left_sum", at, grads + [after(rows[0], direction)] + rows[1:], cut, [(2, *blocks)])
    left_sum = total(ring_scatter(left_sum, "z")).astype(bf16)

    back = call(back_kernel, "back", at, directions + rights, tall, [blocks])
    back[0] = after(back[0], left_sum)
    others[0] = after(others[0], directions[1])
    right_sum = call(right_kernel, "right_sum", at, others + grads + rows, wide, [(2, *blocks), (4, 1024, 256)])
    back = total(ring_scatter(back, "z")).astype(bf16)
    right_sum = ring_scatter(right_sum, "y")

    backs = ring_gather(after(back, *right_sum), "p")
    pieces = exchange([left_sum[s] for s in range(4)], "x")
    right_stat_new = stat_decay * right_stat + (1.0 - stat_decay) * total(right_sum)
    update = call(update_kernel, "update", at, lefts + backs, wide, [square, square])
    update = total(ring_scatter(update, "o"))
    left_stat_new = call(
        left_stat_kernel, "left_stat", at, pieces + [left_stat], [jax.ShapeDtypeStruct((1024, 256), f32)]
    )[0]
    return (update, left_stat_new, right_stat_new, first_new, second_new)


def solution(mesh):
    placed = (
        P(("layer", "dp"), "mp"),
        P(("layer", "mp"), "dp"),
        P(("layer", "dp"), "mp"),
        P(("layer", "mp"), "dp"),
        P(("layer", "dp"), "mp"),
        P(("layer", "dp"), "mp"),
        P(("layer", "dp"), "mp"),
    )
    return jax.shard_map(
        per_device,
        mesh=mesh,
        in_specs=placed,
        out_specs=(
            P(("layer", "dp"), "mp"),
            P(("layer", "mp"), "dp"),
            P(("layer", "dp"), "mp"),
            P(("layer", "dp"), "mp"),
            P(("layer", "dp"), "mp"),
        ),
        check_vma=False,
    )
```

time: 503 us -> 268 us (0.53)
  waiting for transfers between devices: 441 us -> 121 us
  starting transfers between devices: 0.54 us -> 106 us
  matrix products: 39 us -> 0 us
  Pallas kernels: 0 us -> 26.3 us
  between operations: 13.9 us -> 0.99 us
    all_gather x5 -> x0, waiting for transfers between devices: 224 us -> none  [the longest x1 72.6 us: per_device(): grad_cols = lax.all_gather(grad, 'dp', axis=0, tiled=True)]
    reduce_scatter x4 -> x0, waiting for transfers between devices: 214 us -> none  [the longest x1 85.6 us: per_device(): lax.psum_scatter(contract(left_cols, back_trans, 1, 1).astype(jnp.bfloat1...]
    ppermute x0 -> x53, waiting for transfers between devices: none -> 121 us  [permute(): return lax.ppermute(value, ('layer', 'dp', 'mp'), pairs)]
    ppermute x0 -> x53, starting transfers between devices: none -> 106 us  [permute(): return lax.ppermute(value, ('layer', 'dp', 'mp'), pairs)]
    dot_general x6 -> x0, matrix products: 39 us -> none  [the longest x5 32.4 us: contract(): lax.dot_general(left, right, (((left_dim,), (right_dim,)), ((), ())), pre...]
    pallas_call x0 -> x7, Pallas kernels: none -> 26.3 us  [call(): pl.pallas_call(kernel, out_shape=out_shapes, in_specs=[pl.BlockSpec(memor...]
  transfers between devices with their start and end apart: 9 -> 53, of which waited for: 9 -> 24; matrix products, arithmetic and copies ran while one was open for 9% -> 2% of each run, Pallas kernels for 0% -> 10%
where the time goes in v2:
time: 268 us; the launch traced here: 266 us
  waiting for transfers between devices  121 us (45%)
  starting transfers between devices  106 us (40%)
  Pallas kernels  26.3 us (10%)
  other arithmetic  5.85 us (2%)
  local copies, waits for them, and re-layouts  4.87 us (2%)
    ppermute x53, waiting for transfers between devices, permute(): return lax.ppermute(value, ('layer', 'dp', 'mp'), pairs)  121 us
    ppermute x53, starting transfers between devices, permute(): return lax.ppermute(value, ('layer', 'dp', 'mp'), pairs)  106 us
    pallas_call x7, Pallas kernels, call(): pl.pallas_call(kernel, out_shape=out_shapes, in_specs=[pl.BlockSpec(memor...  26.3 us
  transfers between devices with their start and end apart: 53, of which 24 were waited for; matrix products, arithmetic and copies ran while one was open for 2% of the time, Pallas kernels for 10%

profile of v2, /device:TPU:24, one launch (start us, length us, event | category | flops | bytes accessed | tf_op | source)
XLA Modules:
  0.0 265.6 jit_solution(910992570044693866)
XLA Ops:
  2.7 3.5 %collective-permute-start.3 = (bf16[256,256]{1,0:T(8,128)(2,1)S(1)}, bf16[256,256]{1,0:T(8,128)(2,1)S(1)}, u32[]{:S(2)}, u32[]{:S(2)}) collective-permute-start(bf16[256,256]{1,0:T(8,128)(2,1)S(1)} %get-tuple-element.83), channel_id=1, source_target_pairs={{0,4},{1,5},{2,6},{3,7},{4,8},{5,9},{6,10},{7,11},{8,12},{9,13},{1... | collective-permute-start | bytes 393224 | tf_op jit(solution)/shard_map/ppermute | solution.py:29
  6.2 4.6 %collective-permute-start.2 = (bf16[256,256]{1,0:T(8,128)(2,1)S(1)}, bf16[256,256]{1,0:T(8,128)(2,1)S(1)}, u32[]{:S(2)}, u32[]{:S(2)}) collective-permute-start(bf16[256,256]{1,0:T(8,128)(2,1)S(1)} %get-tuple-element.84), channel_id=1, source_target_pairs={{0,8},{1,9},{2,10},{3,11},{4,12},{5,13},{6,14},{7,15},{8,0},{9,1},... | collective-permute-start | bytes 393224 | tf_op jit(solution)/shard_map/ppermute | solution.py:29
  10.8 3.3 %collective-permute-start.1 = (bf16[256,256]{1,0:T(8,128)(2,1)S(1)}, bf16[256,256]{1,0:T(8,128)(2,1)S(1)}, u32[]{:S(2)}, u32[]{:S(2)}) collective-permute-start(bf16[256,256]{1,0:T(8,128)(2,1)S(1)} %get-tuple-element.85), channel_id=1, source_target_pairs={{0,12},{1,13},{2,14},{3,15},{4,0},{5,1},{6,2},{7,3},{8,4},{9,5},{1... | collective-permute-start | bytes 393224 | tf_op jit(solution)/shard_map/ppermute | solution.py:29
  14.2 2.7 %collective-permute-start.8 = (bf16[256,1024]{1,0:T(8,128)(2,1)S(1)}, bf16[256,1024]{1,0:T(8,128)(2,1)}, u32[]{:S(2)}, u32[]{:S(2)}) collective-permute-start(bf16[256,1024]{1,0:T(8,128)(2,1)S(1)} %copy-done), channel_id=1, source_target_pairs={{0,32},{1,33},{2,34},{3,35},{4,36},{5,37},{6,38},{7,39},{8,40},{9,... | collective-permute-start | bytes 1572872 | tf_op jit(solution)/shard_map/ppermute | solution.py:29
  19.8 5.0 %collective-permute-start.5 = (bf16[4,256,256]{2,1,0:T(8,128)(2,1)S(1)}, bf16[4,256,256]{2,1,0:T(8,128)(2,1)S(1)}, u32[]{:S(2)}, u32[]{:S(2)}) collective-permute-start(bf16[4,256,256]{2,1,0:T(8,128)(2,1)S(1)} %pad_maximum_fusion.refs_0_), channel_id=1, source_target_pairs={{0,2},{1,3},{2,0},{3,1},{4,6},{5,7},{6,4},{7,5},{8,10},{9,11},{10,... | collective-permute-start | bytes 1572872 | tf_op jit(solution)/shard_map/ppermute | solution.py:29
  26.9 3.8 %collective-permute-done.7.refs_5_.refs_1_ = bf16[256,1024]{1,0:T(8,128)(2,1)} collective-permute-done((bf16[256,1024]{1,0:T(8,128)(2,1)S(1)}, bf16[256,1024]{1,0:T(8,128)(2,1)}, u32[]{:S(2)}, u32[]{:S(2)}) %collective-permute-start.7) | collective-permute-done | bytes 524320 | tf_op jit(solution)/shard_map/ppermute | solution.py:29
  31.0 14.7 %collective-permute-done.5.refs_2_ = bf16[4,256,256]{2,1,0:T(8,128)(2,1)S(1)} collective-permute-done((bf16[4,256,256]{2,1,0:T(8,128)(2,1)S(1)}, bf16[4,256,256]{2,1,0:T(8,128)(2,1)S(1)}, u32[]{:S(2)}, u32[]{:S(2)}) %collective-permute-start.5) | collective-permute-done | bytes 524320 | tf_op jit(solution)/shard_map/ppermute | solution.py:29
  45.7 4.5 %half.1 = (bf16[1024,256]{1,0:T(8,128)(2,1)S(1)}, bf16[1024,256]{1,0:T(8,128)(2,1)S(1)}, bf16[1024,256]{1,0:T(8,128)(2,1)S(1)}, bf16[1024,256]{1,0:T(8,128)(2,1)S(1)}) custom-call(s32[6]{0:T(128)S(1)} %stack.57.at, bf16[4,256,256]{2,1,0:T(8,128)(2,1)S(1)} %pad_maximum_fusion.refs_0_, bf16[4,256,256]{2,1,0:T(8,128)(2,1)S(1)} %collective-permute-done.4.refs_1_, ...), custom_call_target="tpu_custom_call" | custom-call | flops 2147483648 | bytes 6291456 | tf_op jit(solution)/shard_map/half/pallas_call | solution.py:194
  50.2 3.5 %collective-permute-start.10 = (bf16[1024,256]{1,0:T(8,128)(2,1)S(1)}, bf16[1024,256]{1,0:T(8,128)(2,1)S(1)}, u32[]{:S(2)}, u32[]{:S(2)}) collective-permute-start(bf16[1024,256]{1,0:T(8,128)(2,1)S(1)} %get-tuple-element.39), channel_id=1, source_target_pairs={{0,4},{1,5},{2,6},{3,7},{4,8},{5,9},{6,10},{7,11},{8,12},{9,13},{1... | collective-permute-start | bytes 1572872 | tf_op jit(solution)/shard_map/ppermute | solution.py:29
  53.7 2.4 collective-permute-start.11
  58.0 2.6 collective-permute-start.15
  61.8 5.8 %collective-permute-start.14 = (bf16[256,1024]{1,0:T(8,128)(2,1)S(1)}, bf16[256,1024]{1,0:T(8,128)(2,1)S(1)}, u32[]{:S(2)}, u32[]{:S(2)}) collective-permute-start(bf16[256,1024]{1,0:T(8,128)(2,1)S(1)} %collective-permute-done.13.refs_4_), channel_id=1, source_target_pairs={{0,48},{1,49},{2,50},{3,51},{4,52},{5,53},{6,54},{7,55},{8,56},{9,... | collective-permute-start | bytes 1572872 | tf_op jit(solution)/shard_map/ppermute | solution.py:29
  67.6 7.4 %collective-permute-done.11 = bf16[1024,256]{1,0:T(8,128)(2,1)S(1)} collective-permute-done((bf16[1024,256]{1,0:T(8,128)(2,1)S(1)}, bf16[1024,256]{1,0:T(8,128)(2,1)S(1)}, u32[]{:S(2)}, u32[]{:S(2)}) %collective-permute-start.11) | collective-permute-done | bytes 524320 | tf_op jit(solution)/shard_map/ppermute | solution.py:29
  76.1 7.5 %collective-permute-done.14.refs_5_ = bf16[256,1024]{1,0:T(8,128)(2,1)S(1)} collective-permute-done((bf16[256,1024]{1,0:T(8,128)(2,1)S(1)}, bf16[256,1024]{1,0:T(8,128)(2,1)S(1)}, u32[]{:S(2)}, u32[]{:S(2)}) %collective-permute-start.14) | collective-permute-done | bytes 524320 | tf_op jit(solution)/shard_map/ppermute | solution.py:29
  84.4 2.9 %collective-permute-start.18 = (bf16[1024,256]{1,0:T(8,128)(2,1)S(1)}, bf16[1024,256]{1,0:T(8,128)(2,1)}, u32[]{:S(2)}, u32[]{:S(2)}) collective-permute-start(bf16[1024,256]{1,0:T(8,128)(2,1)S(1)} %add_convert_fusion.2.refs_0_), channel_id=1, source_target_pairs={{0,2},{1,3},{2,0},{3,1},{4,6},{5,7},{6,4},{7,5},{8,10},{9,11},{10,... | collective-permute-start | bytes 1572872 | tf_op jit(solution)/shard_map/ppermute | solution.py:29
  87.7 2.4 collective-permute-start.22
  90.6 21.0 %collective-permute-done.19.refs_3_ = bf16[1024,256]{1,0:T(8,128)(2,1)} collective-permute-done((bf16[1024,256]{1,0:T(8,128)(2,1)S(1)}, bf16[1024,256]{1,0:T(8,128)(2,1)}, u32[]{:S(2)}, u32[]{:S(2)}) %collective-permute-start.19) | collective-permute-done | bytes 524320 | tf_op jit(solution)/shard_map/ppermute | solution.py:29
  111.6 2.8 %collective-permute-start.27 = (bf16[256,256]{1,0:T(8,128)(2,1)S(1)}, bf16[256,256]{1,0:T(8,128)(2,1)S(1)}, u32[]{:S(2)}, u32[]{:S(2)}) collective-permute-start(bf16[256,256]{1,0:T(8,128)(2,1)S(1)} %get-tuple-element.80), channel_id=1, source_target_pairs={{0,8},{1,9},{2,10},{3,11},{4,12},{5,13},{6,14},{7,15},{8,0},{9,1},... | collective-permute-start | bytes 393224 | tf_op jit(solution)/shard_map/ppermute | solution.py:29
  114.4 2.3 collective-permute-start.26
  117.8 4.1 %rotate.1 = (bf16[256,1024]{1,0:T(8,128)(2,1)S(1)}, bf16[256,1024]{1,0:T(8,128)(2,1)S(1)}, bf16[256,1024]{1,0:T(8,128)(2,1)S(1)}, bf16[256,1024]{1,0:T(8,128)(2,1)S(1)}) custom-call(s32[6]{0:T(128)S(1)} %stack.57.at, bf16[1024,256]{1,0:T(8,128)(2,1)S(1)} %add_convert_fusion.2.refs_0_, bf16[1024,256]{1,0:T(8,128)(2,1)} %collective-permute-done.17.refs_1_, ...), custom_call_target="tpu_custom_call" | custom-call | flops 2147483648 | bytes 6291456 | tf_op jit(solution)/shard_map/rotate/pallas_call | solution.py:194
  122.0 2.4 collective-permute-start.20
  124.4 3.1 %collective-permute-start.24 = (bf16[256,1024]{1,0:T(8,128)(2,1)S(1)}, bf16[256,1024]{1,0:T(8,128)(2,1)S(1)}, u32[]{:S(2)}, u32[]{:S(2)}) collective-permute-start(bf16[256,1024]{1,0:T(8,128)(2,1)S(1)} %get-tuple-element.47), channel_id=1, source_target_pairs={{0,8},{1,9},{2,10},{3,11},{4,12},{5,13},{6,14},{7,15},{8,0},{9,1},... | collective-permute-start | bytes 1572872 | tf_op jit(solution)/shard_map/ppermute | solution.py:29
  129.6 2.7 collective-permute-done.20.refs_5_.refs_9_
  132.3 3.5 %collective-permute-start.30 = (bf16[4,256,256]{2,1,0:T(8,128)(2,1)S(1)}, bf16[4,256,256]{2,1,0:T(8,128)(2,1)S(1)}, u32[]{:S(2)}, u32[]{:S(2)}) collective-permute-start(bf16[4,256,256]{2,1,0:T(8,128)(2,1)S(1)} %pad_maximum_fusion.1.refs_0_), channel_id=1, source_target_pairs={{0,2},{1,3},{2,0},{3,1},{4,6},{5,7},{6,4},{7,5},{8,10},{9,11},{10,... | collective-permute-start | bytes 1572872 | tf_op jit(solution)/shard_map/ppermute | solution.py:29
  135.8 5.5 %collective-permute-start.29 = (bf16[4,256,256]{2,1,0:T(8,128)(2,1)S(1)}, bf16[4,256,256]{2,1,0:T(8,128)(2,1)S(1)}, u32[]{:S(2)}, u32[]{:S(2)}) collective-permute-start(bf16[4,256,256]{2,1,0:T(8,128)(2,1)S(1)} %pad_maximum_fusion.1.refs_0_), channel_id=1, source_target_pairs={{0,3},{1,0},{2,1},{3,2},{4,7},{5,4},{6,5},{7,6},{8,11},{9,8},{10,9... | collective-permute-start | bytes 1572872 | tf_op jit(solution)/shard_map/ppermute | solution.py:29
  141.3 2.3 collective-permute-done.25
  143.6 2.2 divide_convert_fusion
  145.8 6.6 %collective-permute-done.31.refs_3_ = bf16[4,256,256]{2,1,0:T(8,128)(2,1)S(1)} collective-permute-done((bf16[4,256,256]{2,1,0:T(8,128)(2,1)S(1)}, bf16[4,256,256]{2,1,0:T(8,128)(2,1)S(1)}, u32[]{:S(2)}, u32[]{:S(2)}) %collective-permute-start.31) | collective-permute-done | bytes 524320 | tf_op jit(solution)/shard_map/ppermute | solution.py:29
  152.4 2.9 %collective-permute-done.29.refs_1_ = bf16[4,256,256]{2,1,0:T(8,128)(2,1)S(1)} collective-permute-done((bf16[4,256,256]{2,1,0:T(8,128)(2,1)S(1)}, bf16[4,256,256]{2,1,0:T(8,128)(2,1)S(1)}, u32[]{:S(2)}, u32[]{:S(2)}) %collective-permute-start.29) | collective-permute-done | bytes 524320 | tf_op jit(solution)/shard_map/ppermute | solution.py:29
  159.5 4.0 %left_sum.1 = (bf16[4,256,256]{2,1,0:T(8,128)(2,1)S(1)}, bf16[4,256,256]{2,1,0:T(8,128)(2,1)S(1)}, bf16[4,256,256]{2,1,0:T(8,128)(2,1)S(1)}, bf16[4,256,256]{2,1,0:T(8,128)(2,1)S(1)}) custom-call(s32[6]{0:T(128)S(1)} %stack.57.at, bf16[256,1024]{1,0:T(8,128)(2,1)S(1)} %copy-done, bf16[256,1024]{1,0:T(8,128)(2,1)} %collective-permute-done.7.refs_5_.refs_1_, ...), custom_call_target="tpu_custom_call" | custom-call | flops 2147483648 | bytes 6291456 | tf_op jit(solution)/shard_map/left_sum/pallas_call | solution.py:194
  164.0 3.7 %collective-permute-start.36 = (bf16[4,256,256]{2,1,0:T(8,128)(2,1)S(1)}, bf16[4,256,256]{2,1,0:T(8,128)(2,1)S(1)}, u32[]{:S(2)}, u32[]{:S(2)}) collective-permute-start(bf16[4,256,256]{2,1,0:T(8,128)(2,1)S(1)} %get-tuple-element.55), channel_id=1, source_target_pairs={{0,2},{1,3},{2,0},{3,1},{4,6},{5,7},{6,4},{7,5},{8,10},{9,11},{10,... | collective-permute-start | bytes 1572872 | tf_op jit(solution)/shard_map/ppermute | solution.py:29
  167.7 3.7 %collective-permute-done.34.refs_3_ = bf16[256,1024]{1,0:T(8,128)(2,1)S(1)} collective-permute-done((bf16[256,1024]{1,0:T(8,128)(2,1)S(1)}, bf16[256,1024]{1,0:T(8,128)(2,1)S(1)}, u32[]{:S(2)}, u32[]{:S(2)}) %collective-permute-start.34) | collective-permute-done | bytes 524320 | tf_op jit(solution)/shard_map/ppermute | solution.py:29
  171.3 2.6 collective-permute-start.37
  173.9 3.6 %back.1 = (bf16[1024,256]{1,0:T(8,128)(2,1)S(1)}, bf16[1024,256]{1,0:T(8,128)(2,1)S(1)}, bf16[1024,256]{1,0:T(8,128)(2,1)S(1)}, bf16[1024,256]{1,0:T(8,128)(2,1)S(1)}) custom-call(s32[6]{0:T(128)S(1)} %stack.57.at, bf16[256,1024]{1,0:T(8,128)(2,1)S(1)} %get-tuple-element.50.refs_0_, bf16[256,1024]{1,0:T(8,128)(2,1)S(1)} %collective-permute-done.32.refs_1_, ...), custom_call_target="tpu_custom_call" | custom-call | flops 2147483648 | bytes 6291456 | tf_op jit(solution)/shard_map/back/pallas_call | solution.py:194
  177.6 2.3 collective-permute-start.39
  180.8 4.6 %right_sum.1 = (bf16[256,1024]{1,0:T(8,128)(2,1)S(1)}, bf16[256,1024]{1,0:T(8,128)(2,1)S(1)}, bf16[256,1024]{1,0:T(8,128)(2,1)S(1)}, bf16[256,1024]{1,0:T(8,128)(2,1)S(1)}) custom-call(s32[6]{0:T(128)S(1)} %stack.57.at, bf16[4,256,256]{2,1,0:T(8,128)(2,1)S(1)} %pad_maximum_fusion.1.refs_0_, bf16[4,256,256]{2,1,0:T(8,128)(2,1)S(1)} %collective-permute-done.29.refs_1_, ...), custom_call_target="tpu_custom_call" | custom-call | flops 2147483648 | bytes 8388608 | tf_op jit(solution)/shard_map/right_sum/pallas_call | solution.py:194
  185.4 3.8 %collective-permute-done.36 = bf16[4,256,256]{2,1,0:T(8,128)(2,1)S(1)} collective-permute-done((bf16[4,256,256]{2,1,0:T(8,128)(2,1)S(1)}, bf16[4,256,256]{2,1,0:T(8,128)(2,1)S(1)}, u32[]{:S(2)}, u32[]{:S(2)}) %collective-permute-start.36) | collective-permute-done | bytes 524320 | tf_op jit(solution)/shard_map/ppermute | solution.py:29
  192.5 11.6 %collective-permute-start.42 = (bf16[256,1024]{1,0:T(8,128)(2,1)S(1)}, bf16[256,1024]{1,0:T(8,128)(2,1)S(1)}, u32[]{:S(2)}, u32[]{:S(2)}) collective-permute-start(bf16[256,1024]{1,0:T(8,128)(2,1)S(1)} %get-tuple-element.64), channel_id=1, source_target_pairs={{0,32},{1,33},{2,34},{3,35},{4,36},{5,37},{6,38},{7,39},{8,40},{9,... | collective-permute-start | bytes 1572872 | tf_op jit(solution)/shard_map/ppermute | solution.py:29
  206.1 5.5 %collective-permute-done.39 = bf16[1024,256]{1,0:T(8,128)(2,1)S(1)} collective-permute-done((bf16[1024,256]{1,0:T(8,128)(2,1)S(1)}, bf16[1024,256]{1,0:T(8,128)(2,1)S(1)}, u32[]{:S(2)}, u32[]{:S(2)}) %collective-permute-start.39) | collective-permute-done | bytes 524320 | tf_op jit(solution)/shard_map/ppermute | solution.py:29
  213.4 2.9 %collective-permute-done.42 = bf16[256,1024]{1,0:T(8,128)(2,1)S(1)} collective-permute-done((bf16[256,1024]{1,0:T(8,128)(2,1)S(1)}, bf16[256,1024]{1,0:T(8,128)(2,1)S(1)}, u32[]{:S(2)}, u32[]{:S(2)}) %collective-permute-start.42) | collective-permute-done | bytes 524320 | tf_op jit(solution)/shard_map/ppermute | solution.py:29
  216.3 6.7 %collective-permute-done.43 = bf16[256,1024]{1,0:T(8,128)(2,1)S(1)} collective-permute-done((bf16[256,1024]{1,0:T(8,128)(2,1)S(1)}, bf16[256,1024]{1,0:T(8,128)(2,1)S(1)}, u32[]{:S(2)}, u32[]{:S(2)}) %collective-permute-start.43) | collective-permute-done | bytes 524320 | tf_op jit(solution)/shard_map/ppermute | solution.py:29
  223.0 3.2 %collective-permute-start.44 = (bf16[1024,256]{1,0:T(8,128)(2,1)S(1)}, bf16[1024,256]{1,0:T(8,128)(2,1)S(1)}, u32[]{:S(2)}, u32[]{:S(2)}) collective-permute-start(bf16[1024,256]{1,0:T(8,128)(2,1)S(1)} %add_convert_fusion.refs_4_), channel_id=1, source_target_pairs={{0,12},{1,13},{2,14},{3,15},{4,0},{5,1},{6,2},{7,3},{8,4},{9,5},{1... | collective-permute-start | bytes 1572872 | tf_op jit(solution)/shard_map/ppermute | solution.py:29
  227.2 2.2 collective-permute-start.51
  229.4 13.8 %collective-permute-done.46.refs_7_ = bf16[1024,256]{1,0:T(8,128)(2,1)S(1)} collective-permute-done((bf16[1024,256]{1,0:T(8,128)(2,1)S(1)}, bf16[1024,256]{1,0:T(8,128)(2,1)S(1)}, u32[]{:S(2)}, u32[]{:S(2)}) %collective-permute-start.46) | collective-permute-done | bytes 524320 | tf_op jit(solution)/shard_map/ppermute | solution.py:29
  243.9 3.9 %update.1 = (bf16[256,1024]{1,0:T(8,128)(2,1)S(1)}, bf16[256,1024]{1,0:T(8,128)(2,1)S(1)}, bf16[256,1024]{1,0:T(8,128)(2,1)S(1)}, bf16[256,1024]{1,0:T(8,128)(2,1)S(1)}) custom-call(s32[6]{0:T(128)S(1)} %stack.57.at, bf16[4,256,256]{2,1,0:T(8,128)(2,1)S(1)} %pad_maximum_fusion.refs_0_, bf16[4,256,256]{2,1,0:T(8,128)(2,1)S(1)} %copy-done.5, ...), custom_call_target="tpu_custom_call" | custom-call | flops 2147483648 | bytes 6291456 | tf_op jit(solution)/shard_map/update/pallas_call | solution.py:194
  248.0 2.9 %collective-permute-start.48 = (bf16[256,1024]{1,0:T(8,128)(2,1)S(1)}, bf16[256,1024]{1,0:T(8,128)(2,1)S(1)}, u32[]{:S(2)}, u32[]{:S(2)}) collective-permute-start(bf16[256,1024]{1,0:T(8,128)(2,1)S(1)} %get-tuple-element.69), channel_id=1, source_target_pairs={{0,32},{1,33},{2,34},{3,35},{4,36},{5,37},{6,38},{7,39},{8,40},{9,... | collective-permute-start | bytes 1572872 | tf_op jit(solution)/shard_map/ppermute | solution.py:29
  254.4 2.7 %collective-permute-done.47 = bf16[256,1024]{1,0:T(8,128)(2,1)S(1)} collective-permute-done((bf16[256,1024]{1,0:T(8,128)(2,1)S(1)}, bf16[256,1024]{1,0:T(8,128)(2,1)S(1)}, u32[]{:S(2)}, u32[]{:S(2)}) %collective-permute-start.47) | collective-permute-done | bytes 524320 | tf_op jit(solution)/shard_map/ppermute | solution.py:29
  258.8 5.5 %collective-permute-done.49 = bf16[256,1024]{1,0:T(8,128)(2,1)S(1)} collective-permute-done((bf16[256,1024]{1,0:T(8,128)(2,1)S(1)}, bf16[256,1024]{1,0:T(8,128)(2,1)S(1)}, u32[]{:S(2)}, u32[]{:S(2)}) %collective-permute-start.49) | collective-permute-done | bytes 524320 | tf_op jit(solution)/shard_map/ppermute | solution.py:29
  (117 shorter events, 37.4 us)
Async XLA Ops:
  0.6 24.2 %collective-permute-start.9 = (bf16[256,1024]{1,0:T(8,128)(2,1)}, bf16[256,1024]{1,0:T(8,128)(2,1)S(1)}, u32[]{:S(2)}, u32[]{:S(2)}) collective-permute-start(bf16[256,1024]{1,0:T(8,128)(2,1)} %refs_8_), channel_id=1, source_target_pairs={{0,16},{1,17},{2,18},{3,19},{4,20},{5,21},{6,22},{7,23},{8,24},{9,... | collective-permute-start | bytes 1572872 | tf_op jit(solution)/shard_map/ppermute | solution.py:29
  2.0 12.2 %collective-permute-start = (bf16[256,256]{1,0:T(8,128)(2,1)S(1)}, bf16[256,256]{1,0:T(8,128)(2,1)S(1)}, u32[]{:S(2)}, u32[]{:S(2)}) collective-permute-start(bf16[256,256]{1,0:T(8,128)(2,1)S(1)} %get-tuple-element.82), channel_id=1, source_target_pairs={{0,0},{1,1},{2,2},{3,3},{4,4},{5,5},{6,6},{7,7},{8,8},{9,9},{10,10... | collective-permute-start | bytes 393224 | tf_op jit(solution)/shard_map/ppermute | solution.py:29
  2.7 14.2 %collective-permute-start.3 = (bf16[256,256]{1,0:T(8,128)(2,1)S(1)}, bf16[256,256]{1,0:T(8,128)(2,1)S(1)}, u32[]{:S(2)}, u32[]{:S(2)}) collective-permute-start(bf16[256,256]{1,0:T(8,128)(2,1)S(1)} %get-tuple-element.83), channel_id=1, source_target_pairs={{0,4},{1,5},{2,6},{3,7},{4,8},{5,9},{6,10},{7,11},{8,12},{9,13},{1... | collective-permute-start | bytes 393224 | tf_op jit(solution)/shard_map/ppermute | solution.py:29
  6.2 10.7 %collective-permute-start.2 = (bf16[256,256]{1,0:T(8,128)(2,1)S(1)}, bf16[256,256]{1,0:T(8,128)(2,1)S(1)}, u32[]{:S(2)}, u32[]{:S(2)}) collective-permute-start(bf16[256,256]{1,0:T(8,128)(2,1)S(1)} %get-tuple-element.84), channel_id=1, source_target_pairs={{0,8},{1,9},{2,10},{3,11},{4,12},{5,13},{6,14},{7,15},{8,0},{9,1},... | collective-permute-start | bytes 393224 | tf_op jit(solution)/shard_map/ppermute | solution.py:29
  14.2 11.0 %collective-permute-start.8 = (bf16[256,1024]{1,0:T(8,128)(2,1)S(1)}, bf16[256,1024]{1,0:T(8,128)(2,1)}, u32[]{:S(2)}, u32[]{:S(2)}) collective-permute-start(bf16[256,1024]{1,0:T(8,128)(2,1)S(1)} %copy-done), channel_id=1, source_target_pairs={{0,32},{1,33},{2,34},{3,35},{4,36},{5,37},{6,38},{7,39},{8,40},{9,... | collective-permute-start | bytes 1572872 | tf_op jit(solution)/shard_map/ppermute | solution.py:29
  16.9 13.8 %collective-permute-start.7 = (bf16[256,1024]{1,0:T(8,128)(2,1)S(1)}, bf16[256,1024]{1,0:T(8,128)(2,1)}, u32[]{:S(2)}, u32[]{:S(2)}) collective-permute-start(bf16[256,1024]{1,0:T(8,128)(2,1)S(1)} %copy-done), channel_id=1, source_target_pairs={{0,48},{1,49},{2,50},{3,51},{4,52},{5,53},{6,54},{7,55},{8,56},{9,... | collective-permute-start | bytes 1572872 | tf_op jit(solution)/shard_map/ppermute | solution.py:29
  17.8 13.2 %collective-permute-start.6 = (bf16[4,256,256]{2,1,0:T(8,128)(2,1)S(1)}, bf16[4,256,256]{2,1,0:T(8,128)(2,1)S(1)}, u32[]{:S(2)}, u32[]{:S(2)}) collective-permute-start(bf16[4,256,256]{2,1,0:T(8,128)(2,1)S(1)} %pad_maximum_fusion.refs_0_), channel_id=1, source_target_pairs={{0,1},{1,2},{2,3},{3,0},{4,5},{5,6},{6,7},{7,4},{8,9},{9,10},{10,1... | collective-permute-start | bytes 1572872 | tf_op jit(solution)/shard_map/ppermute | solution.py:29
  19.8 25.9 %collective-permute-start.5 = (bf16[4,256,256]{2,1,0:T(8,128)(2,1)S(1)}, bf16[4,256,256]{2,1,0:T(8,128)(2,1)S(1)}, u32[]{:S(2)}, u32[]{:S(2)}) collective-permute-start(bf16[4,256,256]{2,1,0:T(8,128)(2,1)S(1)} %pad_maximum_fusion.refs_0_), channel_id=1, source_target_pairs={{0,2},{1,3},{2,0},{3,1},{4,6},{5,7},{6,4},{7,5},{8,10},{9,11},{10,... | collective-permute-start | bytes 1572872 | tf_op jit(solution)/shard_map/ppermute | solution.py:29
  24.8 20.9 %collective-permute-start.4 = (bf16[4,256,256]{2,1,0:T(8,128)(2,1)S(1)}, bf16[4,256,256]{2,1,0:T(8,128)(2,1)S(1)}, u32[]{:S(2)}, u32[]{:S(2)}) collective-permute-start(bf16[4,256,256]{2,1,0:T(8,128)(2,1)S(1)} %pad_maximum_fusion.refs_0_), channel_id=1, source_target_pairs={{0,3},{1,0},{2,1},{3,2},{4,7},{5,4},{6,5},{7,6},{8,11},{9,8},{10,9... | collective-permute-start | bytes 1572872 | tf_op jit(solution)/shard_map/ppermute | solution.py:29
  25.2 32.3 %collective-permute-start.13 = (bf16[256,1024]{1,0:T(8,128)(2,1)}, bf16[256,1024]{1,0:T(8,128)(2,1)S(1)}, u32[]{:S(2)}, u32[]{:S(2)}) collective-permute-start(bf16[256,1024]{1,0:T(8,128)(2,1)} %param.9), channel_id=1, source_target_pairs={{0,0},{1,1},{2,2},{3,3},{4,4},{5,5},{6,6},{7,7},{8,8},{9,9},{10,10... | collective-permute-start | bytes 1572872 | tf_op jit(solution)/shard_map/ppermute | solution.py:29
  50.2 11.6 %collective-permute-start.10 = (bf16[1024,256]{1,0:T(8,128)(2,1)S(1)}, bf16[1024,256]{1,0:T(8,128)(2,1)S(1)}, u32[]{:S(2)}, u32[]{:S(2)}) collective-permute-start(bf16[1024,256]{1,0:T(8,128)(2,1)S(1)} %get-tuple-element.39), channel_id=1, source_target_pairs={{0,4},{1,5},{2,6},{3,7},{4,8},{5,9},{6,10},{7,11},{8,12},{9,13},{1... | collective-permute-start | bytes 1572872 | tf_op jit(solution)/shard_map/ppermute | solution.py:29
  53.7 21.3 %collective-permute-start.11 = (bf16[1024,256]{1,0:T(8,128)(2,1)S(1)}, bf16[1024,256]{1,0:T(8,128)(2,1)S(1)}, u32[]{:S(2)}, u32[]{:S(2)}) collective-permute-start(bf16[1024,256]{1,0:T(8,128)(2,1)S(1)} %get-tuple-element.40), channel_id=1, source_target_pairs={{0,8},{1,9},{2,10},{3,11},{4,12},{5,13},{6,14},{7,15},{8,0},{9,1},... | collective-permute-start | bytes 1572872 | tf_op jit(solution)/shard_map/ppermute | solution.py:29
  56.1 18.9 %collective-permute-start.12 = (bf16[1024,256]{1,0:T(8,128)(2,1)S(1)}, bf16[1024,256]{1,0:T(8,128)(2,1)S(1)}, u32[]{:S(2)}, u32[]{:S(2)}) collective-permute-start(bf16[1024,256]{1,0:T(8,128)(2,1)S(1)} %get-tuple-element.41), channel_id=1, source_target_pairs={{0,12},{1,13},{2,14},{3,15},{4,0},{5,1},{6,2},{7,3},{8,4},{9,5},{1... | collective-permute-start | bytes 1572872 | tf_op jit(solution)/shard_map/ppermute | solution.py:29
  57.5 17.7 %collective-permute-start.16 = (bf16[256,1024]{1,0:T(8,128)(2,1)S(1)}, bf16[256,1024]{1,0:T(8,128)(2,1)S(1)}, u32[]{:S(2)}, u32[]{:S(2)}) collective-permute-start(bf16[256,1024]{1,0:T(8,128)(2,1)S(1)} %collective-permute-done.13.refs_4_), channel_id=1, source_target_pairs={{0,16},{1,17},{2,18},{3,19},{4,20},{5,21},{6,22},{7,23},{8,24},{9,... | collective-permute-start | bytes 1572872 | tf_op jit(solution)/shard_map/ppermute | solution.py:29
  58.0 17.3 %collective-permute-start.15 = (bf16[256,1024]{1,0:T(8,128)(2,1)S(1)}, bf16[256,1024]{1,0:T(8,128)(2,1)S(1)}, u32[]{:S(2)}, u32[]{:S(2)}) collective-permute-start(bf16[256,1024]{1,0:T(8,128)(2,1)S(1)} %collective-permute-done.13.refs_4_), channel_id=1, source_target_pairs={{0,32},{1,33},{2,34},{3,35},{4,36},{5,37},{6,38},{7,39},{8,40},{9,... | collective-permute-start | bytes 1572872 | tf_op jit(solution)/shard_map/ppermute | solution.py:29
  61.8 21.8 %collective-permute-start.14 = (bf16[256,1024]{1,0:T(8,128)(2,1)S(1)}, bf16[256,1024]{1,0:T(8,128)(2,1)S(1)}, u32[]{:S(2)}, u32[]{:S(2)}) collective-permute-start(bf16[256,1024]{1,0:T(8,128)(2,1)S(1)} %collective-permute-done.13.refs_4_), channel_id=1, source_target_pairs={{0,48},{1,49},{2,50},{3,51},{4,52},{5,53},{6,54},{7,55},{8,56},{9,... | collective-permute-start | bytes 1572872 | tf_op jit(solution)/shard_map/ppermute | solution.py:29
  84.4 27.2 %collective-permute-start.19 = (bf16[1024,256]{1,0:T(8,128)(2,1)S(1)}, bf16[1024,256]{1,0:T(8,128)(2,1)}, u32[]{:S(2)}, u32[]{:S(2)}) collective-permute-start(bf16[1024,256]{1,0:T(8,128)(2,1)S(1)} %add_convert_fusion.2.refs_0_), channel_id=1, source_target_pairs={{0,1},{1,2},{2,3},{3,0},{4,5},{5,6},{6,7},{7,4},{8,9},{9,10},{10,1... | collective-permute-start | bytes 1572872 | tf_op jit(solution)/shard_map/ppermute | solution.py:29
  84.4 30.0 %collective-permute-start.18 = (bf16[1024,256]{1,0:T(8,128)(2,1)S(1)}, bf16[1024,256]{1,0:T(8,128)(2,1)}, u32[]{:S(2)}, u32[]{:S(2)}) collective-permute-start(bf16[1024,256]{1,0:T(8,128)(2,1)S(1)} %add_convert_fusion.2.refs_0_), channel_id=1, source_target_pairs={{0,2},{1,3},{2,0},{3,1},{4,6},{5,7},{6,4},{7,5},{8,10},{9,11},{10,... | collective-permute-start | bytes 1572872 | tf_op jit(solution)/shard_map/ppermute | solution.py:29
  87.3 29.4 %collective-permute-start.17 = (bf16[1024,256]{1,0:T(8,128)(2,1)S(1)}, bf16[1024,256]{1,0:T(8,128)(2,1)}, u32[]{:S(2)}, u32[]{:S(2)}) collective-permute-start(bf16[1024,256]{1,0:T(8,128)(2,1)S(1)} %add_convert_fusion.2.refs_0_), channel_id=1, source_target_pairs={{0,3},{1,0},{2,1},{3,2},{4,7},{5,4},{6,5},{7,6},{8,11},{9,8},{10,9... | collective-permute-start | bytes 1572872 | tf_op jit(solution)/shard_map/ppermute | solution.py:29
  87.7 39.9 %collective-permute-start.22 = (bf16[256,1024]{1,0:T(8,128)(2,1)S(1)}, bf16[256,1024]{1,0:T(8,128)(2,1)}, u32[]{:S(2)}, u32[]{:S(2)}) collective-permute-start(bf16[256,1024]{1,0:T(8,128)(2,1)S(1)} %copy-done), channel_id=1, source_target_pairs={{0,4},{1,5},{2,6},{3,7},{4,8},{5,9},{6,10},{7,11},{8,12},{9,13},{1... | collective-permute-start | bytes 1572872 | tf_op jit(solution)/shard_map/ppermute | solution.py:29
  90.2 31.8 %collective-permute-start.28 = (bf16[256,256]{1,0:T(8,128)(2,1)S(1)}, bf16[256,256]{1,0:T(8,128)(2,1)S(1)}, u32[]{:S(2)}, u32[]{:S(2)}) collective-permute-start(bf16[256,256]{1,0:T(8,128)(2,1)S(1)} %get-tuple-element.79), channel_id=1, source_target_pairs={{0,4},{1,5},{2,6},{3,7},{4,8},{5,9},{6,10},{7,11},{8,12},{9,13},{1... | collective-permute-start | bytes 393224 | tf_op jit(solution)/shard_map/ppermute | solution.py:29
  111.6 12.8 %collective-permute-start.27 = (bf16[256,256]{1,0:T(8,128)(2,1)S(1)}, bf16[256,256]{1,0:T(8,128)(2,1)S(1)}, u32[]{:S(2)}, u32[]{:S(2)}) collective-permute-start(bf16[256,256]{1,0:T(8,128)(2,1)S(1)} %get-tuple-element.80), channel_id=1, source_target_pairs={{0,8},{1,9},{2,10},{3,11},{4,12},{5,13},{6,14},{7,15},{8,0},{9,1},... | collective-permute-start | bytes 393224 | tf_op jit(solution)/shard_map/ppermute | solution.py:29
  116.7 12.8 %collective-permute-start.21 = (bf16[256,1024]{1,0:T(8,128)(2,1)S(1)}, bf16[256,1024]{1,0:T(8,128)(2,1)S(1)}, u32[]{:S(2)}, u32[]{:S(2)}) collective-permute-start(bf16[256,1024]{1,0:T(8,128)(2,1)S(1)} %copy-done), channel_id=1, source_target_pairs={{0,8},{1,9},{2,10},{3,11},{4,12},{5,13},{6,14},{7,15},{8,0},{9,1},... | collective-permute-start | bytes 1572872 | tf_op jit(solution)/shard_map/ppermute | solution.py:29
  124.4 11.5 %collective-permute-start.23 = (bf16[256,1024]{1,0:T(8,128)(2,1)S(1)}, bf16[256,1024]{1,0:T(8,128)(2,1)S(1)}, u32[]{:S(2)}, u32[]{:S(2)}) collective-permute-start(bf16[256,1024]{1,0:T(8,128)(2,1)S(1)} %get-tuple-element.46), channel_id=1, source_target_pairs={{0,4},{1,5},{2,6},{3,7},{4,8},{5,9},{6,10},{7,11},{8,12},{9,13},{1... | collective-permute-start | bytes 1572872 | tf_op jit(solution)/shard_map/ppermute | solution.py:29
  124.4 16.9 %collective-permute-start.24 = (bf16[256,1024]{1,0:T(8,128)(2,1)S(1)}, bf16[256,1024]{1,0:T(8,128)(2,1)S(1)}, u32[]{:S(2)}, u32[]{:S(2)}) collective-permute-start(bf16[256,1024]{1,0:T(8,128)(2,1)S(1)} %get-tuple-element.47), channel_id=1, source_target_pairs={{0,8},{1,9},{2,10},{3,11},{4,12},{5,13},{6,14},{7,15},{8,0},{9,1},... | collective-permute-start | bytes 1572872 | tf_op jit(solution)/shard_map/ppermute | solution.py:29
  127.5 16.0 %collective-permute-start.25 = (bf16[256,1024]{1,0:T(8,128)(2,1)S(1)}, bf16[256,1024]{1,0:T(8,128)(2,1)S(1)}, u32[]{:S(2)}, u32[]{:S(2)}) collective-permute-start(bf16[256,1024]{1,0:T(8,128)(2,1)S(1)} %get-tuple-element.48), channel_id=1, source_target_pairs={{0,12},{1,13},{2,14},{3,15},{4,0},{5,1},{6,2},{7,3},{8,4},{9,5},{1... | collective-permute-start | bytes 1572872 | tf_op jit(solution)/shard_map/ppermute | solution.py:29
  129.6 22.9 %collective-permute-start.31 = (bf16[4,256,256]{2,1,0:T(8,128)(2,1)S(1)}, bf16[4,256,256]{2,1,0:T(8,128)(2,1)S(1)}, u32[]{:S(2)}, u32[]{:S(2)}) collective-permute-start(bf16[4,256,256]{2,1,0:T(8,128)(2,1)S(1)} %pad_maximum_fusion.1.refs_0_), channel_id=1, source_target_pairs={{0,1},{1,2},{2,3},{3,0},{4,5},{5,6},{6,7},{7,4},{8,9},{9,10},{10,1... | collective-permute-start | bytes 1572872 | tf_op jit(solution)/shard_map/ppermute | solution.py:29
  132.3 20.1 %collective-permute-start.30 = (bf16[4,256,256]{2,1,0:T(8,128)(2,1)S(1)}, bf16[4,256,256]{2,1,0:T(8,128)(2,1)S(1)}, u32[]{:S(2)}, u32[]{:S(2)}) collective-permute-start(bf16[4,256,256]{2,1,0:T(8,128)(2,1)S(1)} %pad_maximum_fusion.1.refs_0_), channel_id=1, source_target_pairs={{0,2},{1,3},{2,0},{3,1},{4,6},{5,7},{6,4},{7,5},{8,10},{9,11},{10,... | collective-permute-start | bytes 1572872 | tf_op jit(solution)/shard_map/ppermute | solution.py:29
  135.8 19.5 %collective-permute-start.29 = (bf16[4,256,256]{2,1,0:T(8,128)(2,1)S(1)}, bf16[4,256,256]{2,1,0:T(8,128)(2,1)S(1)}, u32[]{:S(2)}, u32[]{:S(2)}) collective-permute-start(bf16[4,256,256]{2,1,0:T(8,128)(2,1)S(1)} %pad_maximum_fusion.1.refs_0_), channel_id=1, source_target_pairs={{0,3},{1,0},{2,1},{3,2},{4,7},{5,4},{6,5},{7,6},{8,11},{9,8},{10,9... | collective-permute-start | bytes 1572872 | tf_op jit(solution)/shard_map/ppermute | solution.py:29
  155.3 16.0 %collective-permute-start.34 = (bf16[256,1024]{1,0:T(8,128)(2,1)S(1)}, bf16[256,1024]{1,0:T(8,128)(2,1)S(1)}, u32[]{:S(2)}, u32[]{:S(2)}) collective-permute-start(bf16[256,1024]{1,0:T(8,128)(2,1)S(1)} %get-tuple-element.50.refs_0_), channel_id=1, source_target_pairs={{0,4},{1,5},{2,6},{3,7},{4,8},{5,9},{6,10},{7,11},{8,12},{9,13},{1... | collective-permute-start | bytes 1572872 | tf_op jit(solution)/shard_map/ppermute | solution.py:29
  156.5 17.5 %collective-permute-start.33 = (bf16[256,1024]{1,0:T(8,128)(2,1)S(1)}, bf16[256,1024]{1,0:T(8,128)(2,1)S(1)}, u32[]{:S(2)}, u32[]{:S(2)}) collective-permute-start(bf16[256,1024]{1,0:T(8,128)(2,1)S(1)} %get-tuple-element.50.refs_0_), channel_id=1, source_target_pairs={{0,8},{1,9},{2,10},{3,11},{4,12},{5,13},{6,14},{7,15},{8,0},{9,1},... | collective-permute-start | bytes 1572872 | tf_op jit(solution)/shard_map/ppermute | solution.py:29
  158.1 15.8 %collective-permute-start.32 = (bf16[256,1024]{1,0:T(8,128)(2,1)S(1)}, bf16[256,1024]{1,0:T(8,128)(2,1)S(1)}, u32[]{:S(2)}, u32[]{:S(2)}) collective-permute-start(bf16[256,1024]{1,0:T(8,128)(2,1)S(1)} %get-tuple-element.50.refs_0_), channel_id=1, source_target_pairs={{0,12},{1,13},{2,14},{3,15},{4,0},{5,1},{6,2},{7,3},{8,4},{9,5},{1... | collective-permute-start | bytes 1572872 | tf_op jit(solution)/shard_map/ppermute | solution.py:29
  163.5 16.4 %collective-permute-start.35 = (bf16[4,256,256]{2,1,0:T(8,128)(2,1)S(1)}, bf16[4,256,256]{2,1,0:T(8,128)(2,1)S(1)}, u32[]{:S(2)}, u32[]{:S(2)}) collective-permute-start(bf16[4,256,256]{2,1,0:T(8,128)(2,1)S(1)} %get-tuple-element.54), channel_id=1, source_target_pairs={{0,1},{1,2},{2,3},{3,0},{4,5},{5,6},{6,7},{7,4},{8,9},{9,10},{10,1... | collective-permute-start | bytes 1572872 | tf_op jit(solution)/shard_map/ppermute | solution.py:29
  164.0 25.3 %collective-permute-start.36 = (bf16[4,256,256]{2,1,0:T(8,128)(2,1)S(1)}, bf16[4,256,256]{2,1,0:T(8,128)(2,1)S(1)}, u32[]{:S(2)}, u32[]{:S(2)}) collective-permute-start(bf16[4,256,256]{2,1,0:T(8,128)(2,1)S(1)} %get-tuple-element.55), channel_id=1, source_target_pairs={{0,2},{1,3},{2,0},{3,1},{4,6},{5,7},{6,4},{7,5},{8,10},{9,11},{10,... | collective-permute-start | bytes 1572872 | tf_op jit(solution)/shard_map/ppermute | solution.py:29
  171.3 21.1 %collective-permute-start.37 = (bf16[4,256,256]{2,1,0:T(8,128)(2,1)S(1)}, bf16[4,256,256]{2,1,0:T(8,128)(2,1)S(1)}, u32[]{:S(2)}, u32[]{:S(2)}) collective-permute-start(bf16[4,256,256]{2,1,0:T(8,128)(2,1)S(1)} %get-tuple-element.56), channel_id=1, source_target_pairs={{0,3},{1,0},{2,1},{3,2},{4,7},{5,4},{6,5},{7,6},{8,11},{9,8},{10,9... | collective-permute-start | bytes 1572872 | tf_op jit(solution)/shard_map/ppermute | solution.py:29
  177.5 26.6 %collective-permute-start.38 = (bf16[1024,256]{1,0:T(8,128)(2,1)S(1)}, bf16[1024,256]{1,0:T(8,128)(2,1)S(1)}, u32[]{:S(2)}, u32[]{:S(2)}) collective-permute-start(bf16[1024,256]{1,0:T(8,128)(2,1)S(1)} %get-tuple-element.58), channel_id=1, source_target_pairs={{0,1},{1,2},{2,3},{3,0},{4,5},{5,6},{6,7},{7,4},{8,9},{9,10},{10,1... | collective-permute-start | bytes 1572872 | tf_op jit(solution)/shard_map/ppermute | solution.py:29
  177.6 34.1 %collective-permute-start.39 = (bf16[1024,256]{1,0:T(8,128)(2,1)S(1)}, bf16[1024,256]{1,0:T(8,128)(2,1)S(1)}, u32[]{:S(2)}, u32[]{:S(2)}) collective-permute-start(bf16[1024,256]{1,0:T(8,128)(2,1)S(1)} %get-tuple-element.59), channel_id=1, source_target_pairs={{0,2},{1,3},{2,0},{3,1},{4,6},{5,7},{6,4},{7,5},{8,10},{9,11},{10,... | collective-permute-start | bytes 1572872 | tf_op jit(solution)/shard_map/ppermute | solution.py:29
  179.9 33.2 %collective-permute-start.40 = (bf16[1024,256]{1,0:T(8,128)(2,1)S(1)}, bf16[1024,256]{1,0:T(8,128)(2,1)S(1)}, u32[]{:S(2)}, u32[]{:S(2)}) collective-permute-start(bf16[1024,256]{1,0:T(8,128)(2,1)S(1)} %get-tuple-element.60), channel_id=1, source_target_pairs={{0,3},{1,0},{2,1},{3,2},{4,7},{5,4},{6,5},{7,6},{8,11},{9,8},{10,9... | collective-permute-start | bytes 1572872 | tf_op jit(solution)/shard_map/ppermute | solution.py:29
  189.2 24.1 %collective-permute-start.41 = (bf16[256,1024]{1,0:T(8,128)(2,1)S(1)}, bf16[256,1024]{1,0:T(8,128)(2,1)S(1)}, u32[]{:S(2)}, u32[]{:S(2)}) collective-permute-start(bf16[256,1024]{1,0:T(8,128)(2,1)S(1)} %get-tuple-element.63), channel_id=1, source_target_pairs={{0,16},{1,17},{2,18},{3,19},{4,20},{5,21},{6,22},{7,23},{8,24},{9,... | collective-permute-start | bytes 1572872 | tf_op jit(solution)/shard_map/ppermute | solution.py:29
  192.5 23.8 %collective-permute-start.42 = (bf16[256,1024]{1,0:T(8,128)(2,1)S(1)}, bf16[256,1024]{1,0:T(8,128)(2,1)S(1)}, u32[]{:S(2)}, u32[]{:S(2)}) collective-permute-start(bf16[256,1024]{1,0:T(8,128)(2,1)S(1)} %get-tuple-element.64), channel_id=1, source_target_pairs={{0,32},{1,33},{2,34},{3,35},{4,36},{5,37},{6,38},{7,39},{8,40},{9,... | collective-permute-start | bytes 1572872 | tf_op jit(solution)/shard_map/ppermute | solution.py:29
  204.1 18.9 %collective-permute-start.43 = (bf16[256,1024]{1,0:T(8,128)(2,1)S(1)}, bf16[256,1024]{1,0:T(8,128)(2,1)S(1)}, u32[]{:S(2)}, u32[]{:S(2)}) collective-permute-start(bf16[256,1024]{1,0:T(8,128)(2,1)S(1)} %get-tuple-element.65), channel_id=1, source_target_pairs={{0,48},{1,49},{2,50},{3,51},{4,52},{5,53},{6,54},{7,55},{8,56},{9,... | collective-permute-start | bytes 1572872 | tf_op jit(solution)/shard_map/ppermute | solution.py:29
  223.0 20.1 %collective-permute-start.46 = (bf16[1024,256]{1,0:T(8,128)(2,1)S(1)}, bf16[1024,256]{1,0:T(8,128)(2,1)S(1)}, u32[]{:S(2)}, u32[]{:S(2)}) collective-permute-start(bf16[1024,256]{1,0:T(8,128)(2,1)S(1)} %add_convert_fusion.refs_4_), channel_id=1, source_target_pairs={{0,4},{1,5},{2,6},{3,7},{4,8},{5,9},{6,10},{7,11},{8,12},{9,13},{1... | collective-permute-start | bytes 1572872 | tf_op jit(solution)/shard_map/ppermute | solution.py:29
  223.0 20.1 %collective-permute-start.45 = (bf16[1024,256]{1,0:T(8,128)(2,1)S(1)}, bf16[1024,256]{1,0:T(8,128)(2,1)S(1)}, u32[]{:S(2)}, u32[]{:S(2)}) collective-permute-start(bf16[1024,256]{1,0:T(8,128)(2,1)S(1)} %add_convert_fusion.refs_4_), channel_id=1, source_target_pairs={{0,8},{1,9},{2,10},{3,11},{4,12},{5,13},{6,14},{7,15},{8,0},{9,1},... | collective-permute-start | bytes 1572872 | tf_op jit(solution)/shard_map/ppermute | solution.py:29
  223.0 20.1 %collective-permute-start.44 = (bf16[1024,256]{1,0:T(8,128)(2,1)S(1)}, bf16[1024,256]{1,0:T(8,128)(2,1)S(1)}, u32[]{:S(2)}, u32[]{:S(2)}) collective-permute-start(bf16[1024,256]{1,0:T(8,128)(2,1)S(1)} %add_convert_fusion.refs_4_), channel_id=1, source_target_pairs={{0,12},{1,13},{2,14},{3,15},{4,0},{5,1},{6,2},{7,3},{8,4},{9,5},{1... | collective-permute-start | bytes 1572872 | tf_op jit(solution)/shard_map/ppermute | solution.py:29
  226.3 24.7 %collective-permute-start.52 = (bf16[256,256]{1,0:T(8,128)(2,1)S(1)}, bf16[256,256]{1,0:T(8,128)(2,1)S(1)}, u32[]{:S(2)}, u32[]{:S(2)}) collective-permute-start(bf16[256,256]{1,0:T(8,128)(2,1)S(1)} %get-tuple-element.74), channel_id=1, source_target_pairs={{0,4},{1,5},{2,6},{3,7},{4,8},{5,9},{6,10},{7,11},{8,12},{9,13},{1... | collective-permute-start | bytes 393224 | tf_op jit(solution)/shard_map/ppermute | solution.py:29
  227.2 24.1 %collective-permute-start.51 = (bf16[256,256]{1,0:T(8,128)(2,1)S(1)}, bf16[256,256]{1,0:T(8,128)(2,1)S(1)}, u32[]{:S(2)}, u32[]{:S(2)}) collective-permute-start(bf16[256,256]{1,0:T(8,128)(2,1)S(1)} %get-tuple-element.75), channel_id=1, source_target_pairs={{0,8},{1,9},{2,10},{3,11},{4,12},{5,13},{6,14},{7,15},{8,0},{9,1},... | collective-permute-start | bytes 393224 | tf_op jit(solution)/shard_map/ppermute | solution.py:29
  248.0 10.8 %collective-permute-start.48 = (bf16[256,1024]{1,0:T(8,128)(2,1)S(1)}, bf16[256,1024]{1,0:T(8,128)(2,1)S(1)}, u32[]{:S(2)}, u32[]{:S(2)}) collective-permute-start(bf16[256,1024]{1,0:T(8,128)(2,1)S(1)} %get-tuple-element.69), channel_id=1, source_target_pairs={{0,32},{1,33},{2,34},{3,35},{4,36},{5,37},{6,38},{7,39},{8,40},{9,... | collective-permute-start | bytes 1572872 | tf_op jit(solution)/shard_map/ppermute | solution.py:29
  250.9 13.4 %collective-permute-start.49 = (bf16[256,1024]{1,0:T(8,128)(2,1)S(1)}, bf16[256,1024]{1,0:T(8,128)(2,1)S(1)}, u32[]{:S(2)}, u32[]{:S(2)}) collective-permute-start(bf16[256,1024]{1,0:T(8,128)(2,1)S(1)} %get-tuple-element.70), channel_id=1, source_target_pairs={{0,48},{1,49},{2,50},{3,51},{4,52},{5,53},{6,54},{7,55},{8,56},{9,... | collective-permute-start | bytes 1572872 | tf_op jit(solution)/shard_map/ppermute | solution.py:29
  (25 other events, 371.5 us)

commit v3 on v2

--- a/solution.py
+++ b/solution.py
@@ -214,44 +214,75 @@
     cut = [jax.ShapeDtypeStruct((4, 256, 256), bf16)] * 4
     square, blocks = (1024, 1024), (4, 256, 1024)
 
-    left = left_basis.reshape(4, 256, 256)
-    left = left_blocks([pick(left, jnp.where(layer == 0, (x + j) % SIDE, j), 0) for j in range(4)])
-    grads = ring_gather(grad, "o")
-    lefts = ring_gather(jnp.stack(left), "z")
-    right = permute(right_basis, lambda layer, x, y, z: (y, x, z) if layer else (x, y, z))
-    rights = ring_gather(right, "o")
-    other = exchange([pick(grad, (x + j) % SIDE, 1) for j in range(4)], "x")
-
+    scope = jax.named_scope
+    with scope("grad_o"):
+        grads = ring_gather(grad, "o")
+    with scope("left_blocks"):
+        left = left_basis.reshape(4, 256, 256)
+        left = left_blocks([pick(left, jnp.where(layer == 0, (x + j) % SIDE, j), 0) for j in range(4)])
+    with scope("left_z"):
+        lefts = ring_gather(jnp.stack(left), "z")
+    held, right = lax.optimization_barrier((grad, right_basis, left[1]))[:2]
+    with scope("right_swap"):
+        right = permute(right, lambda layer, x, y, z: (y, x, z) if layer else (x, y, z))
+    with scope("other_x"):
+        other = exchange([pick(held, (x + j) % SIDE, 1) for j in range(4)], "x")
+
+    lefts[0] = after(lefts[0], *other)
     half = call(half_kernel, "half", at, lefts + grads, tall, [square, square])
-    half = total(ring_scatter(half, "p")).astype(bf16)
-
-    halves = ring_gather(after(half, *rights), "z")
-    rows = ring_gather(after(grad, half), "p")
+    with scope("half_p"):
+        half = ring_scatter(half, "p")
+        half[0] = after(half[0], right)
+        half = total(half).astype(bf16)
+
+    with scope("half_z"):
+        halves = ring_gather(half, "z")
+    held, right = lax.optimization_barrier((grad, right, half))[:2]
+    with scope("right_o"):
+        rights = ring_gather(right, "o")
+    with scope("rows_p"):
+        rows = ring_gather(held, "p")
 
     rotated = call(rotate_kernel, "rotate", at, halves + rights, wide, [blocks])
-    rotated[0] = after(rotated[0], *rows)
-    rotated = total(ring_scatter(rotated, "p"))
+    with scope("rotated_p"):
+        rotated = ring_scatter(rotated, "p")
+        rotated[0] = after(rotated[0], *rows)
+        rotated = total(rotated)
     first_new = first_decay * first_moment + (1.0 - first_decay) * rotated
     second_new = second_decay * second_moment + (1.0 - second_decay) * rotated * rotated
     direction = (first_new / first_bias / (jnp.sqrt(second_new / second_bias) + adam_eps)).astype(bf16)
-    others = ring_gather(after(jnp.stack(other), halves[1]), "z")
-
-    directions = ring_gather(after(direction, *others), "p")
-    left_sum = call(left_kernel, "left_sum", at, grads + [after(rows[0], direction)] + rows[1:], cut, [(2, *blocks)])
-    left_sum = total(ring_scatter(left_sum, "z")).astype(bf16)
-
+    with scope("other_z"):
+        others = ring_gather(after(jnp.stack(other), *halves), "z")
+
+    with scope("direction_p"):
+        directions = ring_gather(direction, "p")
+    left_sum = call(left_kernel, "left_sum", at, grads + rows, cut, [(2, *blocks)])
+
+    directions[0] = after(directions[0], *others, left_sum[0])
     back = call(back_kernel, "back", at, directions + rights, tall, [blocks])
-    back[0] = after(back[0], left_sum)
-    others[0] = after(others[0], directions[1])
     right_sum = call(right_kernel, "right_sum", at, others + grads + rows, wide, [(2, *blocks), (4, 1024, 256)])
-    back = total(ring_scatter(back, "z")).astype(bf16)
-    right_sum = ring_scatter(right_sum, "y")
-
-    backs = ring_gather(after(back, *right_sum), "p")
-    pieces = exchange([left_sum[s] for s in range(4)], "x")
+    with scope("back_z"):
+        back = ring_scatter(back, "z")
+    with scope("right_sum_y"):
+        right_sum = ring_scatter(right_sum, "y")
+    back[0] = after(back[0], right_sum[0])
+    back = total(back).astype(bf16)
+
+    with scope("back_p"):
+        backs = ring_gather(back, "p")
+    with scope("left_sum_z"):
+        left_sum = ring_scatter([after(part, back) for part in left_sum], "z")
+    backs[0] = after(backs[0], *right_sum)
+    update = call(update_kernel, "update", at, lefts + backs, wide, [square, square])
+    left_sum[0] = after(left_sum[0], update[0])
+    left_sum = total(left_sum).astype(bf16)
+    with scope("update_o"):
+        update = ring_scatter(update, "o")
     right_stat_new = stat_decay * right_stat + (1.0 - stat_decay) * total(right_sum)
-    update = call(update_kernel, "update", at, lefts + backs, wide, [square, square])
-    update = total(ring_scatter(update, "o"))
+    with scope("left_sum_x"):
+        pieces = exchange([left_sum[s] for s in range(4)], "x")
+    update = total(update)
+    pieces[0] = after(pieces[0], update)
     left_stat_new = call(
         left_stat_kernel, "left_stat", at, pieces + [left_stat], [jax.ShapeDtypeStruct((1024, 256), f32)]
     )[0]

time: 268 us -> 226 us (0.84)
  waiting for transfers between devices: 121 us -> 79.1 us
  local copies, waits for them, and re-layouts: 4.87 us -> 1.44 us
  starting transfers between devices: 106 us -> 109 us
    ppermute x53, waiting for transfers between devices: 121 us -> 79.1 us  [permute(): return lax.ppermute(value, ('layer', 'dp', 'mp'), pairs)]
    unnamed x40 -> x24, local copies, waits for them, and re-layouts: 3.49 us -> 0.05 us
  transfers between devices with their start and end apart: 53 -> 53, of which waited for: 24 -> 17; matrix products, arithmetic and copies ran while one was open for 2% -> 4% of each run, Pallas kernels for 10% -> 9%
where the time goes in v3:
time: 226 us; the launch traced here: 223 us
  starting transfers between devices  109 us (48%)
  waiting for transfers between devices  79.1 us (35%)
  Pallas kernels  25.5 us (11%)
  other arithmetic  6.75 us (3%)
    ppermute x53, starting transfers between devices, permute(): return lax.ppermute(value, ('layer', 'dp', 'mp'), pairs)  109 us
    ppermute x53, waiting for transfers between devices, permute(): return lax.ppermute(value, ('layer', 'dp', 'mp'), pairs)  79.1 us
    pallas_call x7, Pallas kernels, call(): pl.pallas_call(kernel, out_shape=out_shapes, in_specs=[pl.BlockSpec(memor...  25.5 us
  transfers between devices with their start and end apart: 53, of which 17 were waited for; matrix products, arithmetic and copies ran while one was open for 4% of the time, Pallas kernels for 9%

profile of v3, /device:TPU:24, one launch (start us, length us, event | category | flops | bytes accessed | tf_op | source)
XLA Modules:
  0.0 222.8 jit_solution(13450110959087544859)
XLA Ops:
  2.0 4.8 %collective-permute-start.1 = (bf16[256,256]{1,0:T(8,128)(2,1)S(1)}, bf16[256,256]{1,0:T(8,128)(2,1)S(1)}, u32[]{:S(2)}, u32[]{:S(2)}) collective-permute-start(bf16[256,256]{1,0:T(8,128)(2,1)S(1)} %get-tuple-element.101), channel_id=1, source_target_pairs={{0,12},{1,13},{2,14},{3,15},{4,0},{5,1},{6,2},{7,3},{8,4},{9,5},{1... | collective-permute-start | bytes 393224 | tf_op jit(solution)/shard_map/left_blocks/ppermute | solution.py:29
  7.5 1.9 collective-permute-start.3
  9.4 4.2 %collective-permute-start.2 = (bf16[256,256]{1,0:T(8,128)(2,1)S(1)}, bf16[256,256]{1,0:T(8,128)(2,1)S(1)}, u32[]{:S(2)}, u32[]{:S(2)}) collective-permute-start(bf16[256,256]{1,0:T(8,128)(2,1)S(1)} %get-tuple-element.100), channel_id=1, source_target_pairs={{0,8},{1,9},{2,10},{3,11},{4,12},{5,13},{6,14},{7,15},{8,0},{9,1},... | collective-permute-start | bytes 393224 | tf_op jit(solution)/shard_map/left_blocks/ppermute | solution.py:29
  13.7 1.9 collective-permute-start.6
  16.4 2.0 collective-permute-start.4
  18.4 2.6 %collective-permute-start.11 = (bf16[256,1024]{1,0:T(8,128)(2,1)S(1)}, bf16[256,1024]{1,0:T(8,128)(2,1)}, u32[]{:S(2)}, u32[]{:S(2)}) collective-permute-start(bf16[256,1024]{1,0:T(8,128)(2,1)S(1)} %copy-done), channel_id=1, source_target_pairs={{0,32},{1,33},{2,34},{3,35},{4,36},{5,37},{6,38},{7,39},{8,40},{9,... | collective-permute-start | bytes 1572872 | tf_op jit(solution)/shard_map/grad_o/ppermute | solution.py:29
  21.1 5.8 %collective-permute-start.10 = (bf16[256,1024]{1,0:T(8,128)(2,1)S(1)}, bf16[256,1024]{1,0:T(8,128)(2,1)}, u32[]{:S(2)}, u32[]{:S(2)}) collective-permute-start(bf16[256,1024]{1,0:T(8,128)(2,1)S(1)} %copy-done), channel_id=1, source_target_pairs={{0,48},{1,49},{2,50},{3,51},{4,52},{5,53},{6,54},{7,55},{8,56},{9,... | collective-permute-start | bytes 1572872 | tf_op jit(solution)/shard_map/grad_o/ppermute | solution.py:29
  26.9 2.2 collective-permute-start.9
  29.0 7.8 %collective-permute-start.8 = (bf16[4,256,256]{2,1,0:T(8,128)(2,1)S(1)}, bf16[4,256,256]{2,1,0:T(8,128)(2,1)S(1)}, u32[]{:S(2)}, u32[]{:S(2)}) collective-permute-start(bf16[4,256,256]{2,1,0:T(8,128)(2,1)S(1)} %pad_maximum_fusion.refs_0_), channel_id=1, source_target_pairs={{0,2},{1,3},{2,0},{3,1},{4,6},{5,7},{6,4},{7,5},{8,10},{9,11},{10,... | collective-permute-start | bytes 1572872 | tf_op jit(solution)/shard_map/left_z/ppermute | solution.py:29
  38.7 17.3 %collective-permute-done.9.refs_3_ = bf16[4,256,256]{2,1,0:T(8,128)(2,1)S(1)} collective-permute-done((bf16[4,256,256]{2,1,0:T(8,128)(2,1)S(1)}, bf16[4,256,256]{2,1,0:T(8,128)(2,1)S(1)}, u32[]{:S(2)}, u32[]{:S(2)}) %collective-permute-start.9) | collective-permute-done | bytes 524320 | tf_op jit(solution)/shard_map/left_z/ppermute | solution.py:29
  56.6 4.3 %half.1 = (bf16[1024,256]{1,0:T(8,128)(2,1)S(1)}, bf16[1024,256]{1,0:T(8,128)(2,1)S(1)}, bf16[1024,256]{1,0:T(8,128)(2,1)S(1)}, bf16[1024,256]{1,0:T(8,128)(2,1)S(1)}) custom-call(s32[6]{0:T(128)S(1)} %stack.57.at, bf16[4,256,256]{2,1,0:T(8,128)(2,1)S(1)} %pad_maximum_fusion.refs_0_, bf16[4,256,256]{2,1,0:T(8,128)(2,1)S(1)} %collective-permute-done.7.refs_1_, ...), custom_call_target="tpu_custom_call" | custom-call | flops 2147483648 | bytes 6291456 | tf_op jit(solution)/shard_map/half/pallas_call | solution.py:194
  60.9 1.9 collective-permute-start.15
  64.2 12.8 %collective-permute-done.14 = bf16[1024,256]{1,0:T(8,128)(2,1)S(1)} collective-permute-done((bf16[1024,256]{1,0:T(8,128)(2,1)S(1)}, bf16[1024,256]{1,0:T(8,128)(2,1)S(1)}, u32[]{:S(2)}, u32[]{:S(2)}) %collective-permute-start.14) | collective-permute-done | bytes 524320 | tf_op jit(solution)/shard_map/half_p/ppermute | solution.py:29
  78.5 3.6 %collective-permute-start.21 = (bf16[256,1024]{1,0:T(8,128)(2,1)S(1)}, bf16[256,1024]{1,0:T(8,128)(2,1)S(1)}, u32[]{:S(2)}, u32[]{:S(2)}) collective-permute-start(bf16[256,1024]{1,0:T(8,128)(2,1)S(1)} %collective-permute-done.13.refs_4_), channel_id=1, source_target_pairs={{0,32},{1,33},{2,34},{3,35},{4,36},{5,37},{6,38},{7,39},{8,40},{9,... | collective-permute-start | bytes 1572872 | tf_op jit(solution)/shard_map/right_o/ppermute | solution.py:29
  82.6 3.4 %collective-permute-start.18 = (bf16[1024,256]{1,0:T(8,128)(2,1)S(1)}, bf16[1024,256]{1,0:T(8,128)(2,1)S(1)}, u32[]{:S(2)}, u32[]{:S(2)}) collective-permute-start(bf16[1024,256]{1,0:T(8,128)(2,1)S(1)} %add_convert_fusion.2.refs_0_), channel_id=1, source_target_pairs={{0,2},{1,3},{2,0},{3,1},{4,6},{5,7},{6,4},{7,5},{8,10},{9,11},{10,... | collective-permute-start | bytes 1572872 | tf_op jit(solution)/shard_map/half_z/ppermute | solution.py:29
  87.3 2.6 %collective-permute-start.17 = (bf16[1024,256]{1,0:T(8,128)(2,1)S(1)}, bf16[1024,256]{1,0:T(8,128)(2,1)S(1)}, u32[]{:S(2)}, u32[]{:S(2)}) collective-permute-start(bf16[1024,256]{1,0:T(8,128)(2,1)S(1)} %add_convert_fusion.2.refs_0_), channel_id=1, source_target_pairs={{0,3},{1,0},{2,1},{3,2},{4,7},{5,4},{6,5},{7,6},{8,11},{9,8},{10,9... | collective-permute-start | bytes 1572872 | tf_op jit(solution)/shard_map/half_z/ppermute | solution.py:29
  90.5 4.4 %collective-permute-done.20.refs_5_ = bf16[256,1024]{1,0:T(8,128)(2,1)S(1)} collective-permute-done((bf16[256,1024]{1,0:T(8,128)(2,1)S(1)}, bf16[256,1024]{1,0:T(8,128)(2,1)S(1)}, u32[]{:S(2)}, u32[]{:S(2)}) %collective-permute-start.20) | collective-permute-done | bytes 524320 | tf_op jit(solution)/shard_map/right_o/ppermute | solution.py:29
  94.9 1.8 collective-permute-start.24
  96.7 2.2 collective-permute-start.23
  98.8 8.5 %collective-permute-done.18.refs_2_ = bf16[1024,256]{1,0:T(8,128)(2,1)S(1)} collective-permute-done((bf16[1024,256]{1,0:T(8,128)(2,1)S(1)}, bf16[1024,256]{1,0:T(8,128)(2,1)S(1)}, u32[]{:S(2)}, u32[]{:S(2)}) %collective-permute-start.18) | collective-permute-done | bytes 524320 | tf_op jit(solution)/shard_map/half_z/ppermute | solution.py:29
  107.3 3.6 %rotate.1 = (bf16[256,1024]{1,0:T(8,128)(2,1)S(1)}, bf16[256,1024]{1,0:T(8,128)(2,1)S(1)}, bf16[256,1024]{1,0:T(8,128)(2,1)S(1)}, bf16[256,1024]{1,0:T(8,128)(2,1)S(1)}) custom-call(s32[6]{0:T(128)S(1)} %stack.57.at, bf16[1024,256]{1,0:T(8,128)(2,1)S(1)} %add_convert_fusion.2.refs_0_, bf16[1024,256]{1,0:T(8,128)(2,1)S(1)} %collective-permute-done.17.refs_1_, ...), custom_call_target="tpu_custom_call" | custom-call | flops 2147483648 | bytes 6291456 | tf_op jit(solution)/shard_map/rotate/pallas_call | solution.py:194
  113.1 2.5 %collective-permute-start.28 = (bf16[256,1024]{1,0:T(8,128)(2,1)S(1)}, bf16[256,1024]{1,0:T(8,128)(2,1)S(1)}, u32[]{:S(2)}, u32[]{:S(2)}) collective-permute-start(bf16[256,1024]{1,0:T(8,128)(2,1)S(1)} %get-tuple-element.60), channel_id=1, source_target_pairs={{0,12},{1,13},{2,14},{3,15},{4,0},{5,1},{6,2},{7,3},{8,4},{9,5},{1... | collective-permute-start | bytes 1572872 | tf_op jit(solution)/shard_map/rotated_p/ppermute | solution.py:29
  116.6 2.6 %collective-permute-start.31 = (bf16[4,256,256]{2,1,0:T(8,128)(2,1)S(1)}, bf16[4,256,256]{2,1,0:T(8,128)(2,1)S(1)}, u32[]{:S(2)}, u32[]{:S(2)}) collective-permute-start(bf16[4,256,256]{2,1,0:T(8,128)(2,1)S(1)} %pad_maximum_fusion.1.refs_0_), channel_id=1, source_target_pairs={{0,1},{1,2},{2,3},{3,0},{4,5},{5,6},{6,7},{7,4},{8,9},{9,10},{10,1... | collective-permute-start | bytes 1572872 | tf_op jit(solution)/shard_map/other_z/ppermute | solution.py:29
  120.2 6.8 %collective-permute-done.26 = bf16[256,1024]{1,0:T(8,128)(2,1)S(1)} collective-permute-done((bf16[256,1024]{1,0:T(8,128)(2,1)S(1)}, bf16[256,1024]{1,0:T(8,128)(2,1)S(1)}, u32[]{:S(2)}, u32[]{:S(2)}) %collective-permute-start.26) | collective-permute-done | bytes 524320 | tf_op jit(solution)/shard_map/rotated_p/ppermute | solution.py:29
  127.0 2.1 collective-permute-start.29
  129.1 2.2 divide_convert_fusion
  131.5 2.7 %collective-permute-start.33 = (bf16[256,1024]{1,0:T(8,128)(2,1)S(1)}, bf16[256,1024]{1,0:T(8,128)(2,1)S(1)}, u32[]{:S(2)}, u32[]{:S(2)}) collective-permute-start(bf16[256,1024]{1,0:T(8,128)(2,1)S(1)} %get-tuple-element.63.refs_0_), channel_id=1, source_target_pairs={{0,8},{1,9},{2,10},{3,11},{4,12},{5,13},{6,14},{7,15},{8,0},{9,1},... | collective-permute-start | bytes 1572872 | tf_op jit(solution)/shard_map/direction_p/ppermute | solution.py:29
  134.8 3.9 %left_sum.1 = (bf16[4,256,256]{2,1,0:T(8,128)(2,1)S(1)}, bf16[4,256,256]{2,1,0:T(8,128)(2,1)S(1)}, bf16[4,256,256]{2,1,0:T(8,128)(2,1)S(1)}, bf16[4,256,256]{2,1,0:T(8,128)(2,1)S(1)}) custom-call(s32[6]{0:T(128)S(1)} %stack.57.at, bf16[256,1024]{1,0:T(8,128)(2,1)S(1)} %copy-done, bf16[256,1024]{1,0:T(8,128)(2,1)} %collective-permute-done.10.refs_5_.refs_1_, ...), custom_call_target="tpu_custom_call" | custom-call | flops 2147483648 | bytes 6291456 | tf_op jit(solution)/shard_map/left_sum/pallas_call | solution.py:194
  138.7 2.1 collective-permute-done.30.refs_2_
  140.7 6.6 %collective-permute-done.34.refs_3_ = bf16[256,1024]{1,0:T(8,128)(2,1)S(1)} collective-permute-done((bf16[256,1024]{1,0:T(8,128)(2,1)S(1)}, bf16[256,1024]{1,0:T(8,128)(2,1)S(1)}, u32[]{:S(2)}, u32[]{:S(2)}) %collective-permute-start.34) | collective-permute-done | bytes 524320 | tf_op jit(solution)/shard_map/direction_p/ppermute | solution.py:29
  148.2 3.6 %back.1 = (bf16[1024,256]{1,0:T(8,128)(2,1)S(1)}, bf16[1024,256]{1,0:T(8,128)(2,1)S(1)}, bf16[1024,256]{1,0:T(8,128)(2,1)S(1)}, bf16[1024,256]{1,0:T(8,128)(2,1)S(1)}) custom-call(s32[6]{0:T(128)S(1)} %stack.57.at, bf16[256,1024]{1,0:T(8,128)(2,1)S(1)} %get-tuple-element.63.refs_0_, bf16[256,1024]{1,0:T(8,128)(2,1)S(1)} %collective-permute-done.32.refs_1_, ...), custom_call_target="tpu_custom_call" | custom-call | flops 2147483648 | bytes 6291456 | tf_op jit(solution)/shard_map/back/pallas_call | solution.py:194
  152.5 1.9 collective-permute-start.36
  154.4 1.9 collective-permute-start.37
  156.3 4.6 %right_sum.1 = (bf16[256,1024]{1,0:T(8,128)(2,1)S(1)}, bf16[256,1024]{1,0:T(8,128)(2,1)S(1)}, bf16[256,1024]{1,0:T(8,128)(2,1)S(1)}, bf16[256,1024]{1,0:T(8,128)(2,1)S(1)}) custom-call(s32[6]{0:T(128)S(1)} %stack.57.at, bf16[4,256,256]{2,1,0:T(8,128)(2,1)S(1)} %pad_maximum_fusion.1.refs_0_, bf16[4,256,256]{2,1,0:T(8,128)(2,1)S(1)} %collective-permute-done.29.refs_1_, ...), custom_call_target="tpu_custom_call" | custom-call | flops 2147483648 | bytes 8388608 | tf_op jit(solution)/shard_map/right_sum/pallas_call | solution.py:194
  161.8 2.3 %collective-permute-start.39 = (bf16[256,1024]{1,0:T(8,128)(2,1)S(1)}, bf16[256,1024]{1,0:T(8,128)(2,1)S(1)}, u32[]{:S(2)}, u32[]{:S(2)}) collective-permute-start(bf16[256,1024]{1,0:T(8,128)(2,1)S(1)} %get-tuple-element.71), channel_id=1, source_target_pairs={{0,32},{1,33},{2,34},{3,35},{4,36},{5,37},{6,38},{7,39},{8,40},{9,... | collective-permute-start | bytes 1572872 | tf_op jit(solution)/shard_map/right_sum_y/ppermute | solution.py:29
  164.9 10.8 %collective-permute-start.40 = (bf16[256,1024]{1,0:T(8,128)(2,1)S(1)}, bf16[256,1024]{1,0:T(8,128)(2,1)S(1)}, u32[]{:S(2)}, u32[]{:S(2)}) collective-permute-start(bf16[256,1024]{1,0:T(8,128)(2,1)S(1)} %get-tuple-element.72), channel_id=1, source_target_pairs={{0,48},{1,49},{2,50},{3,51},{4,52},{5,53},{6,54},{7,55},{8,56},{9,... | collective-permute-start | bytes 1572872 | tf_op jit(solution)/shard_map/right_sum_y/ppermute | solution.py:29
  177.5 2.7 %collective-permute-start.41 = (bf16[1024,256]{1,0:T(8,128)(2,1)S(1)}, bf16[1024,256]{1,0:T(8,128)(2,1)S(1)}, u32[]{:S(2)}, u32[]{:S(2)}) collective-permute-start(bf16[1024,256]{1,0:T(8,128)(2,1)S(1)} %add_convert_fusion.1.refs_4_), channel_id=1, source_target_pairs={{0,12},{1,13},{2,14},{3,15},{4,0},{5,1},{6,2},{7,3},{8,4},{9,5},{1... | collective-permute-start | bytes 1572872 | tf_op jit(solution)/shard_map/back_p/ppermute | solution.py:29
  180.2 2.0 collective-permute-start.47
  182.2 8.6 %collective-permute-done.40 = bf16[256,1024]{1,0:T(8,128)(2,1)S(1)} collective-permute-done((bf16[256,1024]{1,0:T(8,128)(2,1)S(1)}, bf16[256,1024]{1,0:T(8,128)(2,1)S(1)}, u32[]{:S(2)}, u32[]{:S(2)}) %collective-permute-start.40) | collective-permute-done | bytes 524320 | tf_op jit(solution)/shard_map/right_sum_y/ppermute | solution.py:29
  190.8 2.1 collective-permute-start.48
  192.9 2.0 collective-permute-start.49
  196.3 3.9 %update.1 = (bf16[256,1024]{1,0:T(8,128)(2,1)S(1)}, bf16[256,1024]{1,0:T(8,128)(2,1)S(1)}, bf16[256,1024]{1,0:T(8,128)(2,1)S(1)}, bf16[256,1024]{1,0:T(8,128)(2,1)S(1)}) custom-call(s32[6]{0:T(128)S(1)} %stack.57.at, bf16[4,256,256]{2,1,0:T(8,128)(2,1)S(1)} %pad_maximum_fusion.refs_0_, bf16[4,256,256]{2,1,0:T(8,128)(2,1)S(1)} %collective-permute-done.7.refs_1_, ...), custom_call_target="tpu_custom_call" | custom-call | flops 2147483648 | bytes 6291456 | tf_op jit(solution)/shard_map/update/pallas_call | solution.py:194
  200.3 1.8 collective-permute-start.45
  202.1 5.0 %collective-permute-start.46 = (bf16[256,1024]{1,0:T(8,128)(2,1)S(1)}, bf16[256,1024]{1,0:T(8,128)(2,1)S(1)}, u32[]{:S(2)}, u32[]{:S(2)}) collective-permute-start(bf16[256,1024]{1,0:T(8,128)(2,1)S(1)} %get-tuple-element.77), channel_id=1, source_target_pairs={{0,48},{1,49},{2,50},{3,51},{4,52},{5,53},{6,54},{7,55},{8,56},{9,... | collective-permute-start | bytes 1572872 | tf_op jit(solution)/shard_map/update_o/ppermute | solution.py:29
  207.1 3.8 %collective-permute-done.49 = bf16[4,256,256]{2,1,0:T(8,128)(2,1)S(1)} collective-permute-done((bf16[4,256,256]{2,1,0:T(8,128)(2,1)S(1)}, bf16[4,256,256]{2,1,0:T(8,128)(2,1)S(1)}, u32[]{:S(2)}, u32[]{:S(2)}) %collective-permute-start.49) | collective-permute-done | bytes 524320 | tf_op jit(solution)/shard_map/left_sum_z/ppermute | solution.py:29
  211.3 2.3 %collective-permute-start.51 = (bf16[256,256]{1,0:T(8,128)(2,1)S(1)}, bf16[256,256]{1,0:T(8,128)(2,1)S(1)}, u32[]{:S(2)}, u32[]{:S(2)}) collective-permute-start(bf16[256,256]{1,0:T(8,128)(2,1)S(1)} %get-tuple-element.91), channel_id=1, source_target_pairs={{0,8},{1,9},{2,10},{3,11},{4,12},{5,13},{6,14},{7,15},{8,0},{9,1},... | collective-permute-start | bytes 393224 | tf_op jit(solution)/shard_map/left_sum_x/ppermute | solution.py:29
  213.6 2.5 %collective-permute-start.50 = (bf16[256,256]{1,0:T(8,128)(2,1)S(1)}, bf16[256,256]{1,0:T(8,128)(2,1)S(1)}, u32[]{:S(2)}, u32[]{:S(2)}) collective-permute-start(bf16[256,256]{1,0:T(8,128)(2,1)S(1)} %get-tuple-element.92), channel_id=1, source_target_pairs={{0,12},{1,13},{2,14},{3,15},{4,0},{5,1},{6,2},{7,3},{8,4},{9,5},{1... | collective-permute-start | bytes 393224 | tf_op jit(solution)/shard_map/left_sum_x/ppermute | solution.py:29
  218.0 2.3 %collective-permute-done.52.refs_3_ = bf16[256,256]{1,0:T(8,128)(2,1)S(1)} collective-permute-done((bf16[256,256]{1,0:T(8,128)(2,1)S(1)}, bf16[256,256]{1,0:T(8,128)(2,1)S(1)}, u32[]{:S(2)}, u32[]{:S(2)}) %collective-permute-start.52) | collective-permute-done | bytes 131104 | tf_op jit(solution)/shard_map/left_sum_x/ppermute | solution.py:29
  (101 shorter events, 27.0 us)
Async XLA Ops:
  0.6 36.2 %collective-permute-start.12 = (bf16[256,1024]{1,0:T(8,128)(2,1)}, bf16[256,1024]{1,0:T(8,128)(2,1)S(1)}, u32[]{:S(2)}, u32[]{:S(2)}) collective-permute-start(bf16[256,1024]{1,0:T(8,128)(2,1)} %refs_8_), channel_id=1, source_target_pairs={{0,16},{1,17},{2,18},{3,19},{4,20},{5,21},{6,22},{7,23},{8,24},{9,... | collective-permute-start | bytes 1572872 | tf_op jit(solution)/shard_map/grad_o/ppermute | solution.py:29
  2.0 11.6 %collective-permute-start.1 = (bf16[256,256]{1,0:T(8,128)(2,1)S(1)}, bf16[256,256]{1,0:T(8,128)(2,1)S(1)}, u32[]{:S(2)}, u32[]{:S(2)}) collective-permute-start(bf16[256,256]{1,0:T(8,128)(2,1)S(1)} %get-tuple-element.101), channel_id=1, source_target_pairs={{0,12},{1,13},{2,14},{3,15},{4,0},{5,1},{6,2},{7,3},{8,4},{9,5},{1... | collective-permute-start | bytes 393224 | tf_op jit(solution)/shard_map/left_blocks/ppermute | solution.py:29
  15.6 11.3 %collective-permute-start.5 = (bf16[256,256]{1,0:T(8,128)(2,1)S(1)}, bf16[256,256]{1,0:T(8,128)(2,1)S(1)}, u32[]{:S(2)}, u32[]{:S(2)}) collective-permute-start(bf16[256,256]{1,0:T(8,128)(2,1)S(1)} %get-tuple-element.95), channel_id=1, source_target_pairs={{0,8},{1,9},{2,10},{3,11},{4,12},{5,13},{6,14},{7,15},{8,0},{9,1},... | collective-permute-start | bytes 393224 | tf_op jit(solution)/shard_map/other_x/ppermute | solution.py:29
  16.4 12.6 %collective-permute-start.4 = (bf16[256,256]{1,0:T(8,128)(2,1)S(1)}, bf16[256,256]{1,0:T(8,128)(2,1)}, u32[]{:S(2)}, u32[]{:S(2)}) collective-permute-start(bf16[256,256]{1,0:T(8,128)(2,1)S(1)} %get-tuple-element.96), channel_id=1, source_target_pairs={{0,12},{1,13},{2,14},{3,15},{4,0},{5,1},{6,2},{7,3},{8,4},{9,5},{1... | collective-permute-start | bytes 393224 | tf_op jit(solution)/shard_map/other_x/ppermute | solution.py:29
  18.4 18.6 %collective-permute-start.11 = (bf16[256,1024]{1,0:T(8,128)(2,1)S(1)}, bf16[256,1024]{1,0:T(8,128)(2,1)}, u32[]{:S(2)}, u32[]{:S(2)}) collective-permute-start(bf16[256,1024]{1,0:T(8,128)(2,1)S(1)} %copy-done), channel_id=1, source_target_pairs={{0,32},{1,33},{2,34},{3,35},{4,36},{5,37},{6,38},{7,39},{8,40},{9,... | collective-permute-start | bytes 1572872 | tf_op jit(solution)/shard_map/grad_o/ppermute | solution.py:29
  21.1 17.6 %collective-permute-start.10 = (bf16[256,1024]{1,0:T(8,128)(2,1)S(1)}, bf16[256,1024]{1,0:T(8,128)(2,1)}, u32[]{:S(2)}, u32[]{:S(2)}) collective-permute-start(bf16[256,1024]{1,0:T(8,128)(2,1)S(1)} %copy-done), channel_id=1, source_target_pairs={{0,48},{1,49},{2,50},{3,51},{4,52},{5,53},{6,54},{7,55},{8,56},{9,... | collective-permute-start | bytes 1572872 | tf_op jit(solution)/shard_map/grad_o/ppermute | solution.py:29
  26.9 29.1 %collective-permute-start.9 = (bf16[4,256,256]{2,1,0:T(8,128)(2,1)S(1)}, bf16[4,256,256]{2,1,0:T(8,128)(2,1)S(1)}, u32[]{:S(2)}, u32[]{:S(2)}) collective-permute-start(bf16[4,256,256]{2,1,0:T(8,128)(2,1)S(1)} %pad_maximum_fusion.refs_0_), channel_id=1, source_target_pairs={{0,1},{1,2},{2,3},{3,0},{4,5},{5,6},{6,7},{7,4},{8,9},{9,10},{10,1... | collective-permute-start | bytes 1572872 | tf_op jit(solution)/shard_map/left_z/ppermute | solution.py:29
  29.0 26.9 %collective-permute-start.8 = (bf16[4,256,256]{2,1,0:T(8,128)(2,1)S(1)}, bf16[4,256,256]{2,1,0:T(8,128)(2,1)S(1)}, u32[]{:S(2)}, u32[]{:S(2)}) collective-permute-start(bf16[4,256,256]{2,1,0:T(8,128)(2,1)S(1)} %pad_maximum_fusion.refs_0_), channel_id=1, source_target_pairs={{0,2},{1,3},{2,0},{3,1},{4,6},{5,7},{6,4},{7,5},{8,10},{9,11},{10,... | collective-permute-start | bytes 1572872 | tf_op jit(solution)/shard_map/left_z/ppermute | solution.py:29
  36.8 19.7 %collective-permute-start.7 = (bf16[4,256,256]{2,1,0:T(8,128)(2,1)S(1)}, bf16[4,256,256]{2,1,0:T(8,128)(2,1)S(1)}, u32[]{:S(2)}, u32[]{:S(2)}) collective-permute-start(bf16[4,256,256]{2,1,0:T(8,128)(2,1)S(1)} %pad_maximum_fusion.refs_0_), channel_id=1, source_target_pairs={{0,3},{1,0},{2,1},{3,2},{4,7},{5,4},{6,5},{7,6},{8,11},{9,8},{10,9... | collective-permute-start | bytes 1572872 | tf_op jit(solution)/shard_map/left_z/ppermute | solution.py:29
  37.0 27.2 %collective-permute-start.13 = (bf16[256,1024]{1,0:T(8,128)(2,1)}, bf16[256,1024]{1,0:T(8,128)(2,1)S(1)}, u32[]{:S(2)}, u32[]{:S(2)}) collective-permute-start(bf16[256,1024]{1,0:T(8,128)(2,1)} %param.9), channel_id=1, source_target_pairs={{0,0},{1,1},{2,2},{3,3},{4,4},{5,5},{6,6},{7,7},{8,8},{9,9},{10,10... | collective-permute-start | bytes 1572872 | tf_op jit(solution)/shard_map/right_swap/ppermute | solution.py:29
  60.9 16.1 %collective-permute-start.14 = (bf16[1024,256]{1,0:T(8,128)(2,1)S(1)}, bf16[1024,256]{1,0:T(8,128)(2,1)S(1)}, u32[]{:S(2)}, u32[]{:S(2)}) collective-permute-start(bf16[1024,256]{1,0:T(8,128)(2,1)S(1)} %get-tuple-element.51), channel_id=1, source_target_pairs={{0,4},{1,5},{2,6},{3,7},{4,8},{5,9},{6,10},{7,11},{8,12},{9,13},{1... | collective-permute-start | bytes 1572872 | tf_op jit(solution)/shard_map/half_p/ppermute | solution.py:29
  60.9 16.0 %collective-permute-start.15 = (bf16[1024,256]{1,0:T(8,128)(2,1)S(1)}, bf16[1024,256]{1,0:T(8,128)(2,1)S(1)}, u32[]{:S(2)}, u32[]{:S(2)}) collective-permute-start(bf16[1024,256]{1,0:T(8,128)(2,1)S(1)} %get-tuple-element.52), channel_id=1, source_target_pairs={{0,8},{1,9},{2,10},{3,11},{4,12},{5,13},{6,14},{7,15},{8,0},{9,1},... | collective-permute-start | bytes 1572872 | tf_op jit(solution)/shard_map/half_p/ppermute | solution.py:29
  62.9 15.0 %collective-permute-start.16 = (bf16[1024,256]{1,0:T(8,128)(2,1)S(1)}, bf16[1024,256]{1,0:T(8,128)(2,1)S(1)}, u32[]{:S(2)}, u32[]{:S(2)}) collective-permute-start(bf16[1024,256]{1,0:T(8,128)(2,1)S(1)} %get-tuple-element.53), channel_id=1, source_target_pairs={{0,12},{1,13},{2,14},{3,15},{4,0},{5,1},{6,2},{7,3},{8,4},{9,5},{1... | collective-permute-start | bytes 1572872 | tf_op jit(solution)/shard_map/half_p/ppermute | solution.py:29
  78.1 9.2 %collective-permute-start.22 = (bf16[256,1024]{1,0:T(8,128)(2,1)S(1)}, bf16[256,1024]{1,0:T(8,128)(2,1)S(1)}, u32[]{:S(2)}, u32[]{:S(2)}) collective-permute-start(bf16[256,1024]{1,0:T(8,128)(2,1)S(1)} %collective-permute-done.13.refs_4_), channel_id=1, source_target_pairs={{0,16},{1,17},{2,18},{3,19},{4,20},{5,21},{6,22},{7,23},{8,24},{9,... | collective-permute-start | bytes 1572872 | tf_op jit(solution)/shard_map/right_o/ppermute | solution.py:29
  78.5 11.4 %collective-permute-start.21 = (bf16[256,1024]{1,0:T(8,128)(2,1)S(1)}, bf16[256,1024]{1,0:T(8,128)(2,1)S(1)}, u32[]{:S(2)}, u32[]{:S(2)}) collective-permute-start(bf16[256,1024]{1,0:T(8,128)(2,1)S(1)} %collective-permute-done.13.refs_4_), channel_id=1, source_target_pairs={{0,32},{1,33},{2,34},{3,35},{4,36},{5,37},{6,38},{7,39},{8,40},{9,... | collective-permute-start | bytes 1572872 | tf_op jit(solution)/shard_map/right_o/ppermute | solution.py:29
  82.1 12.8 %collective-permute-start.20 = (bf16[256,1024]{1,0:T(8,128)(2,1)S(1)}, bf16[256,1024]{1,0:T(8,128)(2,1)S(1)}, u32[]{:S(2)}, u32[]{:S(2)}) collective-permute-start(bf16[256,1024]{1,0:T(8,128)(2,1)S(1)} %collective-permute-done.13.refs_4_), channel_id=1, source_target_pairs={{0,48},{1,49},{2,50},{3,51},{4,52},{5,53},{6,54},{7,55},{8,56},{9,... | collective-permute-start | bytes 1572872 | tf_op jit(solution)/shard_map/right_o/ppermute | solution.py:29
  82.1 14.6 %collective-permute-start.19 = (bf16[1024,256]{1,0:T(8,128)(2,1)S(1)}, bf16[1024,256]{1,0:T(8,128)(2,1)S(1)}, u32[]{:S(2)}, u32[]{:S(2)}) collective-permute-start(bf16[1024,256]{1,0:T(8,128)(2,1)S(1)} %add_convert_fusion.2.refs_0_), channel_id=1, source_target_pairs={{0,1},{1,2},{2,3},{3,0},{4,5},{5,6},{6,7},{7,4},{8,9},{9,10},{10,1... | collective-permute-start | bytes 1572872 | tf_op jit(solution)/shard_map/half_z/ppermute | solution.py:29
  82.6 24.7 %collective-permute-start.18 = (bf16[1024,256]{1,0:T(8,128)(2,1)S(1)}, bf16[1024,256]{1,0:T(8,128)(2,1)S(1)}, u32[]{:S(2)}, u32[]{:S(2)}) collective-permute-start(bf16[1024,256]{1,0:T(8,128)(2,1)S(1)} %add_convert_fusion.2.refs_0_), channel_id=1, source_target_pairs={{0,2},{1,3},{2,0},{3,1},{4,6},{5,7},{6,4},{7,5},{8,10},{9,11},{10,... | collective-permute-start | bytes 1572872 | tf_op jit(solution)/shard_map/half_z/ppermute | solution.py:29
  87.3 20.0 %collective-permute-start.17 = (bf16[1024,256]{1,0:T(8,128)(2,1)S(1)}, bf16[1024,256]{1,0:T(8,128)(2,1)S(1)}, u32[]{:S(2)}, u32[]{:S(2)}) collective-permute-start(bf16[1024,256]{1,0:T(8,128)(2,1)S(1)} %add_convert_fusion.2.refs_0_), channel_id=1, source_target_pairs={{0,3},{1,0},{2,1},{3,2},{4,7},{5,4},{6,5},{7,6},{8,11},{9,8},{10,9... | collective-permute-start | bytes 1572872 | tf_op jit(solution)/shard_map/half_z/ppermute | solution.py:29
  90.0 23.1 %collective-permute-start.25 = (bf16[256,1024]{1,0:T(8,128)(2,1)S(1)}, bf16[256,1024]{1,0:T(8,128)(2,1)S(1)}, u32[]{:S(2)}, u32[]{:S(2)}) collective-permute-start(bf16[256,1024]{1,0:T(8,128)(2,1)S(1)} %copy-done), channel_id=1, source_target_pairs={{0,4},{1,5},{2,6},{3,7},{4,8},{5,9},{6,10},{7,11},{8,12},{9,13},{1... | collective-permute-start | bytes 1572872 | tf_op jit(solution)/shard_map/rows_p/ppermute | solution.py:29
  94.9 21.7 %collective-permute-start.24 = (bf16[256,1024]{1,0:T(8,128)(2,1)S(1)}, bf16[256,1024]{1,0:T(8,128)(2,1)S(1)}, u32[]{:S(2)}, u32[]{:S(2)}) collective-permute-start(bf16[256,1024]{1,0:T(8,128)(2,1)S(1)} %copy-done), channel_id=1, source_target_pairs={{0,8},{1,9},{2,10},{3,11},{4,12},{5,13},{6,14},{7,15},{8,0},{9,1},... | collective-permute-start | bytes 1572872 | tf_op jit(solution)/shard_map/rows_p/ppermute | solution.py:29
  96.7 22.6 %collective-permute-start.23 = (bf16[256,1024]{1,0:T(8,128)(2,1)S(1)}, bf16[256,1024]{1,0:T(8,128)(2,1)S(1)}, u32[]{:S(2)}, u32[]{:S(2)}) collective-permute-start(bf16[256,1024]{1,0:T(8,128)(2,1)S(1)} %copy-done), channel_id=1, source_target_pairs={{0,12},{1,13},{2,14},{3,15},{4,0},{5,1},{6,2},{7,3},{8,4},{9,5},{1... | collective-permute-start | bytes 1572872 | tf_op jit(solution)/shard_map/rows_p/ppermute | solution.py:29
  110.9 16.1 %collective-permute-start.26 = (bf16[256,1024]{1,0:T(8,128)(2,1)S(1)}, bf16[256,1024]{1,0:T(8,128)(2,1)S(1)}, u32[]{:S(2)}, u32[]{:S(2)}) collective-permute-start(bf16[256,1024]{1,0:T(8,128)(2,1)S(1)} %get-tuple-element.58), channel_id=1, source_target_pairs={{0,4},{1,5},{2,6},{3,7},{4,8},{5,9},{6,10},{7,11},{8,12},{9,13},{1... | collective-permute-start | bytes 1572872 | tf_op jit(solution)/shard_map/rotated_p/ppermute | solution.py:29
  112.5 16.6 %collective-permute-start.27 = (bf16[256,1024]{1,0:T(8,128)(2,1)S(1)}, bf16[256,1024]{1,0:T(8,128)(2,1)S(1)}, u32[]{:S(2)}, u32[]{:S(2)}) collective-permute-start(bf16[256,1024]{1,0:T(8,128)(2,1)S(1)} %get-tuple-element.59), channel_id=1, source_target_pairs={{0,8},{1,9},{2,10},{3,11},{4,12},{5,13},{6,14},{7,15},{8,0},{9,1},... | collective-permute-start | bytes 1572872 | tf_op jit(solution)/shard_map/rotated_p/ppermute | solution.py:29
  113.1 16.0 %collective-permute-start.28 = (bf16[256,1024]{1,0:T(8,128)(2,1)S(1)}, bf16[256,1024]{1,0:T(8,128)(2,1)S(1)}, u32[]{:S(2)}, u32[]{:S(2)}) collective-permute-start(bf16[256,1024]{1,0:T(8,128)(2,1)S(1)} %get-tuple-element.60), channel_id=1, source_target_pairs={{0,12},{1,13},{2,14},{3,15},{4,0},{5,1},{6,2},{7,3},{8,4},{9,5},{1... | collective-permute-start | bytes 1572872 | tf_op jit(solution)/shard_map/rotated_p/ppermute | solution.py:29
  116.6 17.6 %collective-permute-start.31 = (bf16[4,256,256]{2,1,0:T(8,128)(2,1)S(1)}, bf16[4,256,256]{2,1,0:T(8,128)(2,1)S(1)}, u32[]{:S(2)}, u32[]{:S(2)}) collective-permute-start(bf16[4,256,256]{2,1,0:T(8,128)(2,1)S(1)} %pad_maximum_fusion.1.refs_0_), channel_id=1, source_target_pairs={{0,1},{1,2},{2,3},{3,0},{4,5},{5,6},{6,7},{7,4},{8,9},{9,10},{10,1... | collective-permute-start | bytes 1572872 | tf_op jit(solution)/shard_map/other_z/ppermute | solution.py:29
  119.2 21.5 %collective-permute-start.30 = (bf16[4,256,256]{2,1,0:T(8,128)(2,1)S(1)}, bf16[4,256,256]{2,1,0:T(8,128)(2,1)S(1)}, u32[]{:S(2)}, u32[]{:S(2)}) collective-permute-start(bf16[4,256,256]{2,1,0:T(8,128)(2,1)S(1)} %pad_maximum_fusion.1.refs_0_), channel_id=1, source_target_pairs={{0,2},{1,3},{2,0},{3,1},{4,6},{5,7},{6,4},{7,5},{8,10},{9,11},{10,... | collective-permute-start | bytes 1572872 | tf_op jit(solution)/shard_map/other_z/ppermute | solution.py:29
  127.0 13.7 %collective-permute-start.29 = (bf16[4,256,256]{2,1,0:T(8,128)(2,1)S(1)}, bf16[4,256,256]{2,1,0:T(8,128)(2,1)S(1)}, u32[]{:S(2)}, u32[]{:S(2)}) collective-permute-start(bf16[4,256,256]{2,1,0:T(8,128)(2,1)S(1)} %pad_maximum_fusion.1.refs_0_), channel_id=1, source_target_pairs={{0,3},{1,0},{2,1},{3,2},{4,7},{5,4},{6,5},{7,6},{8,11},{9,8},{10,9... | collective-permute-start | bytes 1572872 | tf_op jit(solution)/shard_map/other_z/ppermute | solution.py:29
  131.3 16.0 %collective-permute-start.34 = (bf16[256,1024]{1,0:T(8,128)(2,1)S(1)}, bf16[256,1024]{1,0:T(8,128)(2,1)S(1)}, u32[]{:S(2)}, u32[]{:S(2)}) collective-permute-start(bf16[256,1024]{1,0:T(8,128)(2,1)S(1)} %get-tuple-element.63.refs_0_), channel_id=1, source_target_pairs={{0,4},{1,5},{2,6},{3,7},{4,8},{5,9},{6,10},{7,11},{8,12},{9,13},{1... | collective-permute-start | bytes 1572872 | tf_op jit(solution)/shard_map/direction_p/ppermute | solution.py:29
  131.5 15.8 %collective-permute-start.33 = (bf16[256,1024]{1,0:T(8,128)(2,1)S(1)}, bf16[256,1024]{1,0:T(8,128)(2,1)S(1)}, u32[]{:S(2)}, u32[]{:S(2)}) collective-permute-start(bf16[256,1024]{1,0:T(8,128)(2,1)S(1)} %get-tuple-element.63.refs_0_), channel_id=1, source_target_pairs={{0,8},{1,9},{2,10},{3,11},{4,12},{5,13},{6,14},{7,15},{8,0},{9,1},... | collective-permute-start | bytes 1572872 | tf_op jit(solution)/shard_map/direction_p/ppermute | solution.py:29
  134.3 14.0 %collective-permute-start.32 = (bf16[256,1024]{1,0:T(8,128)(2,1)S(1)}, bf16[256,1024]{1,0:T(8,128)(2,1)S(1)}, u32[]{:S(2)}, u32[]{:S(2)}) collective-permute-start(bf16[256,1024]{1,0:T(8,128)(2,1)S(1)} %get-tuple-element.63.refs_0_), channel_id=1, source_target_pairs={{0,12},{1,13},{2,14},{3,15},{4,0},{5,1},{6,2},{7,3},{8,4},{9,5},{1... | collective-permute-start | bytes 1572872 | tf_op jit(solution)/shard_map/direction_p/ppermute | solution.py:29
  151.8 13.1 %collective-permute-start.35 = (bf16[1024,256]{1,0:T(8,128)(2,1)S(1)}, bf16[1024,256]{1,0:T(8,128)(2,1)S(1)}, u32[]{:S(2)}, u32[]{:S(2)}) collective-permute-start(bf16[1024,256]{1,0:T(8,128)(2,1)S(1)} %get-tuple-element.67), channel_id=1, source_target_pairs={{0,1},{1,2},{2,3},{3,0},{4,5},{5,6},{6,7},{7,4},{8,9},{9,10},{10,1... | collective-permute-start | bytes 1572872 | tf_op jit(solution)/shard_map/back_z/ppermute | solution.py:29
  152.5 23.2 %collective-permute-start.36 = (bf16[1024,256]{1,0:T(8,128)(2,1)S(1)}, bf16[1024,256]{1,0:T(8,128)(2,1)S(1)}, u32[]{:S(2)}, u32[]{:S(2)}) collective-permute-start(bf16[1024,256]{1,0:T(8,128)(2,1)S(1)} %get-tuple-element.68), channel_id=1, source_target_pairs={{0,2},{1,3},{2,0},{3,1},{4,6},{5,7},{6,4},{7,5},{8,10},{9,11},{10,... | collective-permute-start | bytes 1572872 | tf_op jit(solution)/shard_map/back_z/ppermute | solution.py:29
  154.4 21.3 %collective-permute-start.37 = (bf16[1024,256]{1,0:T(8,128)(2,1)S(1)}, bf16[1024,256]{1,0:T(8,128)(2,1)S(1)}, u32[]{:S(2)}, u32[]{:S(2)}) collective-permute-start(bf16[1024,256]{1,0:T(8,128)(2,1)S(1)} %get-tuple-element.69), channel_id=1, source_target_pairs={{0,3},{1,0},{2,1},{3,2},{4,7},{5,4},{6,5},{7,6},{8,11},{9,8},{10,9... | collective-permute-start | bytes 1572872 | tf_op jit(solution)/shard_map/back_z/ppermute | solution.py:29
  160.9 16.6 %collective-permute-start.38 = (bf16[256,1024]{1,0:T(8,128)(2,1)S(1)}, bf16[256,1024]{1,0:T(8,128)(2,1)S(1)}, u32[]{:S(2)}, u32[]{:S(2)}) collective-permute-start(bf16[256,1024]{1,0:T(8,128)(2,1)S(1)} %get-tuple-element.70), channel_id=1, source_target_pairs={{0,16},{1,17},{2,18},{3,19},{4,20},{5,21},{6,22},{7,23},{8,24},{9,... | collective-permute-start | bytes 1572872 | tf_op jit(solution)/shard_map/right_sum_y/ppermute | solution.py:29
  161.8 18.5 %collective-permute-start.39 = (bf16[256,1024]{1,0:T(8,128)(2,1)S(1)}, bf16[256,1024]{1,0:T(8,128)(2,1)S(1)}, u32[]{:S(2)}, u32[]{:S(2)}) collective-permute-start(bf16[256,1024]{1,0:T(8,128)(2,1)S(1)} %get-tuple-element.71), channel_id=1, source_target_pairs={{0,32},{1,33},{2,34},{3,35},{4,36},{5,37},{6,38},{7,39},{8,40},{9,... | collective-permute-start | bytes 1572872 | tf_op jit(solution)/shard_map/right_sum_y/ppermute | solution.py:29
  164.9 25.9 %collective-permute-start.40 = (bf16[256,1024]{1,0:T(8,128)(2,1)S(1)}, bf16[256,1024]{1,0:T(8,128)(2,1)S(1)}, u32[]{:S(2)}, u32[]{:S(2)}) collective-permute-start(bf16[256,1024]{1,0:T(8,128)(2,1)S(1)} %get-tuple-element.72), channel_id=1, source_target_pairs={{0,48},{1,49},{2,50},{3,51},{4,52},{5,53},{6,54},{7,55},{8,56},{9,... | collective-permute-start | bytes 1572872 | tf_op jit(solution)/shard_map/right_sum_y/ppermute | solution.py:29
  175.9 17.0 %collective-permute-start.43 = (bf16[1024,256]{1,0:T(8,128)(2,1)S(1)}, bf16[1024,256]{1,0:T(8,128)(2,1)S(1)}, u32[]{:S(2)}, u32[]{:S(2)}) collective-permute-start(bf16[1024,256]{1,0:T(8,128)(2,1)S(1)} %add_convert_fusion.1.refs_4_), channel_id=1, source_target_pairs={{0,4},{1,5},{2,6},{3,7},{4,8},{5,9},{6,10},{7,11},{8,12},{9,13},{1... | collective-permute-start | bytes 1572872 | tf_op jit(solution)/shard_map/back_p/ppermute | solution.py:29
  176.9 19.4 %collective-permute-start.42 = (bf16[1024,256]{1,0:T(8,128)(2,1)S(1)}, bf16[1024,256]{1,0:T(8,128)(2,1)S(1)}, u32[]{:S(2)}, u32[]{:S(2)}) collective-permute-start(bf16[1024,256]{1,0:T(8,128)(2,1)S(1)} %add_convert_fusion.1.refs_4_), channel_id=1, source_target_pairs={{0,8},{1,9},{2,10},{3,11},{4,12},{5,13},{6,14},{7,15},{8,0},{9,1},... | collective-permute-start | bytes 1572872 | tf_op jit(solution)/shard_map/back_p/ppermute | solution.py:29
  177.5 18.8 %collective-permute-start.41 = (bf16[1024,256]{1,0:T(8,128)(2,1)S(1)}, bf16[1024,256]{1,0:T(8,128)(2,1)S(1)}, u32[]{:S(2)}, u32[]{:S(2)}) collective-permute-start(bf16[1024,256]{1,0:T(8,128)(2,1)S(1)} %add_convert_fusion.1.refs_4_), channel_id=1, source_target_pairs={{0,12},{1,13},{2,14},{3,15},{4,0},{5,1},{6,2},{7,3},{8,4},{9,5},{1... | collective-permute-start | bytes 1572872 | tf_op jit(solution)/shard_map/back_p/ppermute | solution.py:29
  180.2 21.9 %collective-permute-start.47 = (bf16[4,256,256]{2,1,0:T(8,128)(2,1)S(1)}, bf16[4,256,256]{2,1,0:T(8,128)(2,1)S(1)}, u32[]{:S(2)}, u32[]{:S(2)}) collective-permute-start(bf16[4,256,256]{2,1,0:T(8,128)(2,1)S(1)} %get-tuple-element.81), channel_id=1, source_target_pairs={{0,1},{1,2},{2,3},{3,0},{4,5},{5,6},{6,7},{7,4},{8,9},{9,10},{10,1... | collective-permute-start | bytes 1572872 | tf_op jit(solution)/shard_map/left_sum_z/ppermute | solution.py:29
  190.8 16.3 %collective-permute-start.48 = (bf16[4,256,256]{2,1,0:T(8,128)(2,1)S(1)}, bf16[4,256,256]{2,1,0:T(8,128)(2,1)S(1)}, u32[]{:S(2)}, u32[]{:S(2)}) collective-permute-start(bf16[4,256,256]{2,1,0:T(8,128)(2,1)S(1)} %get-tuple-element.83), channel_id=1, source_target_pairs={{0,2},{1,3},{2,0},{3,1},{4,6},{5,7},{6,4},{7,5},{8,10},{9,11},{10,... | collective-permute-start | bytes 1572872 | tf_op jit(solution)/shard_map/left_sum_z/ppermute | solution.py:29
  192.9 18.0 %collective-permute-start.49 = (bf16[4,256,256]{2,1,0:T(8,128)(2,1)S(1)}, bf16[4,256,256]{2,1,0:T(8,128)(2,1)S(1)}, u32[]{:S(2)}, u32[]{:S(2)}) collective-permute-start(bf16[4,256,256]{2,1,0:T(8,128)(2,1)S(1)} %get-tuple-element.85), channel_id=1, source_target_pairs={{0,3},{1,0},{2,1},{3,2},{4,7},{5,4},{6,5},{7,6},{8,11},{9,8},{10,9... | collective-permute-start | bytes 1572872 | tf_op jit(solution)/shard_map/left_sum_z/ppermute | solution.py:29
  200.2 13.4 %collective-permute-start.44 = (bf16[256,1024]{1,0:T(8,128)(2,1)S(1)}, bf16[256,1024]{1,0:T(8,128)(2,1)S(1)}, u32[]{:S(2)}, u32[]{:S(2)}) collective-permute-start(bf16[256,1024]{1,0:T(8,128)(2,1)S(1)} %get-tuple-element.75), channel_id=1, source_target_pairs={{0,16},{1,17},{2,18},{3,19},{4,20},{5,21},{6,22},{7,23},{8,24},{9,... | collective-permute-start | bytes 1572872 | tf_op jit(solution)/shard_map/update_o/ppermute | solution.py:29
  200.3 15.8 %collective-permute-start.45 = (bf16[256,1024]{1,0:T(8,128)(2,1)S(1)}, bf16[256,1024]{1,0:T(8,128)(2,1)S(1)}, u32[]{:S(2)}, u32[]{:S(2)}) collective-permute-start(bf16[256,1024]{1,0:T(8,128)(2,1)S(1)} %get-tuple-element.76), channel_id=1, source_target_pairs={{0,32},{1,33},{2,34},{3,35},{4,36},{5,37},{6,38},{7,39},{8,40},{9,... | collective-permute-start | bytes 1572872 | tf_op jit(solution)/shard_map/update_o/ppermute | solution.py:29
  202.1 14.6 %collective-permute-start.46 = (bf16[256,1024]{1,0:T(8,128)(2,1)S(1)}, bf16[256,1024]{1,0:T(8,128)(2,1)S(1)}, u32[]{:S(2)}, u32[]{:S(2)}) collective-permute-start(bf16[256,1024]{1,0:T(8,128)(2,1)S(1)} %get-tuple-element.77), channel_id=1, source_target_pairs={{0,48},{1,49},{2,50},{3,51},{4,52},{5,53},{6,54},{7,55},{8,56},{9,... | collective-permute-start | bytes 1572872 | tf_op jit(solution)/shard_map/update_o/ppermute | solution.py:29
  211.2 9.1 %collective-permute-start.52 = (bf16[256,256]{1,0:T(8,128)(2,1)S(1)}, bf16[256,256]{1,0:T(8,128)(2,1)S(1)}, u32[]{:S(2)}, u32[]{:S(2)}) collective-permute-start(bf16[256,256]{1,0:T(8,128)(2,1)S(1)} %get-tuple-element.90), channel_id=1, source_target_pairs={{0,4},{1,5},{2,6},{3,7},{4,8},{5,9},{6,10},{7,11},{8,12},{9,13},{1... | collective-permute-start | bytes 393224 | tf_op jit(solution)/shard_map/left_sum_x/ppermute | solution.py:29
  211.3 9.0 %collective-permute-start.51 = (bf16[256,256]{1,0:T(8,128)(2,1)S(1)}, bf16[256,256]{1,0:T(8,128)(2,1)S(1)}, u32[]{:S(2)}, u32[]{:S(2)}) collective-permute-start(bf16[256,256]{1,0:T(8,128)(2,1)S(1)} %get-tuple-element.91), channel_id=1, source_target_pairs={{0,8},{1,9},{2,10},{3,11},{4,12},{5,13},{6,14},{7,15},{8,0},{9,1},... | collective-permute-start | bytes 393224 | tf_op jit(solution)/shard_map/left_sum_x/ppermute | solution.py:29
  (17 other events, 244.9 us)

commit v4 on v3

--- a/solution.py
+++ b/solution.py
@@ -123,8 +123,8 @@
     p, o, z = at[1], at[2], at[3]
     halves, rights, outs, right_abs = refs[:4], refs[4:8], refs[8:12], refs[12]
     for i in range(4):
-        right_abs[(o + i) % 4] = rights[i][...]
-    right = jnp.concatenate([right_abs[(z + i) % 4] for i in range(4)], axis=0)
+        right_abs[(o + i + 4 - z) % 4] = rights[i][...]
+    right = right_abs[...].reshape(1024, 1024)
     for j in range(4):
         half = jnp.concatenate([halves[i][span(p + j), :] for i in range(4)], axis=1)
         outs[j][...] = contract(half, right, 1, 0).astype(bf16)
@@ -134,10 +134,10 @@
     p, o, z = at[1], at[2], at[3]
     directions, rights, outs, right_abs = refs[:4], refs[4:8], refs[8:12], refs[12]
     for i in range(4):
-        right_abs[(o + i) % 4] = rights[i][...]
+        right_abs[(o + i + 4 - z) % 4] = rights[i][...]
     direction = jnp.concatenate([d[...] for d in directions], axis=0)
     for j in range(4):
-        back = contract(direction, right_abs[(z + j) % 4], 1, 1).astype(bf16)
+        back = contract(direction, right_abs[j], 1, 1).astype(bf16)
         for i in range(4):
             outs[j][span(p + i), :] = back[i * 256 : (i + 1) * 256]
 
@@ -188,7 +188,7 @@
 
 
 def call(kernel, name, at, operands, out_shapes, scratch=()):
-    flops = 2 * 1024**3
+    flops = 4 * 1024**3
     moved = sum(v.size * v.dtype.itemsize for v in operands)
     moved += sum(v.size * v.dtype.itemsize for v in out_shapes)
     return list(pl.pallas_call(

time: 226 us -> 225 us (level)
  no operation moved by 1% of the time
where the time goes in v4:
time: 225 us; the launch traced here: 223 us
  starting transfers between devices  109 us (48%)
  waiting for transfers between devices  79.1 us (35%)
  Pallas kernels  25.5 us (11%)
  other arithmetic  6.75 us (3%)
    ppermute x53, starting transfers between devices, permute(): return lax.ppermute(value, ('layer', 'dp', 'mp'), pairs)  109 us
    ppermute x53, waiting for transfers between devices, permute(): return lax.ppermute(value, ('layer', 'dp', 'mp'), pairs)  79.1 us
    pallas_call x7, Pallas kernels, call(): pl.pallas_call(kernel, out_shape=out_shapes, in_specs=[pl.BlockSpec(memor...  25.5 us
  transfers between devices with their start and end apart: 53, of which 17 were waited for; matrix products, arithmetic and copies ran while one was open for 4% of the time, Pallas kernels for 9%

profile of v4, /device:TPU:24, one launch (start us, length us, event | category | flops | bytes accessed | tf_op | source)
XLA Modules:
  0.0 222.8 jit_solution(46804974663845472)
XLA Ops:
  2.0 4.8 %collective-permute-start.1 = (bf16[256,256]{1,0:T(8,128)(2,1)S(1)}, bf16[256,256]{1,0:T(8,128)(2,1)S(1)}, u32[]{:S(2)}, u32[]{:S(2)}) collective-permute-start(bf16[256,256]{1,0:T(8,128)(2,1)S(1)} %get-tuple-element.101), channel_id=1, source_target_pairs={{0,12},{1,13},{2,14},{3,15},{4,0},{5,1},{6,2},{7,3},{8,4},{9,5},{1... | collective-permute-start | bytes 393224 | tf_op jit(solution)/shard_map/left_blocks/ppermute | solution.py:29
  7.5 1.9 collective-permute-start.3
  9.4 4.2 %collective-permute-start.2 = (bf16[256,256]{1,0:T(8,128)(2,1)S(1)}, bf16[256,256]{1,0:T(8,128)(2,1)S(1)}, u32[]{:S(2)}, u32[]{:S(2)}) collective-permute-start(bf16[256,256]{1,0:T(8,128)(2,1)S(1)} %get-tuple-element.100), channel_id=1, source_target_pairs={{0,8},{1,9},{2,10},{3,11},{4,12},{5,13},{6,14},{7,15},{8,0},{9,1},... | collective-permute-start | bytes 393224 | tf_op jit(solution)/shard_map/left_blocks/ppermute | solution.py:29
  13.7 1.9 collective-permute-start.6
  16.4 2.0 collective-permute-start.4
  18.4 2.6 %collective-permute-start.11 = (bf16[256,1024]{1,0:T(8,128)(2,1)S(1)}, bf16[256,1024]{1,0:T(8,128)(2,1)}, u32[]{:S(2)}, u32[]{:S(2)}) collective-permute-start(bf16[256,1024]{1,0:T(8,128)(2,1)S(1)} %copy-done), channel_id=1, source_target_pairs={{0,32},{1,33},{2,34},{3,35},{4,36},{5,37},{6,38},{7,39},{8,40},{9,... | collective-permute-start | bytes 1572872 | tf_op jit(solution)/shard_map/grad_o/ppermute | solution.py:29
  21.1 5.8 %collective-permute-start.10 = (bf16[256,1024]{1,0:T(8,128)(2,1)S(1)}, bf16[256,1024]{1,0:T(8,128)(2,1)}, u32[]{:S(2)}, u32[]{:S(2)}) collective-permute-start(bf16[256,1024]{1,0:T(8,128)(2,1)S(1)} %copy-done), channel_id=1, source_target_pairs={{0,48},{1,49},{2,50},{3,51},{4,52},{5,53},{6,54},{7,55},{8,56},{9,... | collective-permute-start | bytes 1572872 | tf_op jit(solution)/shard_map/grad_o/ppermute | solution.py:29
  26.9 2.2 collective-permute-start.9
  29.0 7.8 %collective-permute-start.8 = (bf16[4,256,256]{2,1,0:T(8,128)(2,1)S(1)}, bf16[4,256,256]{2,1,0:T(8,128)(2,1)S(1)}, u32[]{:S(2)}, u32[]{:S(2)}) collective-permute-start(bf16[4,256,256]{2,1,0:T(8,128)(2,1)S(1)} %pad_maximum_fusion.refs_0_), channel_id=1, source_target_pairs={{0,2},{1,3},{2,0},{3,1},{4,6},{5,7},{6,4},{7,5},{8,10},{9,11},{10,... | collective-permute-start | bytes 1572872 | tf_op jit(solution)/shard_map/left_z/ppermute | solution.py:29
  38.7 17.3 %collective-permute-done.9.refs_3_ = bf16[4,256,256]{2,1,0:T(8,128)(2,1)S(1)} collective-permute-done((bf16[4,256,256]{2,1,0:T(8,128)(2,1)S(1)}, bf16[4,256,256]{2,1,0:T(8,128)(2,1)S(1)}, u32[]{:S(2)}, u32[]{:S(2)}) %collective-permute-start.9) | collective-permute-done | bytes 524320 | tf_op jit(solution)/shard_map/left_z/ppermute | solution.py:29
  56.6 4.3 %half.1 = (bf16[1024,256]{1,0:T(8,128)(2,1)S(1)}, bf16[1024,256]{1,0:T(8,128)(2,1)S(1)}, bf16[1024,256]{1,0:T(8,128)(2,1)S(1)}, bf16[1024,256]{1,0:T(8,128)(2,1)S(1)}) custom-call(s32[6]{0:T(128)S(1)} %stack.57.at, bf16[4,256,256]{2,1,0:T(8,128)(2,1)S(1)} %pad_maximum_fusion.refs_0_, bf16[4,256,256]{2,1,0:T(8,128)(2,1)S(1)} %collective-permute-done.7.refs_1_, ...), custom_call_target="tpu_custom_call" | custom-call | flops 4294967296 | bytes 6291456 | tf_op jit(solution)/shard_map/half/pallas_call | solution.py:194
  60.9 1.9 collective-permute-start.15
  64.2 12.8 %collective-permute-done.14 = bf16[1024,256]{1,0:T(8,128)(2,1)S(1)} collective-permute-done((bf16[1024,256]{1,0:T(8,128)(2,1)S(1)}, bf16[1024,256]{1,0:T(8,128)(2,1)S(1)}, u32[]{:S(2)}, u32[]{:S(2)}) %collective-permute-start.14) | collective-permute-done | bytes 524320 | tf_op jit(solution)/shard_map/half_p/ppermute | solution.py:29
  78.5 3.6 %collective-permute-start.21 = (bf16[256,1024]{1,0:T(8,128)(2,1)S(1)}, bf16[256,1024]{1,0:T(8,128)(2,1)S(1)}, u32[]{:S(2)}, u32[]{:S(2)}) collective-permute-start(bf16[256,1024]{1,0:T(8,128)(2,1)S(1)} %collective-permute-done.13.refs_4_), channel_id=1, source_target_pairs={{0,32},{1,33},{2,34},{3,35},{4,36},{5,37},{6,38},{7,39},{8,40},{9,... | collective-permute-start | bytes 1572872 | tf_op jit(solution)/shard_map/right_o/ppermute | solution.py:29
  82.6 3.4 %collective-permute-start.18 = (bf16[1024,256]{1,0:T(8,128)(2,1)S(1)}, bf16[1024,256]{1,0:T(8,128)(2,1)S(1)}, u32[]{:S(2)}, u32[]{:S(2)}) collective-permute-start(bf16[1024,256]{1,0:T(8,128)(2,1)S(1)} %add_convert_fusion.2.refs_0_), channel_id=1, source_target_pairs={{0,2},{1,3},{2,0},{3,1},{4,6},{5,7},{6,4},{7,5},{8,10},{9,11},{10,... | collective-permute-start | bytes 1572872 | tf_op jit(solution)/shard_map/half_z/ppermute | solution.py:29
  87.3 2.6 %collective-permute-start.17 = (bf16[1024,256]{1,0:T(8,128)(2,1)S(1)}, bf16[1024,256]{1,0:T(8,128)(2,1)S(1)}, u32[]{:S(2)}, u32[]{:S(2)}) collective-permute-start(bf16[1024,256]{1,0:T(8,128)(2,1)S(1)} %add_convert_fusion.2.refs_0_), channel_id=1, source_target_pairs={{0,3},{1,0},{2,1},{3,2},{4,7},{5,4},{6,5},{7,6},{8,11},{9,8},{10,9... | collective-permute-start | bytes 1572872 | tf_op jit(solution)/shard_map/half_z/ppermute | solution.py:29
  90.5 4.4 %collective-permute-done.20.refs_5_ = bf16[256,1024]{1,0:T(8,128)(2,1)S(1)} collective-permute-done((bf16[256,1024]{1,0:T(8,128)(2,1)S(1)}, bf16[256,1024]{1,0:T(8,128)(2,1)S(1)}, u32[]{:S(2)}, u32[]{:S(2)}) %collective-permute-start.20) | collective-permute-done | bytes 524320 | tf_op jit(solution)/shard_map/right_o/ppermute | solution.py:29
  94.9 1.8 collective-permute-start.24
  96.7 2.2 collective-permute-start.23
  98.8 8.5 %collective-permute-done.18.refs_2_ = bf16[1024,256]{1,0:T(8,128)(2,1)S(1)} collective-permute-done((bf16[1024,256]{1,0:T(8,128)(2,1)S(1)}, bf16[1024,256]{1,0:T(8,128)(2,1)S(1)}, u32[]{:S(2)}, u32[]{:S(2)}) %collective-permute-start.18) | collective-permute-done | bytes 524320 | tf_op jit(solution)/shard_map/half_z/ppermute | solution.py:29
  107.3 3.6 %rotate.1 = (bf16[256,1024]{1,0:T(8,128)(2,1)S(1)}, bf16[256,1024]{1,0:T(8,128)(2,1)S(1)}, bf16[256,1024]{1,0:T(8,128)(2,1)S(1)}, bf16[256,1024]{1,0:T(8,128)(2,1)S(1)}) custom-call(s32[6]{0:T(128)S(1)} %stack.57.at, bf16[1024,256]{1,0:T(8,128)(2,1)S(1)} %add_convert_fusion.2.refs_0_, bf16[1024,256]{1,0:T(8,128)(2,1)S(1)} %collective-permute-done.17.refs_1_, ...), custom_call_target="tpu_custom_call" | custom-call | flops 4294967296 | bytes 6291456 | tf_op jit(solution)/shard_map/rotate/pallas_call | solution.py:194
  113.1 2.5 %collective-permute-start.28 = (bf16[256,1024]{1,0:T(8,128)(2,1)S(1)}, bf16[256,1024]{1,0:T(8,128)(2,1)S(1)}, u32[]{:S(2)}, u32[]{:S(2)}) collective-permute-start(bf16[256,1024]{1,0:T(8,128)(2,1)S(1)} %get-tuple-element.60), channel_id=1, source_target_pairs={{0,12},{1,13},{2,14},{3,15},{4,0},{5,1},{6,2},{7,3},{8,4},{9,5},{1... | collective-permute-start | bytes 1572872 | tf_op jit(solution)/shard_map/rotated_p/ppermute | solution.py:29
  116.6 2.6 %collective-permute-start.31 = (bf16[4,256,256]{2,1,0:T(8,128)(2,1)S(1)}, bf16[4,256,256]{2,1,0:T(8,128)(2,1)S(1)}, u32[]{:S(2)}, u32[]{:S(2)}) collective-permute-start(bf16[4,256,256]{2,1,0:T(8,128)(2,1)S(1)} %pad_maximum_fusion.1.refs_0_), channel_id=1, source_target_pairs={{0,1},{1,2},{2,3},{3,0},{4,5},{5,6},{6,7},{7,4},{8,9},{9,10},{10,1... | collective-permute-start | bytes 1572872 | tf_op jit(solution)/shard_map/other_z/ppermute | solution.py:29
  120.3 6.8 %collective-permute-done.26 = bf16[256,1024]{1,0:T(8,128)(2,1)S(1)} collective-permute-done((bf16[256,1024]{1,0:T(8,128)(2,1)S(1)}, bf16[256,1024]{1,0:T(8,128)(2,1)S(1)}, u32[]{:S(2)}, u32[]{:S(2)}) %collective-permute-start.26) | collective-permute-done | bytes 524320 | tf_op jit(solution)/shard_map/rotated_p/ppermute | solution.py:29
  127.0 2.1 collective-permute-start.29
  129.1 2.2 divide_convert_fusion
  131.5 2.7 %collective-permute-start.33 = (bf16[256,1024]{1,0:T(8,128)(2,1)S(1)}, bf16[256,1024]{1,0:T(8,128)(2,1)S(1)}, u32[]{:S(2)}, u32[]{:S(2)}) collective-permute-start(bf16[256,1024]{1,0:T(8,128)(2,1)S(1)} %get-tuple-element.63.refs_0_), channel_id=1, source_target_pairs={{0,8},{1,9},{2,10},{3,11},{4,12},{5,13},{6,14},{7,15},{8,0},{9,1},... | collective-permute-start | bytes 1572872 | tf_op jit(solution)/shard_map/direction_p/ppermute | solution.py:29
  134.8 3.9 %left_sum.1 = (bf16[4,256,256]{2,1,0:T(8,128)(2,1)S(1)}, bf16[4,256,256]{2,1,0:T(8,128)(2,1)S(1)}, bf16[4,256,256]{2,1,0:T(8,128)(2,1)S(1)}, bf16[4,256,256]{2,1,0:T(8,128)(2,1)S(1)}) custom-call(s32[6]{0:T(128)S(1)} %stack.57.at, bf16[256,1024]{1,0:T(8,128)(2,1)S(1)} %copy-done, bf16[256,1024]{1,0:T(8,128)(2,1)} %collective-permute-done.10.refs_5_.refs_1_, ...), custom_call_target="tpu_custom_call" | custom-call | flops 4294967296 | bytes 6291456 | tf_op jit(solution)/shard_map/left_sum/pallas_call | solution.py:194
  138.7 2.1 collective-permute-done.30.refs_2_
  140.7 6.6 %collective-permute-done.34.refs_3_ = bf16[256,1024]{1,0:T(8,128)(2,1)S(1)} collective-permute-done((bf16[256,1024]{1,0:T(8,128)(2,1)S(1)}, bf16[256,1024]{1,0:T(8,128)(2,1)S(1)}, u32[]{:S(2)}, u32[]{:S(2)}) %collective-permute-start.34) | collective-permute-done | bytes 524320 | tf_op jit(solution)/shard_map/direction_p/ppermute | solution.py:29
  148.2 3.6 %back.1 = (bf16[1024,256]{1,0:T(8,128)(2,1)S(1)}, bf16[1024,256]{1,0:T(8,128)(2,1)S(1)}, bf16[1024,256]{1,0:T(8,128)(2,1)S(1)}, bf16[1024,256]{1,0:T(8,128)(2,1)S(1)}) custom-call(s32[6]{0:T(128)S(1)} %stack.57.at, bf16[256,1024]{1,0:T(8,128)(2,1)S(1)} %get-tuple-element.63.refs_0_, bf16[256,1024]{1,0:T(8,128)(2,1)S(1)} %collective-permute-done.32.refs_1_, ...), custom_call_target="tpu_custom_call" | custom-call | flops 4294967296 | bytes 6291456 | tf_op jit(solution)/shard_map/back/pallas_call | solution.py:194
  152.5 1.9 collective-permute-start.36
  154.4 1.9 collective-permute-start.37
  156.3 4.6 %right_sum.1 = (bf16[256,1024]{1,0:T(8,128)(2,1)S(1)}, bf16[256,1024]{1,0:T(8,128)(2,1)S(1)}, bf16[256,1024]{1,0:T(8,128)(2,1)S(1)}, bf16[256,1024]{1,0:T(8,128)(2,1)S(1)}) custom-call(s32[6]{0:T(128)S(1)} %stack.57.at, bf16[4,256,256]{2,1,0:T(8,128)(2,1)S(1)} %pad_maximum_fusion.1.refs_0_, bf16[4,256,256]{2,1,0:T(8,128)(2,1)S(1)} %collective-permute-done.29.refs_1_, ...), custom_call_target="tpu_custom_call" | custom-call | flops 4294967296 | bytes 8388608 | tf_op jit(solution)/shard_map/right_sum/pallas_call | solution.py:194
  161.8 2.2 %collective-permute-start.39 = (bf16[256,1024]{1,0:T(8,128)(2,1)S(1)}, bf16[256,1024]{1,0:T(8,128)(2,1)S(1)}, u32[]{:S(2)}, u32[]{:S(2)}) collective-permute-start(bf16[256,1024]{1,0:T(8,128)(2,1)S(1)} %get-tuple-element.71), channel_id=1, source_target_pairs={{0,32},{1,33},{2,34},{3,35},{4,36},{5,37},{6,38},{7,39},{8,40},{9,... | collective-permute-start | bytes 1572872 | tf_op jit(solution)/shard_map/right_sum_y/ppermute | solution.py:29
  164.9 10.8 %collective-permute-start.40 = (bf16[256,1024]{1,0:T(8,128)(2,1)S(1)}, bf16[256,1024]{1,0:T(8,128)(2,1)S(1)}, u32[]{:S(2)}, u32[]{:S(2)}) collective-permute-start(bf16[256,1024]{1,0:T(8,128)(2,1)S(1)} %get-tuple-element.72), channel_id=1, source_target_pairs={{0,48},{1,49},{2,50},{3,51},{4,52},{5,53},{6,54},{7,55},{8,56},{9,... | collective-permute-start | bytes 1572872 | tf_op jit(solution)/shard_map/right_sum_y/ppermute | solution.py:29
  177.5 2.6 %collective-permute-start.41 = (bf16[1024,256]{1,0:T(8,128)(2,1)S(1)}, bf16[1024,256]{1,0:T(8,128)(2,1)S(1)}, u32[]{:S(2)}, u32[]{:S(2)}) collective-permute-start(bf16[1024,256]{1,0:T(8,128)(2,1)S(1)} %add_convert_fusion.1.refs_4_), channel_id=1, source_target_pairs={{0,12},{1,13},{2,14},{3,15},{4,0},{5,1},{6,2},{7,3},{8,4},{9,5},{1... | collective-permute-start | bytes 1572872 | tf_op jit(solution)/shard_map/back_p/ppermute | solution.py:29
  180.2 2.0 collective-permute-start.47
  182.2 8.6 %collective-permute-done.40 = bf16[256,1024]{1,0:T(8,128)(2,1)S(1)} collective-permute-done((bf16[256,1024]{1,0:T(8,128)(2,1)S(1)}, bf16[256,1024]{1,0:T(8,128)(2,1)S(1)}, u32[]{:S(2)}, u32[]{:S(2)}) %collective-permute-start.40) | collective-permute-done | bytes 524320 | tf_op jit(solution)/shard_map/right_sum_y/ppermute | solution.py:29
  190.8 2.1 collective-permute-start.48
  192.9 2.0 collective-permute-start.49
  196.3 3.9 %update.1 = (bf16[256,1024]{1,0:T(8,128)(2,1)S(1)}, bf16[256,1024]{1,0:T(8,128)(2,1)S(1)}, bf16[256,1024]{1,0:T(8,128)(2,1)S(1)}, bf16[256,1024]{1,0:T(8,128)(2,1)S(1)}) custom-call(s32[6]{0:T(128)S(1)} %stack.57.at, bf16[4,256,256]{2,1,0:T(8,128)(2,1)S(1)} %pad_maximum_fusion.refs_0_, bf16[4,256,256]{2,1,0:T(8,128)(2,1)S(1)} %collective-permute-done.7.refs_1_, ...), custom_call_target="tpu_custom_call" | custom-call | flops 4294967296 | bytes 6291456 | tf_op jit(solution)/shard_map/update/pallas_call | solution.py:194
  200.3 1.8 collective-permute-start.45
  202.1 5.0 %collective-permute-start.46 = (bf16[256,1024]{1,0:T(8,128)(2,1)S(1)}, bf16[256,1024]{1,0:T(8,128)(2,1)S(1)}, u32[]{:S(2)}, u32[]{:S(2)}) collective-permute-start(bf16[256,1024]{1,0:T(8,128)(2,1)S(1)} %get-tuple-element.77), channel_id=1, source_target_pairs={{0,48},{1,49},{2,50},{3,51},{4,52},{5,53},{6,54},{7,55},{8,56},{9,... | collective-permute-start | bytes 1572872 | tf_op jit(solution)/shard_map/update_o/ppermute | solution.py:29
  207.1 3.8 %collective-permute-done.49 = bf16[4,256,256]{2,1,0:T(8,128)(2,1)S(1)} collective-permute-done((bf16[4,256,256]{2,1,0:T(8,128)(2,1)S(1)}, bf16[4,256,256]{2,1,0:T(8,128)(2,1)S(1)}, u32[]{:S(2)}, u32[]{:S(2)}) %collective-permute-start.49) | collective-permute-done | bytes 524320 | tf_op jit(solution)/shard_map/left_sum_z/ppermute | solution.py:29
  211.3 2.3 %collective-permute-start.51 = (bf16[256,256]{1,0:T(8,128)(2,1)S(1)}, bf16[256,256]{1,0:T(8,128)(2,1)S(1)}, u32[]{:S(2)}, u32[]{:S(2)}) collective-permute-start(bf16[256,256]{1,0:T(8,128)(2,1)S(1)} %get-tuple-element.91), channel_id=1, source_target_pairs={{0,8},{1,9},{2,10},{3,11},{4,12},{5,13},{6,14},{7,15},{8,0},{9,1},... | collective-permute-start | bytes 393224 | tf_op jit(solution)/shard_map/left_sum_x/ppermute | solution.py:29
  213.6 2.5 %collective-permute-start.50 = (bf16[256,256]{1,0:T(8,128)(2,1)S(1)}, bf16[256,256]{1,0:T(8,128)(2,1)S(1)}, u32[]{:S(2)}, u32[]{:S(2)}) collective-permute-start(bf16[256,256]{1,0:T(8,128)(2,1)S(1)} %get-tuple-element.92), channel_id=1, source_target_pairs={{0,12},{1,13},{2,14},{3,15},{4,0},{5,1},{6,2},{7,3},{8,4},{9,5},{1... | collective-permute-start | bytes 393224 | tf_op jit(solution)/shard_map/left_sum_x/ppermute | solution.py:29
  218.0 2.3 %collective-permute-done.52.refs_3_ = bf16[256,256]{1,0:T(8,128)(2,1)S(1)} collective-permute-done((bf16[256,256]{1,0:T(8,128)(2,1)S(1)}, bf16[256,256]{1,0:T(8,128)(2,1)S(1)}, u32[]{:S(2)}, u32[]{:S(2)}) %collective-permute-start.52) | collective-permute-done | bytes 131104 | tf_op jit(solution)/shard_map/left_sum_x/ppermute | solution.py:29
  (101 shorter events, 27.0 us)
Async XLA Ops:
  0.6 36.2 %collective-permute-start.12 = (bf16[256,1024]{1,0:T(8,128)(2,1)}, bf16[256,1024]{1,0:T(8,128)(2,1)S(1)}, u32[]{:S(2)}, u32[]{:S(2)}) collective-permute-start(bf16[256,1024]{1,0:T(8,128)(2,1)} %refs_8_), channel_id=1, source_target_pairs={{0,16},{1,17},{2,18},{3,19},{4,20},{5,21},{6,22},{7,23},{8,24},{9,... | collective-permute-start | bytes 1572872 | tf_op jit(solution)/shard_map/grad_o/ppermute | solution.py:29
  2.0 11.6 %collective-permute-start.1 = (bf16[256,256]{1,0:T(8,128)(2,1)S(1)}, bf16[256,256]{1,0:T(8,128)(2,1)S(1)}, u32[]{:S(2)}, u32[]{:S(2)}) collective-permute-start(bf16[256,256]{1,0:T(8,128)(2,1)S(1)} %get-tuple-element.101), channel_id=1, source_target_pairs={{0,12},{1,13},{2,14},{3,15},{4,0},{5,1},{6,2},{7,3},{8,4},{9,5},{1... | collective-permute-start | bytes 393224 | tf_op jit(solution)/shard_map/left_blocks/ppermute | solution.py:29
  15.6 11.3 %collective-permute-start.5 = (bf16[256,256]{1,0:T(8,128)(2,1)S(1)}, bf16[256,256]{1,0:T(8,128)(2,1)S(1)}, u32[]{:S(2)}, u32[]{:S(2)}) collective-permute-start(bf16[256,256]{1,0:T(8,128)(2,1)S(1)} %get-tuple-element.95), channel_id=1, source_target_pairs={{0,8},{1,9},{2,10},{3,11},{4,12},{5,13},{6,14},{7,15},{8,0},{9,1},... | collective-permute-start | bytes 393224 | tf_op jit(solution)/shard_map/other_x/ppermute | solution.py:29
  16.4 12.6 %collective-permute-start.4 = (bf16[256,256]{1,0:T(8,128)(2,1)S(1)}, bf16[256,256]{1,0:T(8,128)(2,1)}, u32[]{:S(2)}, u32[]{:S(2)}) collective-permute-start(bf16[256,256]{1,0:T(8,128)(2,1)S(1)} %get-tuple-element.96), channel_id=1, source_target_pairs={{0,12},{1,13},{2,14},{3,15},{4,0},{5,1},{6,2},{7,3},{8,4},{9,5},{1... | collective-permute-start | bytes 393224 | tf_op jit(solution)/shard_map/other_x/ppermute | solution.py:29
  18.4 18.6 %collective-permute-start.11 = (bf16[256,1024]{1,0:T(8,128)(2,1)S(1)}, bf16[256,1024]{1,0:T(8,128)(2,1)}, u32[]{:S(2)}, u32[]{:S(2)}) collective-permute-start(bf16[256,1024]{1,0:T(8,128)(2,1)S(1)} %copy-done), channel_id=1, source_target_pairs={{0,32},{1,33},{2,34},{3,35},{4,36},{5,37},{6,38},{7,39},{8,40},{9,... | collective-permute-start | bytes 1572872 | tf_op jit(solution)/shard_map/grad_o/ppermute | solution.py:29
  21.1 17.6 %collective-permute-start.10 = (bf16[256,1024]{1,0:T(8,128)(2,1)S(1)}, bf16[256,1024]{1,0:T(8,128)(2,1)}, u32[]{:S(2)}, u32[]{:S(2)}) collective-permute-start(bf16[256,1024]{1,0:T(8,128)(2,1)S(1)} %copy-done), channel_id=1, source_target_pairs={{0,48},{1,49},{2,50},{3,51},{4,52},{5,53},{6,54},{7,55},{8,56},{9,... | collective-permute-start | bytes 1572872 | tf_op jit(solution)/shard_map/grad_o/ppermute | solution.py:29
  26.9 29.1 %collective-permute-start.9 = (bf16[4,256,256]{2,1,0:T(8,128)(2,1)S(1)}, bf16[4,256,256]{2,1,0:T(8,128)(2,1)S(1)}, u32[]{:S(2)}, u32[]{:S(2)}) collective-permute-start(bf16[4,256,256]{2,1,0:T(8,128)(2,1)S(1)} %pad_maximum_fusion.refs_0_), channel_id=1, source_target_pairs={{0,1},{1,2},{2,3},{3,0},{4,5},{5,6},{6,7},{7,4},{8,9},{9,10},{10,1... | collective-permute-start | bytes 1572872 | tf_op jit(solution)/shard_map/left_z/ppermute | solution.py:29
  29.0 26.9 %collective-permute-start.8 = (bf16[4,256,256]{2,1,0:T(8,128)(2,1)S(1)}, bf16[4,256,256]{2,1,0:T(8,128)(2,1)S(1)}, u32[]{:S(2)}, u32[]{:S(2)}) collective-permute-start(bf16[4,256,256]{2,1,0:T(8,128)(2,1)S(1)} %pad_maximum_fusion.refs_0_), channel_id=1, source_target_pairs={{0,2},{1,3},{2,0},{3,1},{4,6},{5,7},{6,4},{7,5},{8,10},{9,11},{10,... | collective-permute-start | bytes 1572872 | tf_op jit(solution)/shard_map/left_z/ppermute | solution.py:29
  36.8 19.7 %collective-permute-start.7 = (bf16[4,256,256]{2,1,0:T(8,128)(2,1)S(1)}, bf16[4,256,256]{2,1,0:T(8,128)(2,1)S(1)}, u32[]{:S(2)}, u32[]{:S(2)}) collective-permute-start(bf16[4,256,256]{2,1,0:T(8,128)(2,1)S(1)} %pad_maximum_fusion.refs_0_), channel_id=1, source_target_pairs={{0,3},{1,0},{2,1},{3,2},{4,7},{5,4},{6,5},{7,6},{8,11},{9,8},{10,9... | collective-permute-start | bytes 1572872 | tf_op jit(solution)/shard_map/left_z/ppermute | solution.py:29
  37.0 27.2 %collective-permute-start.13 = (bf16[256,1024]{1,0:T(8,128)(2,1)}, bf16[256,1024]{1,0:T(8,128)(2,1)S(1)}, u32[]{:S(2)}, u32[]{:S(2)}) collective-permute-start(bf16[256,1024]{1,0:T(8,128)(2,1)} %param.9), channel_id=1, source_target_pairs={{0,0},{1,1},{2,2},{3,3},{4,4},{5,5},{6,6},{7,7},{8,8},{9,9},{10,10... | collective-permute-start | bytes 1572872 | tf_op jit(solution)/shard_map/right_swap/ppermute | solution.py:29
  60.9 16.1 %collective-permute-start.14 = (bf16[1024,256]{1,0:T(8,128)(2,1)S(1)}, bf16[1024,256]{1,0:T(8,128)(2,1)S(1)}, u32[]{:S(2)}, u32[]{:S(2)}) collective-permute-start(bf16[1024,256]{1,0:T(8,128)(2,1)S(1)} %get-tuple-element.51), channel_id=1, source_target_pairs={{0,4},{1,5},{2,6},{3,7},{4,8},{5,9},{6,10},{7,11},{8,12},{9,13},{1... | collective-permute-start | bytes 1572872 | tf_op jit(solution)/shard_map/half_p/ppermute | solution.py:29
  60.9 16.0 %collective-permute-start.15 = (bf16[1024,256]{1,0:T(8,128)(2,1)S(1)}, bf16[1024,256]{1,0:T(8,128)(2,1)S(1)}, u32[]{:S(2)}, u32[]{:S(2)}) collective-permute-start(bf16[1024,256]{1,0:T(8,128)(2,1)S(1)} %get-tuple-element.52), channel_id=1, source_target_pairs={{0,8},{1,9},{2,10},{3,11},{4,12},{5,13},{6,14},{7,15},{8,0},{9,1},... | collective-permute-start | bytes 1572872 | tf_op jit(solution)/shard_map/half_p/ppermute | solution.py:29
  62.9 15.0 %collective-permute-start.16 = (bf16[1024,256]{1,0:T(8,128)(2,1)S(1)}, bf16[1024,256]{1,0:T(8,128)(2,1)S(1)}, u32[]{:S(2)}, u32[]{:S(2)}) collective-permute-start(bf16[1024,256]{1,0:T(8,128)(2,1)S(1)} %get-tuple-element.53), channel_id=1, source_target_pairs={{0,12},{1,13},{2,14},{3,15},{4,0},{5,1},{6,2},{7,3},{8,4},{9,5},{1... | collective-permute-start | bytes 1572872 | tf_op jit(solution)/shard_map/half_p/ppermute | solution.py:29
  78.1 9.2 %collective-permute-start.22 = (bf16[256,1024]{1,0:T(8,128)(2,1)S(1)}, bf16[256,1024]{1,0:T(8,128)(2,1)S(1)}, u32[]{:S(2)}, u32[]{:S(2)}) collective-permute-start(bf16[256,1024]{1,0:T(8,128)(2,1)S(1)} %collective-permute-done.13.refs_4_), channel_id=1, source_target_pairs={{0,16},{1,17},{2,18},{3,19},{4,20},{5,21},{6,22},{7,23},{8,24},{9,... | collective-permute-start | bytes 1572872 | tf_op jit(solution)/shard_map/right_o/ppermute | solution.py:29
  78.5 11.4 %collective-permute-start.21 = (bf16[256,1024]{1,0:T(8,128)(2,1)S(1)}, bf16[256,1024]{1,0:T(8,128)(2,1)S(1)}, u32[]{:S(2)}, u32[]{:S(2)}) collective-permute-start(bf16[256,1024]{1,0:T(8,128)(2,1)S(1)} %collective-permute-done.13.refs_4_), channel_id=1, source_target_pairs={{0,32},{1,33},{2,34},{3,35},{4,36},{5,37},{6,38},{7,39},{8,40},{9,... | collective-permute-start | bytes 1572872 | tf_op jit(solution)/shard_map/right_o/ppermute | solution.py:29
  82.1 12.8 %collective-permute-start.20 = (bf16[256,1024]{1,0:T(8,128)(2,1)S(1)}, bf16[256,1024]{1,0:T(8,128)(2,1)S(1)}, u32[]{:S(2)}, u32[]{:S(2)}) collective-permute-start(bf16[256,1024]{1,0:T(8,128)(2,1)S(1)} %collective-permute-done.13.refs_4_), channel_id=1, source_target_pairs={{0,48},{1,49},{2,50},{3,51},{4,52},{5,53},{6,54},{7,55},{8,56},{9,... | collective-permute-start | bytes 1572872 | tf_op jit(solution)/shard_map/right_o/ppermute | solution.py:29
  82.1 14.6 %collective-permute-start.19 = (bf16[1024,256]{1,0:T(8,128)(2,1)S(1)}, bf16[1024,256]{1,0:T(8,128)(2,1)S(1)}, u32[]{:S(2)}, u32[]{:S(2)}) collective-permute-start(bf16[1024,256]{1,0:T(8,128)(2,1)S(1)} %add_convert_fusion.2.refs_0_), channel_id=1, source_target_pairs={{0,1},{1,2},{2,3},{3,0},{4,5},{5,6},{6,7},{7,4},{8,9},{9,10},{10,1... | collective-permute-start | bytes 1572872 | tf_op jit(solution)/shard_map/half_z/ppermute | solution.py:29
  82.6 24.7 %collective-permute-start.18 = (bf16[1024,256]{1,0:T(8,128)(2,1)S(1)}, bf16[1024,256]{1,0:T(8,128)(2,1)S(1)}, u32[]{:S(2)}, u32[]{:S(2)}) collective-permute-start(bf16[1024,256]{1,0:T(8,128)(2,1)S(1)} %add_convert_fusion.2.refs_0_), channel_id=1, source_target_pairs={{0,2},{1,3},{2,0},{3,1},{4,6},{5,7},{6,4},{7,5},{8,10},{9,11},{10,... | collective-permute-start | bytes 1572872 | tf_op jit(solution)/shard_map/half_z/ppermute | solution.py:29
  87.3 20.0 %collective-permute-start.17 = (bf16[1024,256]{1,0:T(8,128)(2,1)S(1)}, bf16[1024,256]{1,0:T(8,128)(2,1)S(1)}, u32[]{:S(2)}, u32[]{:S(2)}) collective-permute-start(bf16[1024,256]{1,0:T(8,128)(2,1)S(1)} %add_convert_fusion.2.refs_0_), channel_id=1, source_target_pairs={{0,3},{1,0},{2,1},{3,2},{4,7},{5,4},{6,5},{7,6},{8,11},{9,8},{10,9... | collective-permute-start | bytes 1572872 | tf_op jit(solution)/shard_map/half_z/ppermute | solution.py:29
  90.0 23.1 %collective-permute-start.25 = (bf16[256,1024]{1,0:T(8,128)(2,1)S(1)}, bf16[256,1024]{1,0:T(8,128)(2,1)S(1)}, u32[]{:S(2)}, u32[]{:S(2)}) collective-permute-start(bf16[256,1024]{1,0:T(8,128)(2,1)S(1)} %copy-done), channel_id=1, source_target_pairs={{0,4},{1,5},{2,6},{3,7},{4,8},{5,9},{6,10},{7,11},{8,12},{9,13},{1... | collective-permute-start | bytes 1572872 | tf_op jit(solution)/shard_map/rows_p/ppermute | solution.py:29
  94.9 21.7 %collective-permute-start.24 = (bf16[256,1024]{1,0:T(8,128)(2,1)S(1)}, bf16[256,1024]{1,0:T(8,128)(2,1)S(1)}, u32[]{:S(2)}, u32[]{:S(2)}) collective-permute-start(bf16[256,1024]{1,0:T(8,128)(2,1)S(1)} %copy-done), channel_id=1, source_target_pairs={{0,8},{1,9},{2,10},{3,11},{4,12},{5,13},{6,14},{7,15},{8,0},{9,1},... | collective-permute-start | bytes 1572872 | tf_op jit(solution)/shard_map/rows_p/ppermute | solution.py:29
  96.7 22.6 %collective-permute-start.23 = (bf16[256,1024]{1,0:T(8,128)(2,1)S(1)}, bf16[256,1024]{1,0:T(8,128)(2,1)S(1)}, u32[]{:S(2)}, u32[]{:S(2)}) collective-permute-start(bf16[256,1024]{1,0:T(8,128)(2,1)S(1)} %copy-done), channel_id=1, source_target_pairs={{0,12},{1,13},{2,14},{3,15},{4,0},{5,1},{6,2},{7,3},{8,4},{9,5},{1... | collective-permute-start | bytes 1572872 | tf_op jit(solution)/shard_map/rows_p/ppermute | solution.py:29
  110.9 16.1 %collective-permute-start.26 = (bf16[256,1024]{1,0:T(8,128)(2,1)S(1)}, bf16[256,1024]{1,0:T(8,128)(2,1)S(1)}, u32[]{:S(2)}, u32[]{:S(2)}) collective-permute-start(bf16[256,1024]{1,0:T(8,128)(2,1)S(1)} %get-tuple-element.58), channel_id=1, source_target_pairs={{0,4},{1,5},{2,6},{3,7},{4,8},{5,9},{6,10},{7,11},{8,12},{9,13},{1... | collective-permute-start | bytes 1572872 | tf_op jit(solution)/shard_map/rotated_p/ppermute | solution.py:29
  112.5 16.6 %collective-permute-start.27 = (bf16[256,1024]{1,0:T(8,128)(2,1)S(1)}, bf16[256,1024]{1,0:T(8,128)(2,1)S(1)}, u32[]{:S(2)}, u32[]{:S(2)}) collective-permute-start(bf16[256,1024]{1,0:T(8,128)(2,1)S(1)} %get-tuple-element.59), channel_id=1, source_target_pairs={{0,8},{1,9},{2,10},{3,11},{4,12},{5,13},{6,14},{7,15},{8,0},{9,1},... | collective-permute-start | bytes 1572872 | tf_op jit(solution)/shard_map/rotated_p/ppermute | solution.py:29
  113.1 16.0 %collective-permute-start.28 = (bf16[256,1024]{1,0:T(8,128)(2,1)S(1)}, bf16[256,1024]{1,0:T(8,128)(2,1)S(1)}, u32[]{:S(2)}, u32[]{:S(2)}) collective-permute-start(bf16[256,1024]{1,0:T(8,128)(2,1)S(1)} %get-tuple-element.60), channel_id=1, source_target_pairs={{0,12},{1,13},{2,14},{3,15},{4,0},{5,1},{6,2},{7,3},{8,4},{9,5},{1... | collective-permute-start | bytes 1572872 | tf_op jit(solution)/shard_map/rotated_p/ppermute | solution.py:29
  116.6 17.6 %collective-permute-start.31 = (bf16[4,256,256]{2,1,0:T(8,128)(2,1)S(1)}, bf16[4,256,256]{2,1,0:T(8,128)(2,1)S(1)}, u32[]{:S(2)}, u32[]{:S(2)}) collective-permute-start(bf16[4,256,256]{2,1,0:T(8,128)(2,1)S(1)} %pad_maximum_fusion.1.refs_0_), channel_id=1, source_target_pairs={{0,1},{1,2},{2,3},{3,0},{4,5},{5,6},{6,7},{7,4},{8,9},{9,10},{10,1... | collective-permute-start | bytes 1572872 | tf_op jit(solution)/shard_map/other_z/ppermute | solution.py:29
  119.3 21.5 %collective-permute-start.30 = (bf16[4,256,256]{2,1,0:T(8,128)(2,1)S(1)}, bf16[4,256,256]{2,1,0:T(8,128)(2,1)S(1)}, u32[]{:S(2)}, u32[]{:S(2)}) collective-permute-start(bf16[4,256,256]{2,1,0:T(8,128)(2,1)S(1)} %pad_maximum_fusion.1.refs_0_), channel_id=1, source_target_pairs={{0,2},{1,3},{2,0},{3,1},{4,6},{5,7},{6,4},{7,5},{8,10},{9,11},{10,... | collective-permute-start | bytes 1572872 | tf_op jit(solution)/shard_map/other_z/ppermute | solution.py:29
  127.0 13.7 %collective-permute-start.29 = (bf16[4,256,256]{2,1,0:T(8,128)(2,1)S(1)}, bf16[4,256,256]{2,1,0:T(8,128)(2,1)S(1)}, u32[]{:S(2)}, u32[]{:S(2)}) collective-permute-start(bf16[4,256,256]{2,1,0:T(8,128)(2,1)S(1)} %pad_maximum_fusion.1.refs_0_), channel_id=1, source_target_pairs={{0,3},{1,0},{2,1},{3,2},{4,7},{5,4},{6,5},{7,6},{8,11},{9,8},{10,9... | collective-permute-start | bytes 1572872 | tf_op jit(solution)/shard_map/other_z/ppermute | solution.py:29
  131.3 16.0 %collective-permute-start.34 = (bf16[256,1024]{1,0:T(8,128)(2,1)S(1)}, bf16[256,1024]{1,0:T(8,128)(2,1)S(1)}, u32[]{:S(2)}, u32[]{:S(2)}) collective-permute-start(bf16[256,1024]{1,0:T(8,128)(2,1)S(1)} %get-tuple-element.63.refs_0_), channel_id=1, source_target_pairs={{0,4},{1,5},{2,6},{3,7},{4,8},{5,9},{6,10},{7,11},{8,12},{9,13},{1... | collective-permute-start | bytes 1572872 | tf_op jit(solution)/shard_map/direction_p/ppermute | solution.py:29
  131.5 15.8 %collective-permute-start.33 = (bf16[256,1024]{1,0:T(8,128)(2,1)S(1)}, bf16[256,1024]{1,0:T(8,128)(2,1)S(1)}, u32[]{:S(2)}, u32[]{:S(2)}) collective-permute-start(bf16[256,1024]{1,0:T(8,128)(2,1)S(1)} %get-tuple-element.63.refs_0_), channel_id=1, source_target_pairs={{0,8},{1,9},{2,10},{3,11},{4,12},{5,13},{6,14},{7,15},{8,0},{9,1},... | collective-permute-start | bytes 1572872 | tf_op jit(solution)/shard_map/direction_p/ppermute | solution.py:29
  134.2 14.0 %collective-permute-start.32 = (bf16[256,1024]{1,0:T(8,128)(2,1)S(1)}, bf16[256,1024]{1,0:T(8,128)(2,1)S(1)}, u32[]{:S(2)}, u32[]{:S(2)}) collective-permute-start(bf16[256,1024]{1,0:T(8,128)(2,1)S(1)} %get-tuple-element.63.refs_0_), channel_id=1, source_target_pairs={{0,12},{1,13},{2,14},{3,15},{4,0},{5,1},{6,2},{7,3},{8,4},{9,5},{1... | collective-permute-start | bytes 1572872 | tf_op jit(solution)/shard_map/direction_p/ppermute | solution.py:29
  151.8 13.1 %collective-permute-start.35 = (bf16[1024,256]{1,0:T(8,128)(2,1)S(1)}, bf16[1024,256]{1,0:T(8,128)(2,1)S(1)}, u32[]{:S(2)}, u32[]{:S(2)}) collective-permute-start(bf16[1024,256]{1,0:T(8,128)(2,1)S(1)} %get-tuple-element.67), channel_id=1, source_target_pairs={{0,1},{1,2},{2,3},{3,0},{4,5},{5,6},{6,7},{7,4},{8,9},{9,10},{10,1... | collective-permute-start | bytes 1572872 | tf_op jit(solution)/shard_map/back_z/ppermute | solution.py:29
  152.5 23.2 %collective-permute-start.36 = (bf16[1024,256]{1,0:T(8,128)(2,1)S(1)}, bf16[1024,256]{1,0:T(8,128)(2,1)S(1)}, u32[]{:S(2)}, u32[]{:S(2)}) collective-permute-start(bf16[1024,256]{1,0:T(8,128)(2,1)S(1)} %get-tuple-element.68), channel_id=1, source_target_pairs={{0,2},{1,3},{2,0},{3,1},{4,6},{5,7},{6,4},{7,5},{8,10},{9,11},{10,... | collective-permute-start | bytes 1572872 | tf_op jit(solution)/shard_map/back_z/ppermute | solution.py:29
  154.4 21.3 %collective-permute-start.37 = (bf16[1024,256]{1,0:T(8,128)(2,1)S(1)}, bf16[1024,256]{1,0:T(8,128)(2,1)S(1)}, u32[]{:S(2)}, u32[]{:S(2)}) collective-permute-start(bf16[1024,256]{1,0:T(8,128)(2,1)S(1)} %get-tuple-element.69), channel_id=1, source_target_pairs={{0,3},{1,0},{2,1},{3,2},{4,7},{5,4},{6,5},{7,6},{8,11},{9,8},{10,9... | collective-permute-start | bytes 1572872 | tf_op jit(solution)/shard_map/back_z/ppermute | solution.py:29
  160.9 16.6 %collective-permute-start.38 = (bf16[256,1024]{1,0:T(8,128)(2,1)S(1)}, bf16[256,1024]{1,0:T(8,128)(2,1)S(1)}, u32[]{:S(2)}, u32[]{:S(2)}) collective-permute-start(bf16[256,1024]{1,0:T(8,128)(2,1)S(1)} %get-tuple-element.70), channel_id=1, source_target_pairs={{0,16},{1,17},{2,18},{3,19},{4,20},{5,21},{6,22},{7,23},{8,24},{9,... | collective-permute-start | bytes 1572872 | tf_op jit(solution)/shard_map/right_sum_y/ppermute | solution.py:29
  161.8 18.4 %collective-permute-start.39 = (bf16[256,1024]{1,0:T(8,128)(2,1)S(1)}, bf16[256,1024]{1,0:T(8,128)(2,1)S(1)}, u32[]{:S(2)}, u32[]{:S(2)}) collective-permute-start(bf16[256,1024]{1,0:T(8,128)(2,1)S(1)} %get-tuple-element.71), channel_id=1, source_target_pairs={{0,32},{1,33},{2,34},{3,35},{4,36},{5,37},{6,38},{7,39},{8,40},{9,... | collective-permute-start | bytes 1572872 | tf_op jit(solution)/shard_map/right_sum_y/ppermute | solution.py:29
  164.9 25.9 %collective-permute-start.40 = (bf16[256,1024]{1,0:T(8,128)(2,1)S(1)}, bf16[256,1024]{1,0:T(8,128)(2,1)S(1)}, u32[]{:S(2)}, u32[]{:S(2)}) collective-permute-start(bf16[256,1024]{1,0:T(8,128)(2,1)S(1)} %get-tuple-element.72), channel_id=1, source_target_pairs={{0,48},{1,49},{2,50},{3,51},{4,52},{5,53},{6,54},{7,55},{8,56},{9,... | collective-permute-start | bytes 1572872 | tf_op jit(solution)/shard_map/right_sum_y/ppermute | solution.py:29
  175.9 17.0 %collective-permute-start.43 = (bf16[1024,256]{1,0:T(8,128)(2,1)S(1)}, bf16[1024,256]{1,0:T(8,128)(2,1)S(1)}, u32[]{:S(2)}, u32[]{:S(2)}) collective-permute-start(bf16[1024,256]{1,0:T(8,128)(2,1)S(1)} %add_convert_fusion.1.refs_4_), channel_id=1, source_target_pairs={{0,4},{1,5},{2,6},{3,7},{4,8},{5,9},{6,10},{7,11},{8,12},{9,13},{1... | collective-permute-start | bytes 1572872 | tf_op jit(solution)/shard_map/back_p/ppermute | solution.py:29
  176.9 19.4 %collective-permute-start.42 = (bf16[1024,256]{1,0:T(8,128)(2,1)S(1)}, bf16[1024,256]{1,0:T(8,128)(2,1)S(1)}, u32[]{:S(2)}, u32[]{:S(2)}) collective-permute-start(bf16[1024,256]{1,0:T(8,128)(2,1)S(1)} %add_convert_fusion.1.refs_4_), channel_id=1, source_target_pairs={{0,8},{1,9},{2,10},{3,11},{4,12},{5,13},{6,14},{7,15},{8,0},{9,1},... | collective-permute-start | bytes 1572872 | tf_op jit(solution)/shard_map/back_p/ppermute | solution.py:29
  177.5 18.8 %collective-permute-start.41 = (bf16[1024,256]{1,0:T(8,128)(2,1)S(1)}, bf16[1024,256]{1,0:T(8,128)(2,1)S(1)}, u32[]{:S(2)}, u32[]{:S(2)}) collective-permute-start(bf16[1024,256]{1,0:T(8,128)(2,1)S(1)} %add_convert_fusion.1.refs_4_), channel_id=1, source_target_pairs={{0,12},{1,13},{2,14},{3,15},{4,0},{5,1},{6,2},{7,3},{8,4},{9,5},{1... | collective-permute-start | bytes 1572872 | tf_op jit(solution)/shard_map/back_p/ppermute | solution.py:29
  180.2 21.9 %collective-permute-start.47 = (bf16[4,256,256]{2,1,0:T(8,128)(2,1)S(1)}, bf16[4,256,256]{2,1,0:T(8,128)(2,1)S(1)}, u32[]{:S(2)}, u32[]{:S(2)}) collective-permute-start(bf16[4,256,256]{2,1,0:T(8,128)(2,1)S(1)} %get-tuple-element.81), channel_id=1, source_target_pairs={{0,1},{1,2},{2,3},{3,0},{4,5},{5,6},{6,7},{7,4},{8,9},{9,10},{10,1... | collective-permute-start | bytes 1572872 | tf_op jit(solution)/shard_map/left_sum_z/ppermute | solution.py:29
  190.8 16.3 %collective-permute-start.48 = (bf16[4,256,256]{2,1,0:T(8,128)(2,1)S(1)}, bf16[4,256,256]{2,1,0:T(8,128)(2,1)S(1)}, u32[]{:S(2)}, u32[]{:S(2)}) collective-permute-start(bf16[4,256,256]{2,1,0:T(8,128)(2,1)S(1)} %get-tuple-element.83), channel_id=1, source_target_pairs={{0,2},{1,3},{2,0},{3,1},{4,6},{5,7},{6,4},{7,5},{8,10},{9,11},{10,... | collective-permute-start | bytes 1572872 | tf_op jit(solution)/shard_map/left_sum_z/ppermute | solution.py:29
  192.9 18.0 %collective-permute-start.49 = (bf16[4,256,256]{2,1,0:T(8,128)(2,1)S(1)}, bf16[4,256,256]{2,1,0:T(8,128)(2,1)S(1)}, u32[]{:S(2)}, u32[]{:S(2)}) collective-permute-start(bf16[4,256,256]{2,1,0:T(8,128)(2,1)S(1)} %get-tuple-element.85), channel_id=1, source_target_pairs={{0,3},{1,0},{2,1},{3,2},{4,7},{5,4},{6,5},{7,6},{8,11},{9,8},{10,9... | collective-permute-start | bytes 1572872 | tf_op jit(solution)/shard_map/left_sum_z/ppermute | solution.py:29
  200.2 13.3 %collective-permute-start.44 = (bf16[256,1024]{1,0:T(8,128)(2,1)S(1)}, bf16[256,1024]{1,0:T(8,128)(2,1)S(1)}, u32[]{:S(2)}, u32[]{:S(2)}) collective-permute-start(bf16[256,1024]{1,0:T(8,128)(2,1)S(1)} %get-tuple-element.75), channel_id=1, source_target_pairs={{0,16},{1,17},{2,18},{3,19},{4,20},{5,21},{6,22},{7,23},{8,24},{9,... | collective-permute-start | bytes 1572872 | tf_op jit(solution)/shard_map/update_o/ppermute | solution.py:29
  200.3 15.8 %collective-permute-start.45 = (bf16[256,1024]{1,0:T(8,128)(2,1)S(1)}, bf16[256,1024]{1,0:T(8,128)(2,1)S(1)}, u32[]{:S(2)}, u32[]{:S(2)}) collective-permute-start(bf16[256,1024]{1,0:T(8,128)(2,1)S(1)} %get-tuple-element.76), channel_id=1, source_target_pairs={{0,32},{1,33},{2,34},{3,35},{4,36},{5,37},{6,38},{7,39},{8,40},{9,... | collective-permute-start | bytes 1572872 | tf_op jit(solution)/shard_map/update_o/ppermute | solution.py:29
  202.1 14.6 %collective-permute-start.46 = (bf16[256,1024]{1,0:T(8,128)(2,1)S(1)}, bf16[256,1024]{1,0:T(8,128)(2,1)S(1)}, u32[]{:S(2)}, u32[]{:S(2)}) collective-permute-start(bf16[256,1024]{1,0:T(8,128)(2,1)S(1)} %get-tuple-element.77), channel_id=1, source_target_pairs={{0,48},{1,49},{2,50},{3,51},{4,52},{5,53},{6,54},{7,55},{8,56},{9,... | collective-permute-start | bytes 1572872 | tf_op jit(solution)/shard_map/update_o/ppermute | solution.py:29
  211.2 9.1 %collective-permute-start.52 = (bf16[256,256]{1,0:T(8,128)(2,1)S(1)}, bf16[256,256]{1,0:T(8,128)(2,1)S(1)}, u32[]{:S(2)}, u32[]{:S(2)}) collective-permute-start(bf16[256,256]{1,0:T(8,128)(2,1)S(1)} %get-tuple-element.90), channel_id=1, source_target_pairs={{0,4},{1,5},{2,6},{3,7},{4,8},{5,9},{6,10},{7,11},{8,12},{9,13},{1... | collective-permute-start | bytes 393224 | tf_op jit(solution)/shard_map/left_sum_x/ppermute | solution.py:29
  211.3 9.1 %collective-permute-start.51 = (bf16[256,256]{1,0:T(8,128)(2,1)S(1)}, bf16[256,256]{1,0:T(8,128)(2,1)S(1)}, u32[]{:S(2)}, u32[]{:S(2)}) collective-permute-start(bf16[256,256]{1,0:T(8,128)(2,1)S(1)} %get-tuple-element.91), channel_id=1, source_target_pairs={{0,8},{1,9},{2,10},{3,11},{4,12},{5,13},{6,14},{7,15},{8,0},{9,1},... | collective-permute-start | bytes 393224 | tf_op jit(solution)/shard_map/left_sum_x/ppermute | solution.py:29
  (17 other events, 245.0 us)
